TPU v7x, 32 devices: a whole 2x2x4 slice. The times are simulated.
32 devices in a mesh: expert: 4 (over y, core), shard: 8 (over z, x).
Axes of the slice: x: 2, y: 2, z: 4, core: 2. Of those that a mesh axis runs over, the one named last changes fastest.
Arguments:
- inputs: bfloat16 [2, 2048, 2048], P(None, ('expert', 'shard')), may hold values from -6 to 6
- segment_ids: int32 [2, 2048], P(None, 'expert'), may hold values from 0 to 3, as said below
- routes: int32 [2, 2048, 8], P(None, ('expert', 'shard')), may hold values from 0 to 15, all different within a row; in each aligned block of 64 rows (0 to 63, 64 to 127, ..., all dimensions but the last counted through in order) at most 64 rows name the same one
- cotangent: bfloat16 [2, 2048, 2048], P(None, ('expert', 'shard')), may hold values from -6 to 6
- query_weight: bfloat16 [2048, 2048], P('shard'), may hold values from -0.125 to 0.125
- key_weight: bfloat16 [2048, 2048], P('shard'), may hold values from -0.125 to 0.125
- value_weight: bfloat16 [2048, 2048], P('shard'), may hold values from -0.125 to 0.125
- output_weight: bfloat16 [2048, 2048], P('shard'), may hold values from -1.5 to 1.5
- router_weight: bfloat16 [2048, 16], P('shard'), may hold values from -0.0625 to 0.0625
- attention_gain: bfloat16 [2048], P('shard'), may hold values from 0.5 to 1.5
- expert_gain: bfloat16 [2048], P('shard'), may hold values from 0.5 to 1.5
- query_gain: bfloat16 [128], P('shard'), may hold values from 0.099609375 to 1.8984375
- key_gain: bfloat16 [128], P('shard'), may hold values from 0.099609375 to 1.8984375
- gate_weight: bfloat16 [32, 2048, 512], P(('expert', 'shard')), may hold values from -0.125 to 0.125
- up_weight: bfloat16 [32, 2048, 512], P(('expert', 'shard')), may hold values from -0.125 to 0.125
- down_weight: bfloat16 [32, 512, 2048], P(('expert', 'shard')), may hold values from -1 to 1
Outputs:
- layer_out: bfloat16 [2, 2048, 2048], P(None, ('expert', 'shard'))
- input_grad: bfloat16 [2, 2048, 2048], P(None, ('expert', 'shard'))
- query_grad: float32 [2048, 2048], P('shard')
- key_grad: float32 [2048, 2048], P('shard')
- value_grad: float32 [2048, 2048], P('shard')
- output_grad: float32 [2048, 2048], P('shard')
- router_grad: float32 [2048, 16], P('shard')
- gain_attention: float32 [2048], P('shard')
- gain_expert: float32 [2048], P('shard')
- gain_query: float32 [128], P('shard')
- gain_key: float32 [128], P('shard')
- gate_grad: float32 [32, 2048, 512], P(('expert', 'shard'))
- up_grad: float32 [32, 2048, 512], P(('expert', 'shard'))
- down_grad: float32 [32, 512, 2048], P(('expert', 'shard'))
Inputs may be any that keep to these rules, and one draw needn't show every extreme that they name: `segment_ids`: within each sequence of 512 tokens (tokens s * 512 to (s + 1) * 512 - 1 of a micro-batch) the ids start at 0 and rise by 0 or 1 from one token to the next; in every micro-batch one sequence is a single document and every other sequence holds exactly four documents. `routes`: A token names 8 different experts; in each micro-batch at most 64 of the 64 tokens of one device name the same expert.
All inputs are finite; a program needn't handle non-finite values.
Results may differ from a plain program's by a relative error of at most 0.025.
Values may be sent and summed in bfloat16 or wider, within the bound.
A program may use at most 208 MiB of HBM per device.

v0:
```python
import math

import jax
import jax.numpy as jnp
from jax import lax
from jax.sharding import PartitionSpec as P

HEADS = 16
HDIM = 128


EPSILON = 1e-05
ROPE_BASE = 10000.0
MASK_FILL = -1e30
PRECISE = lax.Precision.HIGHEST


def rms_scale(values):
    return lax.rsqrt(jnp.mean(values * values, axis=-1, keepdims=True) + EPSILON)


def norm_back(normed_grad, normed, inv_scale):
    return inv_scale * (
        normed_grad - normed * jnp.mean(normed_grad * normed, axis=-1, keepdims=True)
    )


def rotary(places, head_width):
    half_width = head_width // 2
    steps_float = jnp.arange(half_width, dtype=jnp.int32).astype(jnp.float32)
    freqs = jnp.power(ROPE_BASE, -2.0 * steps_float / head_width)
    theta = places[:, None] * freqs[None, :]
    return (jnp.cos(theta)[:, None, :], jnp.sin(theta)[:, None, :])


def rotate(values, cosine_table, sine_table):
    half_width = values.shape[-1] // 2
    front = values[..., :half_width]
    behind = values[..., half_width:]
    return jnp.concatenate(
        [front * cosine_table - behind * sine_table, behind * cosine_table + front * sine_table],
        axis=-1,
    )


def softmax_rows(scores):
    row_peak = jnp.max(scores, axis=-1, keepdims=True)
    exponent = jnp.exp(scores - row_peak)
    return exponent / jnp.sum(exponent, axis=-1, keepdims=True)


def slot_tables(expert_ids, experts, capacity):
    onehot = (expert_ids[:, None] == jnp.arange(experts, dtype=jnp.int32)[None, :]).astype(
        jnp.int32
    )
    rank_in = jnp.cumsum(onehot, axis=0) - 1
    place_in = jnp.sum(rank_in * onehot, axis=1)
    target = expert_ids * capacity + place_in
    pairs = expert_ids.shape[0]
    source = (
        jnp.full((experts * capacity,), pairs, jnp.int32)
        .at[target]
        .set(jnp.arange(pairs, dtype=jnp.int32))
    )
    return (onehot, target, source)


def spread(row_table, lookup, experts, capacity):
    padded_rows = jnp.concatenate(
        [row_table, jnp.zeros((1, row_table.shape[1]), row_table.dtype)], axis=0
    )
    gathered = padded_rows[lookup].reshape(experts, capacity, row_table.shape[1])
    return jnp.repeat(gathered, 2, axis=0)


def gather_back(returned, target, experts, capacity):
    paired = returned.reshape(experts, 2, capacity, returned.shape[2]).astype(jnp.float32)
    merged = (paired[:, 0] + paired[:, 1]).reshape(experts * capacity, returned.shape[2])
    return merged[target]


def reroute(blocks):
    return lax.all_to_all(blocks, ("expert", "shard"), split_axis=0, concat_axis=0, tiled=True)


def per_device(
    inputs,
    segment_ids,
    routes,
    cotangent,
    query_weight,
    key_weight,
    value_weight,
    output_weight,
    router_weight,
    attention_gain,
    expert_gain,
    query_gain,
    key_gain,
    gate_weight,
    up_weight,
    down_weight,
):
    micro_count, block_rows, model_width = inputs.shape
    experts = router_weight.shape[1]
    top_count = routes.shape[2]
    capacity = 2 * block_rows * top_count // experts
    devices = 2 * experts
    score_scale = 1.0 / math.sqrt(HDIM)
    shard_place = lax.axis_index("shard")
    column_width = query_weight.shape[0]
    places = (shard_place * block_rows + jnp.arange(block_rows, dtype=jnp.int32)).astype(
        jnp.float32
    )
    cosine_table, sine_table = rotary(places, HDIM)
    gate_sum = jnp.zeros(gate_weight.shape[1:], jnp.float32)
    up_sum = jnp.zeros(up_weight.shape[1:], jnp.float32)
    down_sum = jnp.zeros(down_weight.shape[1:], jnp.float32)
    layer_rows = []
    input_rows = []
    shard_totals = None
    row_totals = None
    small_totals = None
    for micro_step in range(micro_count):
        gathered = (
            lax.all_gather(query_weight, "shard", axis=0, tiled=True),
            lax.all_gather(key_weight, "shard", axis=0, tiled=True),
            lax.all_gather(value_weight, "shard", axis=0, tiled=True),
            lax.all_gather(output_weight, "shard", axis=0, tiled=True),
            lax.all_gather(router_weight, "shard", axis=0, tiled=True),
            lax.all_gather(attention_gain, "shard", axis=0, tiled=True),
            lax.all_gather(expert_gain, "shard", axis=0, tiled=True),
            lax.all_gather(query_gain, "shard", axis=0, tiled=True),
            lax.all_gather(key_gain, "shard", axis=0, tiled=True),
        )
        query_full, key_full, value_full, output_full, router_full = (
            gathered[0],
            gathered[1],
            gathered[2],
            gathered[3],
            gathered[4],
        )
        attn_gain_full = gathered[5].astype(jnp.float32)
        expert_gain_full = gathered[6].astype(jnp.float32)
        qgain_full = gathered[7].astype(jnp.float32)
        kgain_full = gathered[8].astype(jnp.float32)
        hidden = inputs[micro_step].astype(jnp.float32)
        scale_first = rms_scale(hidden)
        normed_first = hidden * scale_first
        mixer_input = (normed_first * attn_gain_full).astype(jnp.bfloat16)
        query_proj = jnp.dot(mixer_input, query_full, preferred_element_type=jnp.float32).reshape(
            block_rows, HEADS, HDIM
        )
        key_proj = jnp.dot(mixer_input, key_full, preferred_element_type=jnp.float32).reshape(
            block_rows, HEADS, HDIM
        )
        value_low = (
            jnp.dot(mixer_input, value_full, preferred_element_type=jnp.float32)
            .astype(jnp.bfloat16)
            .reshape(block_rows, HEADS, HDIM)
        )
        query_norm_scale = rms_scale(query_proj)
        query_unit = query_proj * query_norm_scale
        query_rot = rotate(query_unit * qgain_full, cosine_table, sine_table).astype(jnp.bfloat16)
        key_norm_scale = rms_scale(key_proj)
        key_unit = key_proj * key_norm_scale
        key_rot = rotate(key_unit * kgain_full, cosine_table, sine_table).astype(jnp.bfloat16)
        keys_all, values_all = (
            lax.all_gather(key_rot, "shard", axis=0, tiled=True),
            lax.all_gather(value_low, "shard", axis=0, tiled=True),
        )
        seg_all = segment_ids[micro_step]
        seg_own = lax.dynamic_slice_in_dim(seg_all, shard_place * block_rows, block_rows)
        same_doc = seg_own[:, None] == seg_all[None, :]

        def scores_of():
            raw_scores = (
                jnp.einsum("qhd,khd->hqk", query_rot, keys_all, preferred_element_type=jnp.float32)
                * score_scale
            )
            return jnp.where(same_doc[None], raw_scores, MASK_FILL)

        scores = scores_of()
        row_peak = jnp.max(scores, axis=-1, keepdims=True)
        exponent = jnp.exp(scores - row_peak)
        row_sums = jnp.sum(exponent, axis=-1, keepdims=True)
        probabilities = exponent / row_sums
        log_total = row_peak + jnp.log(row_sums)
        attended = jnp.einsum(
            "hqk,khd->qhd",
            probabilities.astype(jnp.bfloat16),
            values_all,
            preferred_element_type=jnp.float32,
        )
        attended = attended.reshape(block_rows, model_width).astype(jnp.bfloat16)
        middle = hidden + jnp.dot(attended, output_full, preferred_element_type=jnp.float32)
        scale_second = rms_scale(middle)
        normed_second = middle * scale_second
        expert_input = (normed_second * expert_gain_full).astype(jnp.bfloat16)
        logits = jnp.dot(expert_input, router_full, preferred_element_type=jnp.float32)
        onehot, target, source = slot_tables(routes[micro_step].reshape(-1), experts, capacity)
        choose = onehot.reshape(block_rows, top_count, experts).astype(jnp.float32)
        chosen = jnp.sum(choose * logits[:, None, :], axis=-1)
        gate_share = softmax_rows(chosen)
        received = reroute(spread(expert_input, source // top_count, experts, capacity)).reshape(
            -1, model_width
        )
        gate_pre = jnp.dot(received, gate_weight[0], preferred_element_type=jnp.float32)
        up_pre = jnp.dot(received, up_weight[0], preferred_element_type=jnp.float32)
        sigmoid_gate = jax.nn.sigmoid(gate_pre)
        swish_gate = gate_pre * sigmoid_gate
        activated = (swish_gate * up_pre).astype(jnp.bfloat16)
        partial_out = jnp.dot(activated, down_weight[0], preferred_element_type=jnp.float32).astype(
            jnp.bfloat16
        )
        partial_out = partial_out.reshape(devices, capacity, model_width)
        picked = gather_back(reroute(partial_out), target, experts, capacity).reshape(
            block_rows, top_count, model_width
        )
        result = middle + jnp.sum(gate_share[:, :, None] * picked, axis=1)
        layer_rows.append(result.astype(jnp.bfloat16))
        upstream = cotangent[micro_step].astype(jnp.float32)
        share_grad = jnp.sum(picked * upstream[:, None, :], axis=-1)
        chosen_grad = gate_share * (
            share_grad - jnp.sum(gate_share * share_grad, axis=-1, keepdims=True)
        )
        logits_grad = jnp.sum(choose * chosen_grad[:, :, None], axis=1)
        weighted = (
            (gate_share[:, :, None] * upstream[:, None, :])
            .astype(jnp.bfloat16)
            .reshape(block_rows * top_count, model_width)
        )
        part_grad = reroute(spread(weighted, source, experts, capacity)).reshape(-1, model_width)
        units_grad = jnp.einsum(
            "rd,fd->rf", part_grad, down_weight[0], preferred_element_type=jnp.float32
        )
        down_sum = down_sum + jnp.einsum(
            "rf,rd->fd", activated, part_grad, preferred_element_type=jnp.float32
        )
        gate_pre_grad = (
            units_grad * up_pre * sigmoid_gate * (1.0 + gate_pre * (1.0 - sigmoid_gate))
        ).astype(jnp.bfloat16)
        up_pre_grad = (units_grad * swish_gate).astype(jnp.bfloat16)
        gate_sum = gate_sum + jnp.einsum(
            "rd,rf->df", received, gate_pre_grad, preferred_element_type=jnp.float32
        )
        up_sum = up_sum + jnp.einsum(
            "rd,rf->df", received, up_pre_grad, preferred_element_type=jnp.float32
        )
        row_grad = jnp.einsum(
            "rf,df->rd", gate_pre_grad, gate_weight[0], preferred_element_type=jnp.float32
        )
        row_grad = row_grad + jnp.einsum(
            "rf,df->rd", up_pre_grad, up_weight[0], preferred_element_type=jnp.float32
        )
        row_grad = row_grad.astype(jnp.bfloat16).reshape(devices, capacity, model_width)
        expert_input_grad = jnp.sum(
            gather_back(reroute(row_grad), target, experts, capacity).reshape(
                block_rows, top_count, model_width
            ),
            axis=1,
        )
        router_float = router_full.astype(jnp.float32)
        expert_input_grad = expert_input_grad + jnp.dot(
            logits_grad, router_float.T, precision=PRECISE
        )
        router_term = jnp.dot(expert_input.astype(jnp.float32).T, logits_grad, precision=PRECISE)
        expert_gain_term = jnp.sum(expert_input_grad * normed_second, axis=0)
        middle_grad = upstream + norm_back(
            expert_input_grad * expert_gain_full, normed_second, scale_second
        )
        branch_grad = middle_grad.astype(jnp.bfloat16)
        attended_grad = jnp.einsum(
            "te,de->td", branch_grad, output_full, preferred_element_type=jnp.float32
        )
        attended_grad = attended_grad.astype(jnp.bfloat16).reshape(block_rows, HEADS, HDIM)
        probs_again = jnp.exp(scores_of() - log_total)
        prob_grad = jnp.einsum(
            "qhd,khd->hqk", attended_grad, values_all, preferred_element_type=jnp.float32
        )
        row_delta = jnp.sum(probs_again * prob_grad, axis=-1, keepdims=True)
        score_grad = (probs_again * (prob_grad - row_delta)).astype(jnp.bfloat16)
        query_rot_grad = (
            jnp.einsum("hqk,khd->qhd", score_grad, keys_all, preferred_element_type=jnp.float32)
            * score_scale
        )
        key_side = (
            jnp.einsum("hqk,qhd->khd", score_grad, query_rot, preferred_element_type=jnp.float32)
            * score_scale
        )
        value_side = jnp.einsum(
            "hqk,qhd->khd",
            probs_again.astype(jnp.bfloat16),
            attended_grad,
            preferred_element_type=jnp.float32,
        )
        key_rot_grad, value_own_grad = (
            lax.psum_scatter(
                key_side.astype(jnp.bfloat16), "shard", scatter_dimension=0, tiled=True
            ).astype(jnp.float32),
            lax.psum_scatter(
                value_side.astype(jnp.bfloat16), "shard", scatter_dimension=0, tiled=True
            ).astype(jnp.float32),
        )
        query_unit_grad = rotate(query_rot_grad, cosine_table, -sine_table)
        qgain_term = jnp.sum(query_unit_grad * query_unit, axis=(0, 1))
        query_proj_grad = (
            norm_back(query_unit_grad * qgain_full, query_unit, query_norm_scale)
            .astype(jnp.bfloat16)
            .reshape(block_rows, model_width)
        )
        key_unit_grad = rotate(key_rot_grad, cosine_table, -sine_table)
        kgain_term = jnp.sum(key_unit_grad * key_unit, axis=(0, 1))
        key_proj_grad = (
            norm_back(key_unit_grad * kgain_full, key_unit, key_norm_scale)
            .astype(jnp.bfloat16)
            .reshape(block_rows, model_width)
        )
        value_proj_grad = value_own_grad.astype(jnp.bfloat16).reshape(block_rows, model_width)
        mixer_grad = jnp.einsum(
            "te,de->td", query_proj_grad, query_full, preferred_element_type=jnp.float32
        )
        mixer_grad = mixer_grad + jnp.einsum(
            "te,de->td", key_proj_grad, key_full, preferred_element_type=jnp.float32
        )
        mixer_grad = mixer_grad + jnp.einsum(
            "te,de->td", value_proj_grad, value_full, preferred_element_type=jnp.float32
        )
        attn_gain_term = jnp.sum(mixer_grad * normed_first, axis=0)
        hidden_grad = middle_grad + norm_back(
            mixer_grad * attn_gain_full, normed_first, scale_first
        )
        input_rows.append(hidden_grad.astype(jnp.bfloat16))
        group_rows = (
            lax.all_gather(query_proj_grad, "shard", axis=0, tiled=True),
            lax.all_gather(key_proj_grad, "shard", axis=0, tiled=True),
            lax.all_gather(value_proj_grad, "shard", axis=0, tiled=True),
            lax.all_gather(branch_grad, "shard", axis=0, tiled=True),
            lax.all_gather(mixer_input, "shard", axis=0, tiled=True),
            lax.all_gather(attended, "shard", axis=0, tiled=True),
        )
        mixer_cols = lax.dynamic_slice_in_dim(
            group_rows[4], shard_place * column_width, column_width, 1
        )
        attended_cols = lax.dynamic_slice_in_dim(
            group_rows[5], shard_place * column_width, column_width, 1
        )
        own_terms = (
            jnp.einsum("td,te->de", mixer_cols, group_rows[0], preferred_element_type=jnp.float32),
            jnp.einsum("td,te->de", mixer_cols, group_rows[1], preferred_element_type=jnp.float32),
            jnp.einsum("td,te->de", mixer_cols, group_rows[2], preferred_element_type=jnp.float32),
            jnp.einsum(
                "td,te->de", attended_cols, group_rows[3], preferred_element_type=jnp.float32
            ),
        )
        other_terms = (router_term, attn_gain_term, expert_gain_term, qgain_term, kgain_term)
        row_totals = (
            own_terms if row_totals is None else jax.tree.map(jnp.add, row_totals, own_terms)
        )
        small_totals = (
            other_terms
            if small_totals is None
            else jax.tree.map(jnp.add, small_totals, other_terms)
        )
    small_shares = (
        lax.psum_scatter(
            small_totals[0].astype(jnp.bfloat16), "shard", scatter_dimension=0, tiled=True
        ).astype(jnp.float32),
        lax.psum_scatter(
            small_totals[1].astype(jnp.bfloat16), "shard", scatter_dimension=0, tiled=True
        ).astype(jnp.float32),
        lax.psum_scatter(
            small_totals[2].astype(jnp.bfloat16), "shard", scatter_dimension=0, tiled=True
        ).astype(jnp.float32),
        lax.psum_scatter(
            small_totals[3].astype(jnp.bfloat16), "shard", scatter_dimension=0, tiled=True
        ).astype(jnp.float32),
        lax.psum_scatter(
            small_totals[4].astype(jnp.bfloat16), "shard", scatter_dimension=0, tiled=True
        ).astype(jnp.float32),
    )
    shard_totals = (
        lax.psum(row_totals[0].astype(jnp.bfloat16), "expert").astype(jnp.float32),
        lax.psum(row_totals[1].astype(jnp.bfloat16), "expert").astype(jnp.float32),
        lax.psum(row_totals[2].astype(jnp.bfloat16), "expert").astype(jnp.float32),
        lax.psum(row_totals[3].astype(jnp.bfloat16), "expert").astype(jnp.float32),
        lax.psum(small_shares[0].astype(jnp.bfloat16), "expert").astype(jnp.float32),
        lax.psum(small_shares[1].astype(jnp.bfloat16), "expert").astype(jnp.float32),
        lax.psum(small_shares[2].astype(jnp.bfloat16), "expert").astype(jnp.float32),
        lax.psum(small_shares[3].astype(jnp.bfloat16), "expert").astype(jnp.float32),
        lax.psum(small_shares[4].astype(jnp.bfloat16), "expert").astype(jnp.float32),
    )
    return (
        jnp.stack(layer_rows),
        jnp.stack(input_rows),
        shard_totals[0],
        shard_totals[1],
        shard_totals[2],
        shard_totals[3],
        shard_totals[4],
        shard_totals[5],
        shard_totals[6],
        shard_totals[7],
        shard_totals[8],
        gate_sum[None],
        up_sum[None],
        down_sum[None],
    )


def solution(mesh):
    in_specs = (
        P(None, ("expert", "shard"), None),
        P(None, "expert"),
        P(None, ("expert", "shard"), None),
        P(None, ("expert", "shard"), None),
        P("shard", None),
        P("shard", None),
        P("shard", None),
        P("shard", None),
        P("shard", None),
        P("shard"),
        P("shard"),
        P("shard"),
        P("shard"),
        P(("expert", "shard"), None, None),
        P(("expert", "shard"), None, None),
        P(("expert", "shard"), None, None),
    )
    out_specs = (
        P(None, ("expert", "shard"), None),
        P(None, ("expert", "shard"), None),
        P("shard", None),
        P("shard", None),
        P("shard", None),
        P("shard", None),
        P("shard", None),
        P("shard"),
        P("shard"),
        P("shard"),
        P("shard"),
        P(("expert", "shard"), None, None),
        P(("expert", "shard"), None, None),
        P(("expert", "shard"), None, None),
    )
    return jax.shard_map(
        per_device, mesh=mesh, in_specs=in_specs, out_specs=out_specs, check_vma=False
    )
```

profile of v0, /device:TPU:11, one launch (start us, length us, event | category | flops | bytes accessed | tf_op | source)
XLA Modules:
  0.0 3462.5 jit_solution(8197560353341095256)
XLA Ops:
  42.0 91.5 %all-gather.29.cloned.1.call-done = bf16[2048,2048]{1,0:T(8,128)(2,1)} async-done(((bf16[256,2048]{1,0:T(8,128)(2,1)}), bf16[2048,2048]{1,0:T(8,128)(2,1)}) %all-gather.29.cloned.1.call-update) | async-done | bytes 8388624 | tf_op jit(solution)/shard_map/all_gather | solution.py:127
  145.8 112.9 %all-gather.27.cloned.1.call-done = bf16[2048,2048]{1,0:T(8,128)(2,1)} async-done(((bf16[256,2048]{1,0:T(8,128)(2,1)}), bf16[2048,2048]{1,0:T(8,128)(2,1)}) %all-gather.27.cloned.1.call-update) | async-done | bytes 8388624 | tf_op jit(solution)/shard_map/all_gather | solution.py:126
  294.5 89.5 %all-gather.23.cloned.1.call-done = bf16[2048,2048]{1,0:T(8,128)(2,1)} async-done(((bf16[256,2048]{1,0:T(8,128)(2,1)}), bf16[2048,2048]{1,0:T(8,128)(2,1)}) %all-gather.23.cloned.1.call-update) | async-done | bytes 8388624 | tf_op jit(solution)/shard_map/all_gather | solution.py:128
  488.8 121.3 %all-gather.33.cloned.1.call-done = bf16[2048,2048]{1,0:T(8,128)(2,1)} async-done(((bf16[256,2048]{1,0:T(8,128)(2,1)}), bf16[2048,2048]{1,0:T(8,128)(2,1)}) %all-gather.33.cloned.1.call-update) | async-done | bytes 8388624 | tf_op jit(solution)/shard_map/all_gather | solution.py:129
  637.0 198.5 %all_gather.94 = bf16[2048,16]{0,1:T(8,128)(2,1)S(1)} all-gather(bf16[256,16]{0,1:T(8,128)(2,1)S(1)} %copy-done.129), channel_id=1, replica_groups=mesh['expert'=4,'shard'=8] {'shard'}, dimensions={0}, use_global_device_ids=true | all-gather | bytes 73728 | tf_op jit(solution)/shard_map/all_gather | solution.py:130
  891.1 164.4 %all-to-all-done.4 = bf16[32,64,2048]{2,1,0:T(8,128)(2,1)} async-done(((bf16[32,64,2048]{2,1,0:T(8,128)(2,1)}), bf16[32,64,2048]{2,1,0:T(8,128)(2,1)}, u32[]{:S(2)}, u32[]{:S(2)}) %all-to-all-start.4) | async-done | bytes 8388640 | tf_op jit(solution)/shard_map/all_to_all | solution.py:83
  1109.6 157.2 %all-to-all-done.1 = bf16[32,64,2048]{2,1,0:T(8,128)(2,1)} async-done(((bf16[32,64,2048]{2,1,0:T(8,128)(2,1)}), bf16[32,64,2048]{2,1,0:T(8,128)(2,1)}, u32[]{:S(2)}, u32[]{:S(2)}) %all-to-all-start.1) | async-done | bytes 8388640 | tf_op jit(solution)/shard_map/all_to_all | solution.py:83
  1283.0 76.8 %all-gather.37.cloned.1.call-done = bf16[512,16,128]{2,0,1:T(8,128)(2,1)} async-done(((bf16[64,16,128]{2,0,1:T(8,128)(2,1)}), bf16[512,16,128]{2,0,1:T(8,128)(2,1)}) %all-gather.37.cloned.1.call-update) | async-done | bytes 2097168 | tf_op jit(solution)/shard_map/all_gather | solution.py:169
  1364.5 119.8 %all-gather.35.cloned.1.call-done = bf16[512,16,128]{2,0,1:T(8,128)(2,1)} async-done(((bf16[64,16,128]{2,0,1:T(8,128)(2,1)}), bf16[512,16,128]{2,0,1:T(8,128)(2,1)}) %all-gather.35.cloned.1.call-update) | async-done | bytes 2097168 | tf_op jit(solution)/shard_map/all_gather | solution.py:170
  1598.6 172.1 %all-to-all-done.2 = bf16[32,64,2048]{2,1,0:T(8,128)(2,1)} async-done(((bf16[32,64,2048]{2,1,0:T(8,128)(2,1)}), bf16[32,64,2048]{2,1,0:T(8,128)(2,1)}, u32[]{:S(2)}, u32[]{:S(2)}) %all-to-all-start.2) | async-done | bytes 8388640 | tf_op jit(solution)/shard_map/all_to_all | solution.py:83
  1804.7 164.8 %all-to-all-done.6 = bf16[32,64,2048]{2,1,0:T(8,128)(2,1)} async-done(((bf16[32,64,2048]{2,1,0:T(8,128)(2,1)}), bf16[32,64,2048]{2,1,0:T(8,128)(2,1)}, u32[]{:S(2)}, u32[]{:S(2)}) %all-to-all-start.6) | async-done | bytes 8388640 | tf_op jit(solution)/shard_map/all_to_all | solution.py:83
  2020.5 159.9 %all-to-all-done.3 = bf16[32,64,2048]{2,1,0:T(8,128)(2,1)} async-done(((bf16[32,64,2048]{2,1,0:T(8,128)(2,1)}), bf16[32,64,2048]{2,1,0:T(8,128)(2,1)}, u32[]{:S(2)}, u32[]{:S(2)}) %all-to-all-start.3) | async-done | bytes 8388640 | tf_op jit(solution)/shard_map/all_to_all | solution.py:83
  2224.3 147.8 %all-to-all-done.7 = bf16[32,64,2048]{2,1,0:T(8,128)(2,1)} async-done(((bf16[32,64,2048]{2,1,0:T(8,128)(2,1)}), bf16[32,64,2048]{2,1,0:T(8,128)(2,1)}, u32[]{:S(2)}, u32[]{:S(2)}) %all-to-all-start.7) | async-done | bytes 8388640 | tf_op jit(solution)/shard_map/all_to_all | solution.py:83
  2496.4 65.1 %reduce-scatter.6.cloned.1.call-done = bf16[64,16,128]{2,0,1:T(8,128)(2,1)} async-done(((bf16[512,16,128]{2,0,1:T(8,128)(2,1)}), bf16[64,16,128]{2,0,1:T(8,128)(2,1)}) %reduce-scatter.6.cloned.1.call-update) | async-done | bytes 262160 | tf_op jit(solution)/shard_map/reduce_scatter | solution.py:298
  2563.3 69.7 %reduce-scatter.10.cloned.1.call-done = bf16[64,16,128]{2,0,1:T(8,128)(2,1)} async-done(((bf16[512,16,128]{2,0,1:T(8,128)(2,1)}), bf16[64,16,128]{2,0,1:T(8,128)(2,1)}) %reduce-scatter.10.cloned.1.call-update) | async-done | bytes 262160 | tf_op jit(solution)/shard_map/reduce_scatter | solution.py:298
  2649.9 53.9 %reduce-scatter.12.cloned.1.call-done = bf16[64,16,128]{2,1,0:T(8,128)(2,1)} async-done(((bf16[512,16,128]{2,1,0:T(8,128)(2,1)}), bf16[64,16,128]{2,1,0:T(8,128)(2,1)}) %reduce-scatter.12.cloned.1.call-update) | async-done | bytes 262160 | tf_op jit(solution)/shard_map/reduce_scatter | solution.py:301
  2808.1 46.0 %all-gather.59.cloned.1.call-done = bf16[512,2048]{1,0:T(8,128)(2,1)} async-done(((bf16[64,2048]{1,0:T(8,128)(2,1)}), bf16[512,2048]{1,0:T(8,128)(2,1)}) %all-gather.59.cloned.1.call-update) | async-done | bytes 2097168 | tf_op jit(solution)/shard_map/all_gather | solution.py:340
  2854.1 49.8 %all-gather.61.cloned.1.call-done = bf16[512,2048]{1,0:T(8,128)(2,1)} async-done(((bf16[64,2048]{1,0:T(8,128)(2,1)}), bf16[512,2048]{1,0:T(8,128)(2,1)}) %all-gather.61.cloned.1.call-update) | async-done | bytes 2097168 | tf_op jit(solution)/shard_map/all_gather | solution.py:338
  2953.7 49.8 %all-gather.51.cloned.1.call-done = bf16[512,2048]{1,0:T(8,128)(2,1)} async-done(((bf16[64,2048]{1,0:T(8,128)(2,1)}), bf16[512,2048]{1,0:T(8,128)(2,1)}) %all-gather.51.cloned.1.call-update) | async-done | bytes 2097168 | tf_op jit(solution)/shard_map/all_gather | solution.py:337
  3007.3 46.2 %all-gather.47.cloned.1.call-done = bf16[512,2048]{1,0:T(8,128)(2,1)} async-done(((bf16[64,2048]{1,0:T(8,128)(2,1)}), bf16[512,2048]{1,0:T(8,128)(2,1)}) %all-gather.47.cloned.1.call-update) | async-done | bytes 2097168 | tf_op jit(solution)/shard_map/all_gather | solution.py:336
  3057.2 46.0 %all-gather.41.cloned.1.call-done = bf16[512,2048]{1,0:T(8,128)(2,1)} async-done(((bf16[64,2048]{1,0:T(8,128)(2,1)}), bf16[512,2048]{1,0:T(8,128)(2,1)}) %all-gather.41.cloned.1.call-update) | async-done | bytes 2097168 | tf_op jit(solution)/shard_map/all_gather | solution.py:335
  3107.0 46.2 %all-gather.43.cloned.1.call-done = bf16[512,2048]{1,0:T(8,128)(2,1)} async-done(((bf16[64,2048]{1,0:T(8,128)(2,1)}), bf16[512,2048]{1,0:T(8,128)(2,1)}) %all-gather.43.cloned.1.call-update) | async-done | bytes 2097168 | tf_op jit(solution)/shard_map/all_gather | solution.py:339
  3153.2 49.9 %all-gather.53.cloned.1.call-done = bf16[512,2048]{1,0:T(8,128)(2,1)} async-done(((bf16[64,2048]{1,0:T(8,128)(2,1)}), bf16[512,2048]{1,0:T(8,128)(2,1)}) %all-gather.53.cloned.1.call-update) | async-done | bytes 2097168 | tf_op jit(solution)/shard_map/all_gather | solution.py:337
  3376.6 71.4 %all-reduce.16.cloned.1.call-done = (bf16[256,2048]{1,0:T(8,128)(2,1)}, bf16[256,2048]{1,0:T(8,128)(2,1)}, bf16[256,2048]{1,0:T(8,128)(2,1)}, bf16[256,2048]{1,0:T(8,128)(2,1)}) async-done(((bf16[256,2048]{1,0:T(8,128)(2,1)}, bf16[256,2048]{1,0:T(8,128)(2,1)}, bf16[256,2048]{1,0:T(8,128)(2,1)}, bf16[256,2048]{1,0:T(8,128)(2,1)}), (bf16[256,2048]{1,0:T(8,128)(2,1)}, bf16[256,2048]{1,0:T(8,128)(2,1)}, ...) | async-done | bytes 4194320 | tf_op jit(solution)/shard_map/psum | solution.py:383
  (651 shorter events, 1073.0 us)
Async XLA Ops:
  8.0 250.8 %all-gather.27.cloned.1.call-start = ((), (), s32[]{:S(2)}) async-start(), calls=%async_computation.15 | async-start | bytes 9437184 | tf_op jit(solution)/shard_map/all_gather | solution.py:126
  8.7 375.3 %all-gather.23.cloned.1.call-start = ((), (), s32[]{:S(2)}) async-start(), calls=%async_computation.13 | async-start | bytes 9437184 | tf_op jit(solution)/shard_map/all_gather | solution.py:128
  9.5 426.1 %all-gather.31.cloned.1.call-start = ((), (), s32[]{:S(2)}) async-start(), calls=%async_computation.17 | async-start | bytes 2359296 | tf_op jit(solution)/shard_map/all_gather | solution.py:169
  389.9 220.3 %all-gather.33.cloned.1.call-start = ((), (), s32[]{:S(2)}) async-start(), calls=%async_computation.18 | async-start | bytes 9437184 | tf_op jit(solution)/shard_map/all_gather | solution.py:129
  629.7 220.9 %all-to-all-start = ((bf16[32,64,2048]{2,1,0:T(8,128)(2,1)}), bf16[32,64,2048]{2,1,0:T(8,128)(2,1)}, u32[]{:S(2)}, u32[]{:S(2)}) async-start(bf16[32,64,2048]{2,1,0:T(8,128)(2,1)} %bitcast.479), calls=%async_computation | async-start | bytes 16777216 | tf_op jit(solution)/shard_map/all_to_all | solution.py:83
  1266.8 262.9 %all-to-all-start.5 = ((bf16[32,64,2048]{2,1,0:T(8,128)(2,1)}), bf16[32,64,2048]{2,1,0:T(8,128)(2,1)}, u32[]{:S(2)}, u32[]{:S(2)}) async-start(bf16[32,64,2048]{2,1,0:T(8,128)(2,1)} %bitcast.487), calls=%async_computation.5 | async-start | bytes 16777216 | tf_op jit(solution)/shard_map/all_to_all | solution.py:83
  1274.4 209.9 %all-gather.35.cloned.1.call-start = ((), (), s32[]{:S(2)}) async-start(), calls=%async_computation.19 | async-start | bytes 2359296 | tf_op jit(solution)/shard_map/all_gather | solution.py:170
  2187.2 303.0 %reduce-scatter.8.cloned.1.call-start = ((), (), s32[]{:S(2)}) async-start(), calls=%async_computation.22 | async-start | bytes 2359296 | tf_op jit(solution)/shard_map/reduce_scatter | solution.py:301
  2429.2 203.7 %reduce-scatter.10.cloned.1.call-start = ((), (), s32[]{:S(2)}) async-start(), calls=%async_computation.23 | async-start | bytes 2359296 | tf_op jit(solution)/shard_map/reduce_scatter | solution.py:298
  2440.6 263.1 %reduce-scatter.12.cloned.1.call-start = ((), (), s32[]{:S(2)}) async-start(), calls=%async_computation.24 | async-start | bytes 2359296 | tf_op jit(solution)/shard_map/reduce_scatter | solution.py:301
  2447.5 326.2 %all-gather.55.cloned.1.call-start = ((), (), s32[]{:S(2)}) async-start(), calls=%async_computation.33 | async-start | bytes 2359296 | tf_op jit(solution)/shard_map/all_gather | solution.py:340
  2449.2 355.1 %all-gather.57.cloned.1.call-start = ((), (), s32[]{:S(2)}) async-start(), calls=%async_computation.34 | async-start | bytes 2359296 | tf_op jit(solution)/shard_map/all_gather | solution.py:338
  2449.8 404.3 %all-gather.59.cloned.1.call-start = ((), (), s32[]{:S(2)}) async-start(), calls=%async_computation.35 | async-start | bytes 2359296 | tf_op jit(solution)/shard_map/all_gather | solution.py:340
  2450.6 453.2 %all-gather.61.cloned.1.call-start = ((), (), s32[]{:S(2)}) async-start(), calls=%async_computation.36 | async-start | bytes 2359296 | tf_op jit(solution)/shard_map/all_gather | solution.py:338
  2451.2 502.5 %all-gather.39.cloned.1.call-start = ((), (), s32[]{:S(2)}) async-start(), calls=%async_computation.25 | async-start | bytes 2359296 | tf_op jit(solution)/shard_map/all_gather | solution.py:339
  2451.8 551.7 %all-gather.51.cloned.1.call-start = ((), (), s32[]{:S(2)}) async-start(), calls=%async_computation.31 | async-start | bytes 2359296 | tf_op jit(solution)/shard_map/all_gather | solution.py:337
  2491.9 561.6 %all-gather.47.cloned.1.call-start = ((), (), s32[]{:S(2)}) async-start(), calls=%async_computation.29 | async-start | bytes 2359296 | tf_op jit(solution)/shard_map/all_gather | solution.py:336
  2641.1 462.2 %all-gather.41.cloned.1.call-start = ((), (), s32[]{:S(2)}) async-start(), calls=%async_computation.26 | async-start | bytes 2359296 | tf_op jit(solution)/shard_map/all_gather | solution.py:335
  2647.8 505.4 %all-gather.43.cloned.1.call-start = ((), (), s32[]{:S(2)}) async-start(), calls=%async_computation.27 | async-start | bytes 2359296 | tf_op jit(solution)/shard_map/all_gather | solution.py:339
  2648.5 554.6 %all-gather.53.cloned.1.call-start = ((), (), s32[]{:S(2)}) async-start(), calls=%async_computation.32 | async-start | bytes 2359296 | tf_op jit(solution)/shard_map/all_gather | solution.py:337
  2705.5 547.6 %all-gather.49.cloned.1.call-start = ((), (), s32[]{:S(2)}) async-start(), calls=%async_computation.30 | async-start | bytes 2359296 | tf_op jit(solution)/shard_map/all_gather | solution.py:336
  2727.6 575.3 %all-gather.45.cloned.1.call-start = ((), (), s32[]{:S(2)}) async-start(), calls=%async_computation.28 | async-start | bytes 2359296 | tf_op jit(solution)/shard_map/all_gather | solution.py:335
  2750.1 607.6 %reduce-scatter.14.cloned.1.call-start = ((), (), s32[]{:S(2)}) async-start(), calls=%async_computation.37 | async-start | bytes 73728 | tf_op jit(solution)/shard_map/reduce_scatter | solution.py:366
  2773.4 674.6 %all-reduce.16.cloned.1.call-start = ((), (), s32[]{:S(2)}) async-start(), calls=%async_computation.38 | async-start | bytes 8388608 | tf_op jit(solution)/shard_map/psum | solution.py:383
  (179 other events, 9342.6 us)
Sparse Core Ops, SparseCore 0:
  10.2 123.2 all-gather.28
  135.6 123.1 all-gather.26
  260.9 123.0 all-gather.22
  386.7 48.8 all-gather.30
  488.0 122.1 all-gather.32
  1277.1 82.6 all-gather.36
  1362.6 121.6 all-gather.34
  2422.9 67.2 reduce-scatter.7
  2494.1 67.2 reduce-scatter.5
  2565.6 67.3 reduce-scatter.9
  2636.9 66.7 reduce-scatter.11
  2705.9 48.6 all-gather.54
  2756.5 47.7 all-gather.56
  2806.3 47.7 all-gather.58
  2856.1 47.7 all-gather.60
  2905.9 47.7 all-gather.38
  2955.7 47.8 all-gather.50
  3005.7 47.7 all-gather.46
  3055.5 47.7 all-gather.40
  3105.4 47.7 all-gather.42
  3205.3 47.7 all-gather.48
  3255.1 47.7 all-gather.44
  3306.0 51.6 reduce-scatter.13
  3360.6 87.2 all-reduce.15
  (2 shorter events, 95.4 us)
where the time goes:
time: 3470 us; the launch traced here: 3460 us
  waiting for transfers between devices  2470 us (71%)
  matrix products  334 us (10%)
  blocking collectives  267 us (8%)
  local copies, waits for them, and re-layouts  160 us (5%)
  other arithmetic  154 us (4%)
  starting transfers between devices  63.5 us (2%)
    all_to_all x8, waiting for transfers between devices, reroute(): lax.all_to_all(blocks, ('expert', 'shard'), split_axis=0, concat_axis=0,...  966 us
    all_gather x1, blocking collectives, per_device(): lax.all_gather(router_weight, 'shard', axis=0, tiled=True)  199 us
    all_gather x2, waiting for transfers between devices, per_device(): lax.all_gather(value_low, 'shard', axis=0, tiled=True)  166 us
    reduce_scatter x2, waiting for transfers between devices, per_device(): lax.psum_scatter(key_side.astype(jnp.bfloat16), 'shard', scatter_dimensio...  135 us
    all_gather x1, waiting for transfers between devices, per_device(): lax.all_gather(output_weight, 'shard', axis=0, tiled=True)  121 us
    all_gather x1, waiting for transfers between devices, per_device(): lax.all_gather(query_weight, 'shard', axis=0, tiled=True)  113 us
    all_gather x2, waiting for transfers between devices, per_device(): lax.all_gather(key_rot, 'shard', axis=0, tiled=True)  101 us
    all_gather x2, waiting for transfers between devices, per_device(): lax.all_gather(value_proj_grad, 'shard', axis=0, tiled=True)  99.8 us
  transfers between devices with their start and end apart: 34, of which 31 were waited for; matrix products, arithmetic and copies ran while one was open for 13% of the time, Pallas kernels for 0%

commit v1 on v0

v1 whole, which is shorter than its diff:
```python
import functools
import math

import jax
import jax.numpy as jnp
from jax import lax
from jax.experimental import pallas as pl
from jax.experimental.pallas import tpu as pltpu
from jax.sharding import PartitionSpec as P

HDIM = 128
EPSILON = 1e-05
ROPE_BASE = 10000.0
MASK_FILL = -1e30
PRECISE = lax.Precision.HIGHEST
MESH = pl.DeviceIdType.MESH
F32 = jnp.float32
BF16 = jnp.bfloat16
NN = (((1,), (0,)), ((), ()))
NT = (((1,), (1,)), ((), ()))
TN = (((0,), (0,)), ((), ()))
VMEM_LIMIT = 60 << 20


def dot(left, right, dims):
    return lax.dot_general(left, right, dims, preferred_element_type=F32)


def rms_scale(values):
    return lax.rsqrt(jnp.mean(values * values, axis=-1, keepdims=True) + EPSILON)


def norm_back(normed_grad, normed, inv_scale):
    return inv_scale * (
        normed_grad - normed * jnp.mean(normed_grad * normed, axis=-1, keepdims=True)
    )


def rotary(places, head_width):
    half_width = head_width // 2
    steps_float = jnp.arange(half_width, dtype=jnp.int32).astype(F32)
    freqs = jnp.power(ROPE_BASE, -2.0 * steps_float / head_width)
    theta = places[:, None] * freqs[None, :]
    return (jnp.cos(theta)[:, None, :], jnp.sin(theta)[:, None, :])


def rotate(values, cosine_table, sine_table):
    half_width = values.shape[-1] // 2
    front = values[..., :half_width]
    behind = values[..., half_width:]
    return jnp.concatenate(
        [front * cosine_table - behind * sine_table, behind * cosine_table + front * sine_table],
        axis=-1,
    )


def softmax_rows(scores):
    row_peak = jnp.max(scores, axis=-1, keepdims=True)
    exponent = jnp.exp(scores - row_peak)
    return exponent / jnp.sum(exponent, axis=-1, keepdims=True)


def group_place(wide):
    shard_place = lax.axis_index("shard")
    return lax.axis_index("expert"), shard_place // wide, lax.rem(shard_place, wide)


def greet(group, row, column, deep, wide):
    barrier = pltpu.get_barrier_semaphore()
    for step in range(1, deep):
        pl.semaphore_signal(
            barrier,
            inc=1,
            device_id=(group, lax.rem(row + step, deep) * wide + column),
            device_id_type=MESH,
        )
    for step in range(1, wide):
        pl.semaphore_signal(
            barrier,
            inc=1,
            device_id=(group, row * wide + lax.rem(column + step, wide)),
            device_id_type=MESH,
        )
    pl.semaphore_wait(barrier, deep + wide - 2)


def gather_kernel(deep, wide, own, whole, row_send, row_recv, col_send, col_recv, local):
    group, row, column = group_place(wide)
    me = row * wide + column
    greet(group, row, column, deep, wide)
    pieces = own.shape[0]
    here = pltpu.make_async_copy(own, whole.at[:, me], local)
    here.start()
    sends = []

    def along_row(piece, turn, block, place):
        for step in range(1, wide):
            copy = pltpu.make_async_remote_copy(
                src_ref=block,
                dst_ref=whole.at[piece, place],
                send_sem=col_send.at[piece, turn, step - 1],
                recv_sem=col_recv.at[piece, turn, step - 1],
                device_id=(group, row * wide + lax.rem(column + step, wide)),
                device_id_type=MESH,
            )
            copy.start()
            sends.append(copy)

    def along_column(piece, step, place):
        return pltpu.make_async_remote_copy(
            src_ref=own.at[piece],
            dst_ref=whole.at[piece, place],
            send_sem=row_send.at[piece, step - 1],
            recv_sem=row_recv.at[piece, step - 1],
            device_id=(group, lax.rem(row + step, deep) * wide + column),
            device_id_type=MESH,
        )

    for piece in range(pieces):
        for step in range(1, deep):
            copy = along_column(piece, step, me)
            copy.start()
            sends.append(copy)
        along_row(piece, 0, own.at[piece], me)
    for piece in range(pieces):
        for step in range(1, deep):
            place = lax.rem(row - step + deep, deep) * wide + column
            along_column(piece, step, place).wait_recv()
            along_row(piece, step, whole.at[piece, place], place)
    for piece in range(pieces):
        for turn in range(deep):
            for step in range(1, wide):
                place = (
                    lax.rem(row - turn + deep, deep) * wide
                    + lax.rem(column - step + wide, wide)
                )
                pltpu.make_async_remote_copy(
                    src_ref=own.at[piece],
                    dst_ref=whole.at[piece, place],
                    send_sem=col_send.at[piece, turn, step - 1],
                    recv_sem=col_recv.at[piece, turn, step - 1],
                    device_id=(group, row * wide + lax.rem(column + step, wide)),
                    device_id_type=MESH,
                ).wait_recv()
    for copy in sends:
        copy.wait_send()
    here.wait()


def group_gather(own, deep, wide, collective_id):
    pieces, rows, width = own.shape
    return pl.pallas_call(
        functools.partial(gather_kernel, deep, wide),
        out_shape=jax.ShapeDtypeStruct((pieces, deep * wide, rows, width), own.dtype),
        in_specs=[pl.BlockSpec(memory_space=pl.ANY)],
        out_specs=pl.BlockSpec(memory_space=pl.ANY),
        scratch_shapes=[
            pltpu.SemaphoreType.DMA((pieces, deep - 1)),
            pltpu.SemaphoreType.DMA((pieces, deep - 1)),
            pltpu.SemaphoreType.DMA((pieces, deep, max(1, wide - 1))),
            pltpu.SemaphoreType.DMA((pieces, deep, max(1, wide - 1))),
            pltpu.SemaphoreType.DMA,
        ],
        compiler_params=pltpu.CompilerParams(
            collective_id=collective_id, has_side_effects=True, vmem_limit_bytes=VMEM_LIMIT
        ),
    )(own)


def scatter_kernel(
    deep, wide, parts, total, landed, merged, summed, col_send, col_recv, row_send, row_recv
):
    group, row, column = group_place(wide)
    greet(group, row, column, deep, wide)
    pieces = parts.shape[0]
    sends = []

    def target_row(turn):
        return lax.rem(row + turn + 1, deep)

    def along_row(piece, turn, step):
        return pltpu.make_async_remote_copy(
            src_ref=parts.at[piece, target_row(turn) * wide + lax.rem(column + step, wide)],
            dst_ref=landed.at[piece, turn, step - 1],
            send_sem=col_send.at[piece, turn, step - 1],
            recv_sem=col_recv.at[piece, turn, step - 1],
            device_id=(group, row * wide + lax.rem(column + step, wide)),
            device_id_type=MESH,
        )

    def along_column(piece, turn):
        return pltpu.make_async_remote_copy(
            src_ref=merged.at[piece, turn],
            dst_ref=summed.at[piece, turn],
            send_sem=row_send.at[piece, turn],
            recv_sem=row_recv.at[piece, turn],
            device_id=(group, target_row(turn) * wide + column),
            device_id_type=MESH,
        )

    for piece in range(pieces):
        for turn in range(deep):
            for step in range(1, wide):
                copy = along_row(piece, turn, step)
                copy.start()
                sends.append(copy)
    for piece in range(pieces):
        for turn in range(deep):
            value = parts[piece, target_row(turn) * wide + column].astype(F32)
            for step in range(1, wide):
                along_row(piece, turn, step).wait_recv()
                value = value + landed[piece, turn, step - 1].astype(F32)
            if turn < deep - 1:
                merged[piece, turn] = value.astype(BF16)
                copy = along_column(piece, turn)
                copy.start()
                sends.append(copy)
            else:
                total[piece] = value
    for piece in range(pieces):
        value = total[piece]
        for turn in range(deep - 1):
            along_column(piece, turn).wait_recv()
            value = value + summed[piece, turn].astype(F32)
        total[piece] = value
    for copy in sends:
        copy.wait_send()


def group_scatter(parts, deep, wide, collective_id):
    pieces, _, rows, width = parts.shape
    return pl.pallas_call(
        functools.partial(scatter_kernel, deep, wide),
        out_shape=jax.ShapeDtypeStruct((pieces, rows, width), F32),
        in_specs=[pl.BlockSpec(memory_space=pltpu.VMEM)],
        out_specs=pl.BlockSpec(memory_space=pltpu.VMEM),
        scratch_shapes=[
            pltpu.VMEM((pieces, deep, max(1, wide - 1), rows, width), BF16),
            pltpu.VMEM((pieces, deep - 1, rows, width), BF16),
            pltpu.VMEM((pieces, deep - 1, rows, width), BF16),
            pltpu.SemaphoreType.DMA((pieces, deep, max(1, wide - 1))),
            pltpu.SemaphoreType.DMA((pieces, deep, max(1, wide - 1))),
            pltpu.SemaphoreType.DMA((pieces, deep - 1)),
            pltpu.SemaphoreType.DMA((pieces, deep - 1)),
        ],
        compiler_params=pltpu.CompilerParams(
            collective_id=collective_id, has_side_effects=True, vmem_limit_bytes=VMEM_LIMIT
        ),
    )(parts)


def units_kernel(
    span,
    rows_ref,
    upstream_ref,
    share_ref,
    gate_ref,
    up_ref,
    down_ref,
    hidden_ref,
    gate_pre_ref,
    up_pre_ref,
    dot_ref,
):
    half = pl.program_id(0)
    half_width = gate_ref.shape[2]
    lanes = lax.broadcasted_iota(jnp.int32, share_ref.shape, 1)
    share = jnp.sum(jnp.where(lanes == half, share_ref[...], 0.0), axis=1, keepdims=True)

    def body(step, carry):
        units = pl.ds(pl.multiple_of(step * span, span), span)
        gate_pre = dot(rows_ref[...], gate_ref[0, :, units], NN)
        up_pre = dot(rows_ref[...], up_ref[0, :, units], NN)
        units_grad = dot(upstream_ref[...], down_ref[0, units, :], NT)
        sigmoid_gate = 1.0 / (1.0 + jnp.exp(-gate_pre))
        swish_gate = gate_pre * sigmoid_gate
        activated = swish_gate * up_pre
        dots = jnp.sum(activated * units_grad, axis=1, keepdims=True)
        dot_ref[...] += jnp.where(lanes == half, dots, 0.0)
        hidden_ref[0, :, units] = (activated * share).astype(BF16)
        weighted = units_grad * share
        gate_pre_ref[0, :, units] = (
            weighted * up_pre * (sigmoid_gate * (1.0 + gate_pre * (1.0 - sigmoid_gate)))
        ).astype(BF16)
        up_pre_ref[0, :, units] = (weighted * swish_gate).astype(BF16)
        return carry

    @pl.when(half == 0)
    def _():
        dot_ref[...] = jnp.zeros_like(dot_ref)

    lax.fori_loop(0, half_width // span, body, 0)


def expert_units(rows, upstream, share, gate_all, up_all, down_all):
    tokens, width = rows.shape
    halves, _, units = gate_all.shape

    def each(*shape):
        return pl.BlockSpec((1,) + shape, lambda half: (half,) + (0,) * len(shape))

    whole = pl.BlockSpec(memory_space=pltpu.VMEM)
    return pl.pallas_call(
        functools.partial(units_kernel, 256 if tokens <= 1024 else 128),
        grid=(halves,),
        in_specs=[whole, whole, whole, each(width, units), each(width, units), each(units, width)],
        out_specs=[each(tokens, units), each(tokens, units), each(tokens, units), whole],
        out_shape=[
            jax.ShapeDtypeStruct((halves, tokens, units), BF16),
            jax.ShapeDtypeStruct((halves, tokens, units), BF16),
            jax.ShapeDtypeStruct((halves, tokens, units), BF16),
            jax.ShapeDtypeStruct(share.shape, F32),
        ],
        compiler_params=pltpu.CompilerParams(vmem_limit_bytes=VMEM_LIMIT),
        cost_estimate=pl.CostEstimate(
            flops=6 * tokens * width * units * halves,
            bytes_accessed=6 * width * units * halves,
            transcendentals=0,
        ),
    )(rows, upstream, share, gate_all, up_all, down_all)


def merge_kernel(gate_pre_ref, up_pre_ref, gate_ref, up_ref, grad_ref):
    halves = gate_pre_ref.shape[0]
    grad = dot(gate_pre_ref[0], gate_ref[0], NT) + dot(up_pre_ref[0], up_ref[0], NT)
    for half in range(1, halves):
        grad = grad + dot(gate_pre_ref[half], gate_ref[half], NT)
        grad = grad + dot(up_pre_ref[half], up_ref[half], NT)
    grad_ref[...] = grad.astype(BF16)


def expert_merge(gate_pre, up_pre, gate_all, up_all):
    halves, tokens, units = gate_pre.shape
    width = gate_all.shape[1]
    span = 256
    batch = min(tokens, 1024)
    slab = pl.BlockSpec(
        (halves, batch, units), lambda turn, step: (0, turn, 0), pipeline_mode=pl.Buffered(1)
    )
    tile = pl.BlockSpec((halves, span, units), lambda turn, step: (0, step, 0))
    return pl.pallas_call(
        merge_kernel,
        grid=(tokens // batch, width // span),
        in_specs=[slab, slab, tile, tile],
        out_specs=pl.BlockSpec((batch, span), lambda turn, step: (turn, step)),
        out_shape=jax.ShapeDtypeStruct((tokens, width), BF16),
        compiler_params=pltpu.CompilerParams(vmem_limit_bytes=VMEM_LIMIT),
        cost_estimate=pl.CostEstimate(
            flops=4 * tokens * width * units * halves,
            bytes_accessed=4 * width * units * halves,
            transcendentals=0,
        ),
    )(gate_pre, up_pre, gate_all, up_all)


def output_kernel(hidden_ref, down_ref, out_ref):
    halves = hidden_ref.shape[0]
    out = dot(hidden_ref[0], down_ref[0], NN)
    for half in range(1, halves):
        out = out + dot(hidden_ref[half], down_ref[half], NN)
    out_ref[...] = out.astype(BF16)


def expert_output(hidden, down_all):
    halves, tokens, units = hidden.shape
    width = down_all.shape[2]
    span = 256
    batch = min(tokens, 1024)
    slab = pl.BlockSpec(
        (halves, batch, units), lambda turn, step: (0, turn, 0), pipeline_mode=pl.Buffered(1)
    )
    return pl.pallas_call(
        output_kernel,
        grid=(tokens // batch, width // span),
        in_specs=[slab, pl.BlockSpec((halves, units, span), lambda turn, step: (0, 0, step))],
        out_specs=pl.BlockSpec((batch, span), lambda turn, step: (turn, step)),
        out_shape=jax.ShapeDtypeStruct((tokens, width), BF16),
        compiler_params=pltpu.CompilerParams(vmem_limit_bytes=VMEM_LIMIT),
        cost_estimate=pl.CostEstimate(
            flops=2 * tokens * width * units * halves,
            bytes_accessed=2 * width * units * halves,
            transcendentals=0,
        ),
    )(hidden, down_all)


def weights_kernel(
    span,
    rows_ref,
    upstream_ref,
    hidden_ref,
    gate_pre_ref,
    up_pre_ref,
    gate_grad_ref,
    up_grad_ref,
    down_grad_ref,
):
    def body(step, carry):
        units = pl.ds(pl.multiple_of(step * span, span), span)
        gate_grad_ref[0, :, units] = dot(rows_ref[...], gate_pre_ref[0, :, units], TN).astype(BF16)
        up_grad_ref[0, :, units] = dot(rows_ref[...], up_pre_ref[0, :, units], TN).astype(BF16)
        down_grad_ref[0, units, :] = dot(
            hidden_ref[0, :, units], upstream_ref[...], TN
        ).astype(BF16)
        return carry

    lax.fori_loop(0, gate_grad_ref.shape[2] // span, body, 0)


def expert_weights(rows, upstream, hidden, gate_pre, up_pre):
    tokens, width = rows.shape
    halves, _, units = hidden.shape

    def each(*shape):
        return pl.BlockSpec((1,) + shape, lambda half: (half,) + (0,) * len(shape))

    whole = pl.BlockSpec(memory_space=pltpu.VMEM)
    slab = each(tokens, units)
    return pl.pallas_call(
        functools.partial(weights_kernel, 256),
        grid=(halves,),
        in_specs=[whole, whole, slab, slab, slab],
        out_specs=[each(width, units), each(width, units), each(units, width)],
        out_shape=[
            jax.ShapeDtypeStruct((halves, width, units), BF16),
            jax.ShapeDtypeStruct((halves, width, units), BF16),
            jax.ShapeDtypeStruct((halves, units, width), BF16),
        ],
        compiler_params=pltpu.CompilerParams(vmem_limit_bytes=VMEM_LIMIT),
        cost_estimate=pl.CostEstimate(
            flops=6 * tokens * width * units * halves,
            bytes_accessed=6 * width * units * halves,
            transcendentals=0,
        ),
    )(rows, upstream, hidden, gate_pre, up_pre)


def per_device(
    groups,
    shards,
    wide,
    inputs,
    segment_ids,
    routes,
    cotangent,
    query_weight,
    key_weight,
    value_weight,
    output_weight,
    router_weight,
    attention_gain,
    expert_gain,
    query_gain,
    key_gain,
    gate_weight,
    up_weight,
    down_weight,
):
    micros, rows, width = inputs.shape
    deep = shards // wide
    span = shards * rows
    tokens = micros * span
    experts = router_weight.shape[1]
    column_width = width // shards
    heads = column_width // HDIM
    score_scale = 1.0 / math.sqrt(HDIM)
    shard_place = lax.axis_index("shard")

    gate_all = lax.all_gather(gate_weight, "expert", axis=0, tiled=True)
    up_all = lax.all_gather(up_weight, "expert", axis=0, tiled=True)
    down_all = lax.all_gather(down_weight, "expert", axis=0, tiled=True)

    small_own = jnp.concatenate(
        [router_weight.reshape(-1), attention_gain, expert_gain, query_gain, key_gain]
    )
    small = lax.all_gather(small_own, "shard", axis=0)
    cuts = [column_width * experts, column_width, column_width, HDIM // shards, HDIM // shards]
    starts = [sum(cuts[:place]) for place in range(len(cuts))]
    router_full, attn_gain, expert_gain_full, query_gain_full, key_gain_full = (
        small[:, start : start + length].reshape(-1)
        for start, length in zip(starts, cuts, strict=True)
    )
    router_full = router_full.reshape(width, experts)
    attn_gain = attn_gain.astype(F32)
    expert_gain_full = expert_gain_full.astype(F32)
    query_gain_full = query_gain_full.astype(F32)
    key_gain_full = key_gain_full.astype(F32)
    routes_all = lax.all_gather(routes, "shard", axis=1, tiled=True).reshape(tokens, -1)

    projections = jnp.stack(
        [
            weight.reshape(column_width, shards, column_width)
            for weight in (query_weight, key_weight, value_weight)
        ],
        axis=2,
    )
    projections = lax.all_to_all(
        projections, "shard", split_axis=1, concat_axis=0, tiled=True
    ).reshape(width, 3 * column_width)

    hidden_all = group_gather(inputs, deep, wide, 0).reshape(tokens, width)
    upstream_all = group_gather(cotangent, deep, wide, 1).reshape(tokens, width)

    wide_all = hidden_all.astype(F32)
    mixer_all = (wide_all * rms_scale(wide_all) * attn_gain).astype(BF16)
    projected = jnp.dot(mixer_all, projections, preferred_element_type=F32).reshape(
        micros, span, 3, heads, HDIM
    )
    cosine_table, sine_table = rotary(jnp.arange(span, dtype=jnp.int32).astype(F32), HDIM)
    query_proj, key_proj = projected[:, :, 0], projected[:, :, 1]
    value_low = projected[:, :, 2].astype(BF16)
    query_norm_scale = rms_scale(query_proj)
    query_unit = query_proj * query_norm_scale
    query_rot = rotate(query_unit * query_gain_full, cosine_table, sine_table).astype(BF16)
    key_norm_scale = rms_scale(key_proj)
    key_unit = key_proj * key_norm_scale
    key_rot = rotate(key_unit * key_gain_full, cosine_table, sine_table).astype(BF16)
    same_doc = segment_ids[:, :, None] == segment_ids[:, None, :]
    scores = (
        jnp.einsum("mqhd,mkhd->mhqk", query_rot, key_rot, preferred_element_type=F32) * score_scale
    )
    scores = jnp.where(same_doc[:, None], scores, MASK_FILL)
    row_peak = jnp.max(scores, axis=-1, keepdims=True)
    exponent = jnp.exp(scores - row_peak)
    probs = exponent / jnp.sum(exponent, axis=-1, keepdims=True)
    probs_low = probs.astype(BF16)
    attended = jnp.einsum("mhqk,mkhd->mqhd", probs_low, value_low, preferred_element_type=F32)
    attended = attended.astype(BF16).reshape(tokens, column_width)
    middle_parts = jnp.dot(attended, output_weight, preferred_element_type=F32).astype(BF16)
    hidden = inputs.astype(F32)
    middle = hidden + group_scatter(
        middle_parts.reshape(micros, shards, rows, width), deep, wide, 2
    )

    scale_second = rms_scale(middle)
    normed_second = middle * scale_second
    expert_input = (normed_second * expert_gain_full).astype(BF16)
    expert_all = group_gather(expert_input, deep, wide, 3).reshape(tokens, width)
    logits = jnp.dot(expert_all, router_full, preferred_element_type=F32)
    choose = (routes_all[:, :, None] == jnp.arange(experts, dtype=jnp.int32)).astype(F32)
    share = softmax_rows(jnp.sum(choose * logits[:, None, :], axis=-1))
    share_wide = jnp.sum(choose * share[:, :, None], axis=1)
    served = (jnp.arange(groups, dtype=jnp.int32) * shards + shard_place) // 2
    serves = (served[:, None] == jnp.arange(experts, dtype=jnp.int32)).astype(F32)
    share_own = jnp.pad(
        jnp.dot(share_wide, serves.T, precision=PRECISE), ((0, 0), (0, 128 - groups))
    )
    activated, gate_pre, up_pre, dots = expert_units(
        expert_all, upstream_all, share_own, gate_all, up_all, down_all
    )
    expert_grad_parts = expert_merge(gate_pre, up_pre, gate_all, up_all)
    out_parts = expert_output(activated, down_all)
    gate_terms, up_terms, down_terms = expert_weights(
        expert_all, upstream_all, activated, gate_pre, up_pre
    )
    gate_grad = lax.psum_scatter(gate_terms, "expert", scatter_dimension=0, tiled=True)
    up_grad = lax.psum_scatter(up_terms, "expert", scatter_dimension=0, tiled=True)
    down_grad = lax.psum_scatter(down_terms, "expert", scatter_dimension=0, tiled=True)
    share_grad_wide = lax.psum(
        jnp.dot(dots[:, :groups], serves, precision=PRECISE), "shard"
    )
    expert_grad = group_scatter(
        expert_grad_parts.reshape(micros, shards, rows, width), deep, wide, 4
    )
    result = middle + group_scatter(out_parts.reshape(micros, shards, rows, width), deep, wide, 5)

    share_grad = jnp.sum(choose * share_grad_wide[:, None, :], axis=-1)
    chosen_grad = share * (share_grad - jnp.sum(share * share_grad, axis=-1, keepdims=True))
    logits_grad = jnp.sum(choose * chosen_grad[:, :, None], axis=1)
    own_logits_grad = lax.dynamic_slice_in_dim(
        logits_grad.reshape(micros, span, experts), shard_place * rows, rows, 1
    )
    expert_grad = expert_grad + jnp.dot(
        own_logits_grad, router_full.astype(F32).T, precision=PRECISE
    )
    expert_gain_term = jnp.sum(expert_grad * normed_second, axis=(0, 1))
    middle_grad = cotangent.astype(F32) + norm_back(
        expert_grad * expert_gain_full, normed_second, scale_second
    )
    router_term = jnp.einsum(
        "mtd,mte->de", expert_input.astype(F32), own_logits_grad, precision=PRECISE
    )
    branch_all = group_gather(middle_grad.astype(BF16), deep, wide, 6).reshape(tokens, width)

    attended_grad = jnp.einsum("te,de->td", branch_all, output_weight, preferred_element_type=F32)
    attended_grad = attended_grad.astype(BF16).reshape(micros, span, heads, HDIM)
    output_term = jnp.einsum("td,te->de", attended, branch_all, preferred_element_type=F32)
    prob_grad = jnp.einsum("mqhd,mkhd->mhqk", attended_grad, value_low, preferred_element_type=F32)
    row_delta = jnp.sum(probs * prob_grad, axis=-1, keepdims=True)
    score_grad = (probs * (prob_grad - row_delta)).astype(BF16)
    query_rot_grad = (
        jnp.einsum("mhqk,mkhd->mqhd", score_grad, key_rot, preferred_element_type=F32) * score_scale
    )
    key_rot_grad = (
        jnp.einsum("mhqk,mqhd->mkhd", score_grad, query_rot, preferred_element_type=F32)
        * score_scale
    )
    value_grad_low = jnp.einsum(
        "mhqk,mqhd->mkhd", probs_low, attended_grad, preferred_element_type=F32
    ).astype(BF16)
    query_unit_grad = rotate(query_rot_grad, cosine_table, -sine_table)
    query_gain_term = jnp.sum(query_unit_grad * query_unit, axis=(0, 1, 2))
    query_proj_grad = norm_back(
        query_unit_grad * query_gain_full, query_unit, query_norm_scale
    ).astype(BF16)
    key_unit_grad = rotate(key_rot_grad, cosine_table, -sine_table)
    key_gain_term = jnp.sum(key_unit_grad * key_unit, axis=(0, 1, 2))
    key_proj_grad = norm_back(key_unit_grad * key_gain_full, key_unit, key_norm_scale).astype(BF16)
    projected_grad = jnp.stack([query_proj_grad, key_proj_grad, value_grad_low], axis=2).reshape(
        tokens, 3 * column_width
    )
    mixer_parts = jnp.einsum(
        "te,de->td", projected_grad, projections, preferred_element_type=F32
    ).astype(BF16)
    mixer_grad = group_scatter(mixer_parts.reshape(micros, shards, rows, width), deep, wide, 7)
    scale_first = rms_scale(hidden)
    normed_first = hidden * scale_first
    attn_gain_term = jnp.sum(mixer_grad * normed_first, axis=(0, 1))
    hidden_grad = middle_grad + norm_back(mixer_grad * attn_gain, normed_first, scale_first)

    projection_terms = jnp.einsum(
        "td,te->de", mixer_all, projected_grad, preferred_element_type=F32
    ).astype(BF16)
    projection_terms = lax.all_to_all(
        projection_terms.reshape(width, 1, 3, column_width),
        "shard",
        split_axis=0,
        concat_axis=1,
        tiled=True,
    )
    projection_terms = jnp.transpose(projection_terms, (2, 0, 1, 3)).reshape(
        3, column_width, width
    )
    projection_grads, output_grad = lax.psum(
        (projection_terms, output_term.astype(BF16)), "expert"
    )
    projection_grads = projection_grads.astype(F32)
    tail = jnp.concatenate(
        [router_term.reshape(-1), attn_gain_term, expert_gain_term, query_gain_term, key_gain_term]
    )
    tail = lax.psum(tail, ("expert", "shard"))

    def tail_part(start, length):
        return lax.dynamic_slice_in_dim(tail[start * shards :], shard_place * length, length)

    tails = [tail_part(start, length) for start, length in zip(starts, cuts, strict=True)]
    return (
        result.astype(BF16),
        hidden_grad.astype(BF16),
        projection_grads[0],
        projection_grads[1],
        projection_grads[2],
        output_grad.astype(F32),
        tails[0].reshape(column_width, experts),
        tails[1],
        tails[2],
        tails[3],
        tails[4],
        gate_grad.astype(F32),
        up_grad.astype(F32),
        down_grad.astype(F32),
    )


def solution(mesh):
    groups, shards = mesh.shape["expert"], mesh.shape["shard"]
    wide = shards // 4 if shards % 4 == 0 else 1
    in_specs = (
        P(None, ("expert", "shard"), None),
        P(None, "expert"),
        P(None, ("expert", "shard"), None),
        P(None, ("expert", "shard"), None),
        P("shard", None),
        P("shard", None),
        P("shard", None),
        P("shard", None),
        P("shard", None),
        P("shard"),
        P("shard"),
        P("shard"),
        P("shard"),
        P(("expert", "shard"), None, None),
        P(("expert", "shard"), None, None),
        P(("expert", "shard"), None, None),
    )
    out_specs = (
        P(None, ("expert", "shard"), None),
        P(None, ("expert", "shard"), None),
        P("shard", None),
        P("shard", None),
        P("shard", None),
        P("shard", None),
        P("shard", None),
        P("shard"),
        P("shard"),
        P("shard"),
        P("shard"),
        P(("expert", "shard"), None, None),
        P(("expert", "shard"), None, None),
        P(("expert", "shard"), None, None),
    )
    return jax.shard_map(
        functools.partial(per_device, groups, shards, wide),
        mesh=mesh,
        in_specs=in_specs,
        out_specs=out_specs,
        check_vma=False,
    )
```

time: 3470 us -> 1270 us (0.37)
  waiting for transfers between devices: 2470 us -> 298 us
  Pallas kernels: 0 us -> 730 us
  matrix products: 334 us -> 55.6 us
  blocking collectives: 267 us -> 23.6 us
  other arithmetic: 154 us -> 48.5 us
  local copies, waits for them, and re-layouts: 160 us -> 74 us
  starting transfers between devices: 63.5 us -> 11.2 us
    all_gather x20 -> x3, waiting for transfers between devices: 1160 us -> 0.01 us  [the longest x1 0.01 us: per_device(): gate_all = lax.all_gather(gate_weight, 'expert', axis=0, tiled=True)]
    all_to_all x8 -> x2, waiting for transfers between devices: 966 us -> 0.01 us  [the longest x1 0.01 us: per_device(): lax.all_to_all(projections, 'shard', split_axis=1, concat_axis=0, tiled=T...]
    pallas_call x0 -> x12, Pallas kernels: none -> 730 us  [the longest x4 319 us: group_gather(): pl.pallas_call(functools.partial(gather_kernel, deep, wide), out_shape=ja...]
    dot_general x60 -> x16, matrix products: 334 us -> 50.5 us  [the longest x1 7.8 us: per_device(): jnp.einsum('te,de->td', projected_grad, projections, preferred_element_ty...]
    all_gather x3 -> x1, blocking collectives: 230 us -> 23.6 us  [per_device(): lax.all_gather(routes, 'shard', axis=1, tiled=True).reshape(tokens, -1)]
    gather x8 -> x0, local copies, waits for them, and re-layouts: 69.4 us -> none  [the longest x4 36.1 us: gather_back(): return merged[target]]
    reduce_scatter x5 -> x3, waiting for transfers between devices: 264 us -> 208 us  [the longest x1 70.2 us: per_device(): lax.psum_scatter(down_terms, 'expert', scatter_dimension=0, tiled=True)]
    all_to_all x8 -> x2, starting transfers between devices: 61.8 us -> 10.2 us  [the longest x1 5.61 us: per_device(): lax.all_to_all(projections, 'shard', split_axis=1, concat_axis=0, tiled=T...]
  transfers between devices with their start and end apart: 34 -> 12, of which waited for: 31 -> 5; matrix products, arithmetic and copies ran while one was open for 13% -> 9% of each run, Pallas kernels for 0% -> 50%
where the time goes in v1:
time: 1270 us; the launch traced here: 1260 us
  Pallas kernels  730 us (57%)
  waiting for transfers between devices  298 us (23%)
  local copies, waits for them, and re-layouts  74 us (6%)
  matrix products  55.6 us (4%)
  other arithmetic  48.5 us (4%)
  blocking collectives  23.6 us (2%)
  between operations  17.8 us (1%)
    pallas_call x4, Pallas kernels, group_gather(): pl.pallas_call(functools.partial(gather_kernel, deep, wide), out_shape=ja...  319 us
    pallas_call x4, Pallas kernels, group_scatter(): pl.pallas_call(functools.partial(scatter_kernel, deep, wide), out_shape=j...  300 us
    psum x1, waiting for transfers between devices, per_device(): lax.psum((projection_terms, output_term.astype(BF16)), 'expert')  83.6 us
    reduce_scatter x1, waiting for transfers between devices, per_device(): lax.psum_scatter(down_terms, 'expert', scatter_dimension=0, tiled=True)  70.2 us
    reduce_scatter x1, waiting for transfers between devices, per_device(): lax.psum_scatter(up_terms, 'expert', scatter_dimension=0, tiled=True)  70 us
    reduce_scatter x1, waiting for transfers between devices, per_device(): lax.psum_scatter(gate_terms, 'expert', scatter_dimension=0, tiled=True)  67.4 us
    pallas_call x1, Pallas kernels, expert_units(): pl.pallas_call(functools.partial(units_kernel, 256 if tokens <= 1024 else...  37.5 us
    pallas_call x1, Pallas kernels, expert_weights(): pl.pallas_call(functools.partial(weights_kernel, 256), grid=(halves,), in...  35.5 us
  transfers between devices with their start and end apart: 12, of which 5 were waited for; matrix products, arithmetic and copies ran while one was open for 9% of the time, Pallas kernels for 50%

profile of v1, /device:TPU:11, one launch (start us, length us, event | category | flops | bytes accessed | tf_op | source)
XLA Modules:
  0.0 1259.3 jit_solution(4352199716074509495)
XLA Ops:
  29.1 5.6 all-to-all-start
  34.7 125.8 %shard_map.263 = bf16[2,8,64,2048]{3,2,1,0:T(8,128)(2,1)} custom-call(bf16[2,64,2048]{2,1,0:T(8,128)(2,1)} %own.2), custom_call_target="tpu_custom_call" | custom-call | tf_op jit(solution)/shard_map/pallas_call | solution.py:152
  160.5 69.0 %shard_map.266 = bf16[2,8,64,2048]{3,2,1,0:T(8,128)(2,1)} custom-call(bf16[2,64,2048]{2,1,0:T(8,128)(2,1)} %own.3), custom_call_target="tpu_custom_call" | custom-call | tf_op jit(solution)/shard_map/pallas_call | solution.py:152
  229.6 23.6 %all_gather.20 = s32[2,512,8]{2,0,1:T(2,128)S(1)} all-gather(s32[2,64,8]{2,0,1:T(2,128)S(1)} %copy.137), channel_id=1, replica_groups=mesh['expert'=4,'shard'=8] {'shard'}, dimensions={1}, use_global_device_ids=true | all-gather | bytes 36864 | tf_op jit(solution)/shard_map/all_gather | solution.py:488
  261.8 5.4 fusion.3
  293.9 57.2 %shard_map.264 = f32[2,64,2048]{2,1,0:T(8,128)} custom-call(bf16[2,8,64,2048]{3,2,1,0:T(8,128)(2,1)} %bitcast.149), custom_call_target="tpu_custom_call" | custom-call | tf_op jit(solution)/shard_map/pallas_call | solution.py:232
  354.2 63.2 %shard_map.265 = bf16[2,8,64,2048]{3,2,1,0:T(8,128)(2,1)} custom-call(bf16[2,64,2048]{2,1,0:T(8,128)(2,1)} %multiply_convert_fusion.1.own), custom_call_target="tpu_custom_call" | custom-call | tf_op jit(solution)/shard_map/pallas_call | solution.py:152
  422.6 37.5 %shard_map.267 = (bf16[4,1024,512]{2,1,0:T(8,128)(2,1)}, bf16[4,1024,512]{2,1,0:T(8,128)(2,1)}, bf16[4,1024,512]{2,1,0:T(8,128)(2,1)}, f32[1024,128]{1,0:T(8,128)}) custom-call(bf16[1024,2048]{1,0:T(8,128)(2,1)} %bitcast.147, bf16[1024,2048]{1,0:T(8,128)(2,1)} %bitcast.158, f32[1024,128]{1,0:T(8,128)} %pad.4.share_ref, ...), custom_call_target="tpu_custom_call" | custom-call | flops 25769803776 | bytes 25165824 | tf_op jit(solution)/shard_map/pallas_call | solution.py:303
  462.2 24.2 %shard_map.270 = bf16[1024,2048]{1,0:T(8,128)(2,1)} custom-call(bf16[4,1024,512]{2,1,0:T(8,128)(2,1)} %get-tuple-element.22.gate_pre_ref, bf16[4,1024,512]{2,1,0:T(8,128)(2,1)} %get-tuple-element.23.up_pre_ref, bf16[4,2048,512]{2,1,0:T(8,128)(2,1)} %all-gather.5.cloned.1.call-done.gate_ref, bf16[4,2048,512]{2,1,0:T(8,128)(2,1)} %all-gather.7.cloned.1.call-done.up_ref), custom_call_target="tpu_custom_call" | custom-call | flops 17179869184 | bytes 16777216 | tf_op jit(solution)/shard_map/pallas_call | solution.py:341
  486.4 53.0 %shard_map.271 = f32[2,64,2048]{2,1,0:T(8,128)} custom-call(bf16[2,8,64,2048]{3,2,1,0:T(8,128)(2,1)} %bitcast.155), custom_call_target="tpu_custom_call" | custom-call | tf_op jit(solution)/shard_map/pallas_call | solution.py:232
  546.8 60.5 %shard_map.272 = bf16[2,8,64,2048]{3,2,1,0:T(8,128)(2,1)} custom-call(bf16[2,64,2048]{2,1,0:T(8,128)(2,1)} %fusion.50.own), custom_call_target="tpu_custom_call" | custom-call | tf_op jit(solution)/shard_map/pallas_call | solution.py:152
  634.1 7.8 convolution_convert_fusion.2
  641.9 7.1 copy.151
  653.7 7.8 convolution_convert_fusion.1
  661.5 129.7 %shard_map.273 = f32[2,64,2048]{2,1,0:T(8,128)} custom-call(bf16[2,8,64,2048]{3,2,1,0:T(8,128)(2,1)} %bitcast.156), custom_call_target="tpu_custom_call" | custom-call | tf_op jit(solution)/shard_map/pallas_call | solution.py:232
  802.3 6.2 copy.152
  808.5 5.9 reshape.490
  814.4 35.5 %shard_map.274 = (bf16[4,2048,512]{2,1,0:T(8,128)(2,1)}, bf16[4,2048,512]{2,1,0:T(8,128)(2,1)}, bf16[4,512,2048]{2,1,0:T(8,128)(2,1)}) custom-call(bf16[1024,2048]{1,0:T(8,128)(2,1)} %bitcast.148, bf16[1024,2048]{1,0:T(8,128)(2,1)} %bitcast.159, bf16[4,1024,512]{2,1,0:T(8,128)(2,1)} %get-tuple-element.21.hidden_ref, ...), custom_call_target="tpu_custom_call" | custom-call | flops 25769803776 | bytes 25165824 | tf_op jit(solution)/shard_map/pallas_call | solution.py:419
  851.3 14.0 %shard_map.268 = bf16[1024,2048]{1,0:T(8,128)(2,1)} custom-call(bf16[4,1024,512]{2,1,0:T(8,128)(2,1)} %get-tuple-element.21.hidden_ref, bf16[4,512,2048]{2,1,0:T(8,128)(2,1)} %all-gather.9.cloned.1.call-done.down_ref), custom_call_target="tpu_custom_call" | custom-call | flops 8589934592 | bytes 8388608 | tf_op jit(solution)/shard_map/pallas_call | solution.py:372
  865.3 60.5 %shard_map.269 = f32[2,64,2048]{2,1,0:T(8,128)} custom-call(bf16[2,8,64,2048]{3,2,1,0:T(8,128)(2,1)} %bitcast.157), custom_call_target="tpu_custom_call" | custom-call | tf_op jit(solution)/shard_map/pallas_call | solution.py:232
  940.2 83.6 %all-reduce.14.cloned.1.call-done = (bf16[3,256,2048]{2,1,0:T(8,128)(2,1)}, bf16[256,2048]{1,0:T(8,128)(2,1)}) async-done(((bf16[3,256,2048]{2,1,0:T(8,128)(2,1)}, bf16[256,2048]{1,0:T(8,128)(2,1)}), (bf16[3,256,2048]{2,1,0:T(8,128)(2,1)}, bf16[256,2048]{1,0:T(8,128)(2,1)})) %all-reduce.14.cloned.1.call-update) | async-done | bytes 4194320 | tf_op jit(solution)/shard_map/psum | solution.py:634
  1031.0 67.4 %reduce-scatter.4.cloned.1.call-done = bf16[1,2048,512]{2,1,0:T(8,128)(2,1)} async-done(((bf16[4,2048,512]{2,1,0:T(8,128)(2,1)}), bf16[1,2048,512]{2,1,0:T(8,128)(2,1)}) %reduce-scatter.4.cloned.1.call-update) | async-done | bytes 2097168 | tf_op jit(solution)/shard_map/reduce_scatter | solution.py:556
  1102.6 70.0 %reduce-scatter.6.cloned.1.call-done = bf16[1,2048,512]{2,1,0:T(8,128)(2,1)} async-done(((bf16[4,2048,512]{2,1,0:T(8,128)(2,1)}), bf16[1,2048,512]{2,1,0:T(8,128)(2,1)}) %reduce-scatter.6.cloned.1.call-update) | async-done | bytes 2097168 | tf_op jit(solution)/shard_map/reduce_scatter | solution.py:557
  1176.8 70.2 %reduce-scatter.8.cloned.1.call-done = bf16[1,512,2048]{2,1,0:T(8,128)(2,1)} async-done(((bf16[4,512,2048]{2,1,0:T(8,128)(2,1)}), bf16[1,512,2048]{2,1,0:T(8,128)(2,1)}) %reduce-scatter.8.cloned.1.call-update) | async-done | bytes 2097168 | tf_op jit(solution)/shard_map/reduce_scatter | solution.py:558
  (229 shorter events, 150.8 us)
Async XLA Ops:
  8.0 282.6 %copy-start = (bf16[256,2048]{1,0:T(8,128)(2,1)S(1)}, bf16[256,2048]{1,0:T(8,128)(2,1)}, u32[]{:S(2)}) copy-start(bf16[256,2048]{1,0:T(8,128)(2,1)} %param.23) | copy-start | bytes 3145732
  8.0 252.0 %all-reduce.12.cloned.1.call-start = ((), (), s32[]{:S(2)}) async-start(), calls=%async_computation.13 | async-start | bytes 151552
  14.9 407.7 %all-gather.5.cloned.1.call-start = ((), (), s32[]{:S(2)}) async-start(), calls=%async_computation.5 | async-start | bytes 10485760 | tf_op jit(solution)/shard_map/all_gather | solution.py:469
  15.4 407.2 %all-gather.7.cloned.1.call-start = ((), (), s32[]{:S(2)}) async-start(), calls=%async_computation.6 | async-start | bytes 10485760 | tf_op jit(solution)/shard_map/all_gather | solution.py:470
  16.0 406.6 %all-gather.9.cloned.1.call-start = ((), (), s32[]{:S(2)}) async-start(), calls=%async_computation.7 | async-start | bytes 10485760 | tf_op jit(solution)/shard_map/all_gather | solution.py:471
  29.1 238.1 %all-to-all-start = ((bf16[256,8,3,256]{3,0,2,1:T(8,128)(2,1)}), bf16[256,8,3,256]{3,0,2,1:T(8,128)(2,1)}, u32[]{:S(2)}, u32[]{:S(2)}) async-start(bf16[256,8,3,256]{3,0,2,1:T(8,128)(2,1)} %copy.131), calls=%async_computation | async-start | bytes 6291456 | tf_op jit(solution)/shard_map/all_to_all | solution.py:497
  34.7 194.8 %copy-start.40 = (s32[2,64,8]{1,2,0:T(8,128)S(1)}, s32[2,64,8]{1,2,0:T(8,128)}, u32[]{:S(2)}) copy-start(s32[2,64,8]{1,2,0:T(8,128)} %param.18) | copy-start | bytes 12292
  34.7 504.7 %all-reduce.8.cloned.1.call-start = ((), (), s32[]{:S(2)}) async-start(), calls=%async_computation.8 | async-start | bytes 131072 | tf_op jit(solution)/shard_map/psum | solution.py:559
  160.5 98.4 %copy-start.35 = (s32[2,512]{1,0:T(2,128)S(1)}, s32[2,512]{1,0:T(2,128)}, u32[]{:S(2)}) copy-start(s32[2,512]{1,0:T(2,128)} %param.17) | copy-start | bytes 12292
  261.8 155.7 %copy-start.9 = (bf16[2048,16]{1,0:T(8,128)(2,1)}, bf16[2048,16]{1,0:T(8,128)(2,1)S(1)}, u32[]{:S(2)}) copy-start(bf16[2048,16]{1,0:T(8,128)(2,1)S(1)} %reshape_reshape.3) | copy-start | bytes 196612
  649.0 153.3 %all-to-all-start.1 = ((bf16[2048,1,3,256]{3,2,1,0:T(4,128)(2,1)}), bf16[2048,1,3,256]{3,2,1,0:T(4,128)(2,1)}, u32[]{:S(2)}, u32[]{:S(2)}) async-start(bf16[2048,1,3,256]{3,2,1,0:T(4,128)(2,1)} %copy.151), calls=%async_computation.1 | async-start | bytes 8388608 | tf_op jit(solution)/shard_map/all_to_all | solution.py:624
  653.6 279.7 %all-reduce.10.cloned.1.call-start = ((), (), s32[]{:S(2)}) async-start(), calls=%async_computation.9 | async-start | bytes 303104 | tf_op jit(solution)/shard_map/psum | solution.py:641
  661.5 129.7 %copy-start.8 = (bf16[2,64,2048]{2,1,0:T(8,128)(2,1)S(1)}, bf16[2,64,2048]{2,1,0:T(8,128)(2,1)}, u32[]{:S(2)}) copy-start(bf16[2,64,2048]{2,1,0:T(8,128)(2,1)} %multiply_convert_fusion.1.own) | copy-start | bytes 1572868
  661.5 129.7 %copy-start.27 = (f32[2,64,16]{1,0,2:T(2,128)S(1)}, f32[2,64,16]{1,0,2:T(2,128)}, u32[]{:S(2)}) copy-start(f32[2,64,16]{1,0,2:T(2,128)} %copy-done.26) | copy-start | bytes 24580
  661.5 133.5 %copy-start.6 = (bf16[2,64,2048]{2,1,0:T(8,128)(2,1)S(1)}, bf16[2,64,2048]{2,1,0:T(8,128)(2,1)}, u32[]{:S(2)}) copy-start(bf16[2,64,2048]{2,1,0:T(8,128)(2,1)} %own.2) | copy-start | bytes 1572868
  661.5 133.5 %copy-start.31 = (f32[1,2,8,128]{3,1,2,0:T(2,128)S(1)}, f32[1,2,8,128]{3,1,2,0:T(2,128)}, u32[]{:S(2)}) copy-start(f32[1,2,8,128]{3,1,2,0:T(2,128)} %copy-done.30) | copy-start | bytes 24580
  661.5 135.1 %copy-start.32 = (f32[2048]{0:T(1024)S(1)}, f32[2048]{0:T(1024)}, u32[]{:S(2)}) copy-start(f32[2048]{0:T(1024)} %get-tuple-element.92) | copy-start | bytes 24580
  797.4 226.4 %all-reduce.14.cloned.1.call-start = ((), (), s32[]{:S(2)}) async-start(), calls=%async_computation.14 | async-start | bytes 8388608 | tf_op jit(solution)/shard_map/psum | solution.py:634
  814.3 284.0 %reduce-scatter.4.cloned.1.call-start = ((), (), s32[]{:S(2)}) async-start(), calls=%async_computation.10 | async-start | bytes 10485760 | tf_op jit(solution)/shard_map/reduce_scatter | solution.py:556
  849.9 322.6 %reduce-scatter.6.cloned.1.call-start = ((), (), s32[]{:S(2)}) async-start(), calls=%async_computation.11 | async-start | bytes 10485760 | tf_op jit(solution)/shard_map/reduce_scatter | solution.py:557
  850.5 396.5 %reduce-scatter.8.cloned.1.call-start = ((), (), s32[]{:S(2)}) async-start(), calls=%async_computation.12 | async-start | bytes 10485760 | tf_op jit(solution)/shard_map/reduce_scatter | solution.py:558
  865.3 60.6 %copy-start.34 = (f32[2,64]{1,0:T(2,128)S(1)}, f32[2,64]{1,0:T(2,128)}, u32[]{:S(2)}) copy-start(f32[2,64]{1,0:T(2,128)} %copy-done.33) | copy-start | bytes 1540
  865.3 60.6 %copy-start.37 = (f32[2,64]{1,0:T(2,128)S(1)}, f32[2,64]{1,0:T(2,128)}, u32[]{:S(2)}) copy-start(f32[2,64]{1,0:T(2,128)} %copy-done.36) | copy-start | bytes 1540
  1172.5 78.7 %copy-start.1 = (bf16[256,2048]{1,0:T(8,128)(2,1)S(1)}, bf16[256,2048]{1,0:T(8,128)(2,1)}, u32[]{:S(2)}) copy-start(bf16[256,2048]{1,0:T(8,128)(2,1)} %param.23) | copy-start | bytes 3145732
  (35 other events, 292.4 us)
Sparse Core Ops, SparseCore 0:
  15.0 111.9 all-reduce.11
  462.3 71.2 all-reduce.7
  797.5 135.8 all-reduce.9
  936.8 86.9 all-reduce.13
  1026.4 71.9 reduce-scatter.3
  1100.8 71.6 reduce-scatter.5
  1175.3 71.7 reduce-scatter.7
Sparse Core Ops, SparseCore 1:
  16.9 59.6 all-gather.4
  78.0 58.1 all-gather.6
  137.6 58.1 all-gather.8

commit v2 on v1

v2 whole, which is shorter than its diff:
```python
import functools
import math

import jax
import jax.numpy as jnp
from jax import lax
from jax.experimental import pallas as pl
from jax.experimental.pallas import tpu as pltpu
from jax.sharding import PartitionSpec as P

HDIM = 128
EPSILON = 1e-05
ROPE_BASE = 10000.0
MASK_FILL = -1e30
PRECISE = lax.Precision.HIGHEST
MESH = pl.DeviceIdType.MESH
F32 = jnp.float32
BF16 = jnp.bfloat16
NN = (((1,), (0,)), ((), ()))
NT = (((1,), (1,)), ((), ()))
TN = (((0,), (0,)), ((), ()))
VMEM_LIMIT = 60 << 20
LINK_COST = pl.CostEstimate(flops=60 * 10**9, bytes_accessed=8 << 20, transcendentals=0)


def dot(left, right, dims):
    return lax.dot_general(left, right, dims, preferred_element_type=F32)


def rms_scale(values):
    return lax.rsqrt(jnp.mean(values * values, axis=-1, keepdims=True) + EPSILON)


def norm_back(normed_grad, normed, inv_scale):
    return inv_scale * (
        normed_grad - normed * jnp.mean(normed_grad * normed, axis=-1, keepdims=True)
    )


def rotary(span):
    steps = jnp.arange(HDIM // 2, dtype=jnp.int32).astype(F32)
    freqs = jnp.power(ROPE_BASE, -2.0 * steps / HDIM)
    theta = jnp.arange(span, dtype=jnp.int32).astype(F32)[:, None] * freqs[None, :]
    cosine, sine = jnp.cos(theta), jnp.sin(theta)
    return (
        jnp.concatenate([cosine, cosine], axis=1),
        jnp.concatenate([-sine, sine], axis=1),
    )


def softmax_rows(scores):
    row_peak = jnp.max(scores, axis=-1, keepdims=True)
    exponent = jnp.exp(scores - row_peak)
    return exponent / jnp.sum(exponent, axis=-1, keepdims=True)


class Place:
    def __init__(self, groups, deep, wide):
        self.deep, self.wide = deep, wide
        self.shards, self.groups, self.layers = deep * wide, groups, groups // 2
        group, me = lax.axis_index("expert"), lax.axis_index("shard")
        self.group, self.me = group, me
        self.layer, self.core = group // 2, lax.rem(group, 2)
        self.row, self.column = me // wide, lax.rem(me, wide)

    def peer(self, layer_step=0, core_step=0, row_step=0, column_step=0):
        group, me = self.group, self.me
        if layer_step or core_step:
            group = lax.rem(self.layer + layer_step, self.layers) * 2 + (
                1 - self.core if core_step else self.core
            )
        if row_step or column_step:
            me = lax.rem(self.row + row_step, self.deep) * self.wide + lax.rem(
                self.column + column_step, self.wide
            )
        return group, me

    def grid_place(self, row_step, column_step):
        return self.peer(0, 0, row_step, column_step)[1]

    def back(self, layer_step=0, core_step=0, row_step=0, column_step=0):
        return self.peer(
            (self.layers - layer_step) % self.layers,
            core_step,
            (self.deep - row_step) % self.deep,
            (self.wide - column_step) % self.wide,
        )


def send_to(peer, source, target, send_sem, recv_sem):
    return pltpu.make_async_remote_copy(
        src_ref=source,
        dst_ref=target,
        send_sem=send_sem,
        recv_sem=recv_sem,
        device_id=peer,
        device_id_type=MESH,
    )


def dma(*shape):
    return pltpu.SemaphoreType.DMA(tuple(max(1, size) for size in shape))


ANYWHERE = pl.BlockSpec(memory_space=pl.ANY)
RESIDENT = pl.BlockSpec(memory_space=pltpu.VMEM)


def grid_steps(deep, wide):
    steps = {(0, 0, row, 0) for row in range(1, deep)}
    return steps | {(0, 0, 0, column) for column in range(1, wide)}


def shard_steps(deep, wide):
    return {
        (0, 0, row, column) for row in range(deep) for column in range(wide) if row or column
    }


def expert_steps(layers):
    return {(step, 0, 0, 0) for step in range(1, layers)} | {(0, 1, 0, 0)}


def fuse(parts, layout, collective_id, name):
    groups, deep, wide = layout
    operands = [operand for part in parts for operand in part.operands]
    in_specs = [spec for part in parts for spec in part.in_specs]
    out_shape = [out for part in parts for out in part.outs]
    out_specs = [spec for part in parts for spec in part.out_specs]
    scratch = [buffer for part in parts for buffer in part.scratch]
    steps = sorted(set().union(*(part.steps for part in parts)))

    def kernel(*refs):
        place = Place(groups, deep, wide)
        barrier = pltpu.get_barrier_semaphore()
        for step in steps:
            pl.semaphore_signal(
                barrier, inc=1, device_id=place.peer(*step), device_id_type=MESH
            )
        pl.semaphore_wait(barrier, len(steps))
        ins = list(refs[: len(operands)])
        outs = list(refs[len(operands) : len(operands) + len(out_shape)])
        buffers = list(refs[len(operands) + len(out_shape) :])
        running = []
        for part in parts:
            part_ins = [ins.pop(0) for _ in part.operands]
            part_outs = [outs.pop(0) for _ in part.outs]
            part_buffers = [buffers.pop(0) for _ in part.scratch]
            running.append(part.run(place, *part_ins, *part_outs, *part_buffers))
        while running:
            for part in list(running):
                try:
                    next(part)
                except StopIteration:
                    running.remove(part)

    results = pl.pallas_call(
        kernel,
        out_shape=out_shape,
        in_specs=in_specs,
        out_specs=out_specs,
        scratch_shapes=scratch,
        compiler_params=pltpu.CompilerParams(
            collective_id=collective_id, has_side_effects=True, vmem_limit_bytes=VMEM_LIMIT
        ),
        cost_estimate=LINK_COST,
        name=name,
    )(*operands)
    results = list(results)
    return [[results.pop(0) for _ in part.outs] for part in parts]


class Chain:
    def __init__(self, *parts):
        self.parts = parts
        for name in ("operands", "in_specs", "outs", "out_specs", "scratch"):
            setattr(self, name, [item for part in parts for item in getattr(part, name)])
        self.steps = set().union(*(part.steps for part in parts))

    def run(self, place, *refs):
        refs = list(refs)
        taken = [[] for _ in self.parts]
        for name in ("operands", "outs", "scratch"):
            for part, own in zip(self.parts, taken, strict=True):
                own.extend(refs.pop(0) for _ in getattr(part, name))
        for part, own in zip(self.parts, taken, strict=True):
            yield from part.run(place, *own)


class Gather:
    def __init__(self, own, layout):
        _, deep, wide = layout
        pieces, rows, width = own.shape
        self.operands, self.in_specs = [own], [ANYWHERE]
        self.outs = [jax.ShapeDtypeStruct((pieces, deep * wide, rows, width), own.dtype)]
        self.out_specs = [ANYWHERE]
        self.scratch = [
            dma(pieces, deep - 1),
            dma(pieces, deep - 1),
            dma(pieces, deep, wide - 1),
            dma(pieces, deep, wide - 1),
            dma(1),
        ]
        self.steps = grid_steps(deep, wide)

    def run(self, place, own, whole, row_send, row_recv, col_send, col_recv, local):
        pieces, deep, wide = own.shape[0], place.deep, place.wide
        here = pltpu.make_async_copy(own, whole.at[:, place.me], local.at[0])
        here.start()
        sends = []

        def along_column(piece, step):
            return send_to(
                place.peer(0, 0, step, 0),
                own.at[piece],
                whole.at[piece, place.me],
                row_send.at[piece, step - 1],
                row_recv.at[piece, step - 1],
            )

        def along_row(piece, turn, step, block, source):
            return send_to(
                place.peer(0, 0, 0, step),
                block,
                whole.at[piece, source],
                col_send.at[piece, turn, step - 1],
                col_recv.at[piece, turn, step - 1],
            )

        def forward(piece, turn, block, source):
            for step in range(1, wide):
                sends.append(along_row(piece, turn, step, block, source))
                sends[-1].start()

        for piece in range(pieces):
            for step in range(1, deep):
                sends.append(along_column(piece, step))
                sends[-1].start()
            forward(piece, 0, own.at[piece], place.me)
        yield
        for piece in range(pieces):
            for step in range(1, deep):
                source = place.grid_place(deep - step, 0)
                along_column(piece, step).wait_recv()
                forward(piece, step, whole.at[piece, source], source)
                yield
        for piece in range(pieces):
            for turn in range(deep):
                for step in range(1, wide):
                    source = place.grid_place(deep - turn, wide - step)
                    along_row(piece, turn, step, own.at[piece], source).wait_recv()
                yield
        for copy in sends:
            copy.wait_send()
        here.wait()


class Scatter:
    def __init__(self, parts, layout):
        _, deep, wide = layout
        pieces, _, rows, width = parts.shape
        self.operands, self.in_specs = [parts], [RESIDENT]
        self.outs = [jax.ShapeDtypeStruct((pieces, rows, width), F32)]
        self.out_specs = [RESIDENT]
        self.scratch = [
            pltpu.VMEM((pieces, deep, max(1, wide - 1), rows, width), BF16),
            pltpu.VMEM((pieces, deep - 1, rows, width), BF16),
            pltpu.VMEM((pieces, deep - 1, rows, width), BF16),
            dma(pieces, deep, wide - 1),
            dma(pieces, deep, wide - 1),
            dma(pieces, deep - 1),
            dma(pieces, deep - 1),
        ]
        self.steps = grid_steps(deep, wide)

    def run(
        self, place, parts, total, landed, merged, summed, col_send, col_recv, row_send, row_recv
    ):
        pieces, deep, wide = parts.shape[0], place.deep, place.wide
        sends = []

        def along_row(piece, turn, step):
            return send_to(
                place.peer(0, 0, 0, step),
                parts.at[piece, place.grid_place(turn + 1, step)],
                landed.at[piece, turn, step - 1],
                col_send.at[piece, turn, step - 1],
                col_recv.at[piece, turn, step - 1],
            )

        def along_column(piece, turn):
            return send_to(
                place.peer(0, 0, turn + 1, 0),
                merged.at[piece, turn],
                summed.at[piece, turn],
                row_send.at[piece, turn],
                row_recv.at[piece, turn],
            )

        for piece in range(pieces):
            for turn in range(deep):
                for step in range(1, wide):
                    sends.append(along_row(piece, turn, step))
                    sends[-1].start()
        yield
        for piece in range(pieces):
            for turn in range(deep):
                value = parts[piece, place.grid_place((turn + 1) % deep, 0)].astype(F32)
                for step in range(1, wide):
                    along_row(piece, turn, step).wait_recv()
                    value = value + landed[piece, turn, step - 1].astype(F32)
                if turn < deep - 1:
                    merged[piece, turn] = value.astype(BF16)
                    sends.append(along_column(piece, turn))
                    sends[-1].start()
                else:
                    total[piece] = value
                yield
        for piece in range(pieces):
            value = total[piece]
            for turn in range(deep - 1):
                along_column(piece, turn).wait_recv()
                value = value + summed[piece, turn].astype(F32)
            total[piece] = value
            yield
        for copy in sends:
            copy.wait_send()


class ExpertScatter:
    def __init__(self, terms, layout, chunks=2):
        groups = layout[0]
        layers = groups // 2
        _, rows, width = terms.shape
        part = rows // chunks
        self.operands, self.in_specs = [terms], [ANYWHERE]
        self.outs = [jax.ShapeDtypeStruct((rows, width), BF16)]
        self.out_specs = [RESIDENT]
        self.scratch = [
            pltpu.VMEM((chunks, layers, part, width), BF16),
            pltpu.VMEM((chunks, layers, part, width), BF16),
            pltpu.VMEM((chunks, max(1, layers - 1), part, width), BF16),
            dma(chunks, layers),
            dma(chunks, layers),
            dma(chunks, layers),
            dma(chunks, layers - 1),
            dma(chunks, layers - 1),
        ]
        self.steps = expert_steps(layers)

    def run(
        self,
        place,
        terms,
        total,
        mine,
        landed,
        summed,
        local,
        core_send,
        core_recv,
        layer_send,
        layer_recv,
    ):
        chunks, layers, part, _ = mine.shape
        span = min(part, 128)
        sends = []

        def entry(turn, core):
            return lax.rem(place.layer + turn, layers) * 2 + core

        def block(chunk, turn, core):
            return terms.at[entry(turn, core), pl.ds(chunk * part, part)]

        def load(chunk, turn):
            return pltpu.make_async_copy(
                block(chunk, turn, place.core), mine.at[chunk, turn], local.at[chunk, turn]
            )

        def across(chunk, turn):
            return send_to(
                place.peer(0, 1, 0, 0),
                block(chunk, turn, 1 - place.core),
                landed.at[chunk, turn],
                core_send.at[chunk, turn],
                core_recv.at[chunk, turn],
            )

        def along(chunk, turn):
            return send_to(
                place.peer(turn, 0, 0, 0),
                mine.at[chunk, turn],
                summed.at[chunk, turn - 1],
                layer_send.at[chunk, turn - 1],
                layer_recv.at[chunk, turn - 1],
            )

        order = [*range(1, layers), 0]
        for chunk in range(chunks):
            for turn in order:
                load(chunk, turn).start()
                sends.append(across(chunk, turn))
                sends[-1].start()
        yield
        for chunk in range(chunks):
            for turn in order[:-1]:
                load(chunk, turn).wait()
                across(chunk, turn).wait_recv()

                def merge(step, carry, chunk=chunk, turn=turn):
                    rows = pl.ds(pl.multiple_of(step * span, span), span)
                    value = mine[chunk, turn, rows].astype(F32)
                    value = value + landed[chunk, turn, rows].astype(F32)
                    mine[chunk, turn, rows] = value.astype(BF16)
                    return carry

                lax.fori_loop(0, part // span, merge, 0)
                sends.append(along(chunk, turn))
                sends[-1].start()
                yield
        for chunk in range(chunks):
            load(chunk, 0).wait()
            across(chunk, 0).wait_recv()
            for turn in order[:-1]:
                along(chunk, turn).wait_recv()

            def finish(step, carry, chunk=chunk):
                rows = pl.ds(pl.multiple_of(step * span, span), span)
                here = pl.ds(pl.multiple_of(chunk * part + step * span, span), span)
                value = mine[chunk, 0, rows].astype(F32) + landed[chunk, 0, rows].astype(F32)
                for turn in order[:-1]:
                    value = value + summed[chunk, turn - 1, rows].astype(F32)
                total[here] = value.astype(BF16)
                return carry

            lax.fori_loop(0, part // span, finish, 0)
            yield
        for copy in sends:
            copy.wait_send()


class ExpertWeights:
    SPAN = 256

    def __init__(self, rows, upstream, hidden, gate_pre, up_pre, down_all, layout):
        tokens, width = rows.shape
        halves, _, units = hidden.shape
        self.terms = jax.ShapeDtypeStruct((halves, width, units), BF16)
        self.inner = ExpertScatter(self.terms, layout)
        self.operands = [rows, upstream, hidden, gate_pre, up_pre, down_all]
        self.in_specs = [RESIDENT] * 5 + [ANYWHERE]
        self.outs = [
            self.terms,
            self.terms,
            jax.ShapeDtypeStruct((halves, units, width), BF16),
            jax.ShapeDtypeStruct((tokens, width), BF16),
            *self.inner.outs,
        ]
        self.out_specs = [ANYWHERE] * 3 + [RESIDENT] * 2
        self.scratch = [
            pltpu.VMEM((2, width, units), BF16),
            pltpu.VMEM((units, width), BF16),
            pltpu.VMEM((2, halves, units, self.SPAN), BF16),
            dma(2),
            dma(1),
            dma(2),
            *self.inner.scratch,
        ]
        self.steps = self.inner.steps

    def run(
        self,
        place,
        rows,
        upstream,
        hidden,
        gate_pre,
        up_pre,
        down_all,
        gate_terms,
        up_terms,
        down_terms,
        out,
        gate_total,
        stage,
        stage_down,
        tiles,
        stage_sem,
        stage_down_sem,
        tile_sem,
        *inner_scratch,
    ):
        halves, _, units = hidden.shape
        width = rows.shape[1]
        span = self.SPAN
        state = {"slot": 0, "busy": [None, None], "down": None}

        def columns(grads, target):
            for half in range(halves):
                slot = state["slot"]
                if state["busy"][slot] is not None:
                    state["busy"][slot].wait()
                for step in range(units // span):
                    here = pl.ds(step * span, span)
                    stage[slot, :, here] = dot(rows[...], grads[half, :, here], TN).astype(BF16)
                    if step < units // span - 1:
                        yield
                copy = pltpu.make_async_copy(stage.at[slot], target.at[half], stage_sem.at[slot])
                copy.start()
                state["busy"][slot] = copy
                state["slot"] = 1 - slot
                yield

        def drain():
            for slot in (0, 1):
                if state["busy"][slot] is not None:
                    state["busy"][slot].wait()
                    state["busy"][slot] = None

        def downs():
            copy = None
            for half in range(halves):
                if copy is not None:
                    copy.wait()
                for step in range(units // span):
                    here = pl.ds(step * span, span)
                    stage_down[here, :] = dot(hidden[half, :, here], upstream[...], TN).astype(
                        BF16
                    )
                    if step < units // span - 1:
                        yield
                copy = pltpu.make_async_copy(
                    stage_down, down_terms.at[half], stage_down_sem.at[0]
                )
                copy.start()
                yield
            copy.wait()

        def tile(step):
            return pltpu.make_async_copy(
                down_all.at[:, :, pl.ds(step * span, span)],
                tiles.at[step % 2],
                tile_sem.at[step % 2],
            )

        def outputs():
            for step in range(width // span):
                if step + 1 < width // span:
                    tile(step + 1).start()
                tile(step).wait()
                value = dot(hidden[0], tiles[step % 2, 0], NN)
                for half in range(1, halves):
                    value = value + dot(hidden[half], tiles[step % 2, half], NN)
                out[:, pl.ds(step * span, span)] = value.astype(BF16)
                yield

        def rest():
            yield from columns(up_pre, up_terms)
            yield from downs()
            yield from outputs()
            drain()

        tile(0).start()
        for index, _ in enumerate(columns(gate_pre, gate_terms)):
            if index % 4 == 3:
                yield
        drain()
        inner = self.inner.run(place, gate_terms, gate_total, *inner_scratch)
        next(inner)
        others = rest()
        waiting, working = True, True
        while waiting or working:
            for _ in range(4):
                working = working and next(others, "end") != "end"
            if waiting:
                waiting = next(inner, "end") != "end"
            yield


class Columns:
    def __init__(self, weights, small, layout):
        groups, deep, wide = layout
        shards = deep * wide
        depth = weights[0].shape[0]
        self.operands, self.in_specs = [*weights, small], [ANYWHERE] * 4
        self.outs = [
            jax.ShapeDtypeStruct((shards, groups, depth // groups, 3 * depth), BF16),
            jax.ShapeDtypeStruct((shards,) + small.shape, BF16),
        ]
        self.out_specs = [ANYWHERE] * 2
        self.scratch = [
            dma(3, shards - 1),
            dma(3, shards - 1),
            dma(shards - 1),
            dma(shards - 1),
            dma(groups // 2 - 1),
            dma(groups // 2 - 1),
            dma(groups // 2),
            dma(groups // 2),
            dma(4),
        ]
        self.steps = shard_steps(deep, wide) | expert_steps(groups // 2)

    def run(
        self,
        place,
        query_weight,
        key_weight,
        value_weight,
        small,
        projections,
        small_all,
        weight_send,
        weight_recv,
        small_send,
        small_recv,
        layer_send,
        layer_recv,
        core_send,
        core_recv,
        local,
    ):
        weights = (query_weight, key_weight, value_weight)
        layers, group, me = place.layers, place.group, place.me
        part = projections.shape[2]
        depth = query_weight.shape[0]
        steps = sorted(shard_steps(place.deep, place.wide))
        sends = []

        def block(which, target):
            return weights[which].at[
                pl.ds(pl.multiple_of(group * part, part), part),
                pl.ds(pl.multiple_of(target * depth, depth), depth),
            ]

        def slot(which, source):
            return projections.at[source, group, :, pl.ds(which * depth, depth)]

        def weight_copy(which, index):
            return send_to(
                place.peer(*steps[index]),
                block(which, place.peer(*steps[index])[1]),
                slot(which, me),
                weight_send.at[which, index],
                weight_recv.at[which, index],
            )

        def small_copy(index):
            return send_to(
                place.peer(*steps[index]),
                small,
                small_all.at[me],
                small_send.at[index],
                small_recv.at[index],
            )

        def slab_copy(peer, layer, core, send_sem, recv_sem):
            slab = projections.at[:, layer * 2 + core]
            return send_to(peer, slab, slab, send_sem, recv_sem)

        def layer_copy(step, layer):
            return slab_copy(
                place.peer(step, 0, 0, 0),
                layer,
                place.core,
                layer_send.at[step - 1],
                layer_recv.at[step - 1],
            )

        def core_copy(step, layer, core):
            return slab_copy(
                place.peer(0, 1, 0, 0), layer, core, core_send.at[step], core_recv.at[step]
            )

        here = [
            pltpu.make_async_copy(block(which, me), slot(which, me), local.at[which])
            for which in range(3)
        ]
        here.append(pltpu.make_async_copy(small, small_all.at[me], local.at[3]))
        for copy in here:
            copy.start()
        for index in range(len(steps)):
            for which in range(3):
                sends.append(weight_copy(which, index))
                sends[-1].start()
            sends.append(small_copy(index))
            sends[-1].start()
        yield
        for copy in here:
            copy.wait()
        for index in range(len(steps)):
            for which in range(3):
                weight_copy(which, index).wait_recv()
        for step in range(1, layers):
            sends.append(layer_copy(step, place.layer))
            sends[-1].start()
        sends.append(core_copy(0, place.layer, place.core))
        sends[-1].start()
        yield
        for step in range(1, layers):
            layer = lax.rem(place.layer + layers - step, layers)
            layer_copy(step, layer).wait_recv()
            sends.append(core_copy(step, layer, place.core))
            sends[-1].start()
            yield
        for step in range(layers):
            layer = lax.rem(place.layer + layers - step, layers)
            core_copy(step, layer, 1 - place.core).wait_recv()
            yield
        for index in range(len(steps)):
            small_copy(index).wait_recv()
        for copy in sends:
            copy.wait_send()


class Rows:
    def __init__(self, terms, row_terms, tail, layout):
        groups, deep, wide = layout
        layers = groups // 2
        shards, _, part, width = terms.shape
        depth = row_terms.shape[2]
        self.operands = [terms, row_terms, tail]
        self.in_specs = [RESIDENT] * 3
        self.outs = [
            jax.ShapeDtypeStruct((groups, part, depth), BF16),
            jax.ShapeDtypeStruct(tail.shape[1:], F32),
            *[jax.ShapeDtypeStruct((groups, part, depth), BF16)] * 3,
        ]
        self.out_specs = [RESIDENT] * 5
        others = max(1, layers - 1)
        self.scratch = [
            pltpu.VMEM((groups, shards, part, width), BF16),
            pltpu.VMEM((layers, shards, part, width), BF16),
            pltpu.VMEM((others, shards, part, width), BF16),
            pltpu.VMEM((others, shards, part, width), BF16),
            pltpu.VMEM((shards, part, width), BF16),
            pltpu.VMEM((layers, part, depth), BF16),
            pltpu.VMEM((others, part, depth), BF16),
            pltpu.VMEM((others, part, depth), BF16),
            pltpu.VMEM(tail.shape, F32),
            pltpu.VMEM((groups,) + tail.shape[1:], F32),
            dma(2, layers),
            dma(2, layers),
            dma(2, others),
            dma(2, others),
            dma(shards - 1),
            dma(shards - 1),
            dma(2, others),
            dma(2, others),
            dma(2, layers),
            dma(2, layers),
            dma(shards - 1),
            dma(shards - 1),
            dma(groups - 1),
            dma(groups - 1),
        ]
        self.steps = shard_steps(deep, wide) | expert_steps(layers)
        self.steps |= {(layer, core, 0, 0) for layer in range(layers) for core in (0, 1)}
        self.steps -= {(0, 0, 0, 0)}

    def run(
        self,
        place,
        terms,
        row_terms,
        tail,
        whole_rows,
        tail_out,
        query_out,
        key_out,
        value_out,
        whole,
        landed,
        merged,
        summed,
        ready,
        landed_rows,
        merged_rows,
        summed_rows,
        tails,
        tail_sums,
        core_send,
        core_recv,
        layer_send,
        layer_recv,
        swap_send,
        swap_recv,
        out_send,
        out_recv,
        over_send,
        over_recv,
        tail_send,
        tail_recv,
        sum_send,
        sum_recv,
    ):
        layers, group, me, core = place.layers, place.group, place.me, place.core
        shards = place.shards
        steps = sorted(shard_steps(place.deep, place.wide))
        group_steps = [
            (layer, flip, 0, 0) for layer in range(layers) for flip in (0, 1) if layer or flip
        ]
        sends = []

        def start(copy):
            copy.start()
            sends.append(copy)

        def layer_at(turn):
            return lax.rem(place.layer + turn, layers)

        def tail_copy(index):
            peer = place.peer(*steps[index])
            return send_to(
                peer, tail.at[peer[1]], tails.at[me], tail_send.at[index], tail_recv.at[index]
            )

        def sum_copy(index):
            return send_to(
                place.peer(*group_steps[index]),
                tail_sums.at[group],
                tail_sums.at[group],
                sum_send.at[index],
                sum_recv.at[index],
            )

        def across(which, turn):
            entry = layer_at(turn) * 2 + 1 - core
            source = row_terms.at[entry] if which else terms.at[:, entry]
            target = landed_rows.at[turn] if which else landed.at[turn]
            return send_to(
                place.peer(0, 1, 0, 0),
                source,
                target,
                core_send.at[which, turn],
                core_recv.at[which, turn],
            )

        def along(which, turn):
            source = merged_rows.at[turn - 1] if which else merged.at[turn - 1]
            target = summed_rows.at[turn - 1] if which else summed.at[turn - 1]
            return send_to(
                place.peer(turn, 0, 0, 0),
                source,
                target,
                layer_send.at[which, turn - 1],
                layer_recv.at[which, turn - 1],
            )

        def swap(index):
            peer = place.peer(*steps[index])
            return send_to(
                peer,
                ready.at[peer[1]],
                whole.at[group, me],
                swap_send.at[index],
                swap_recv.at[index],
            )

        def out(which, turn, entry):
            slab = whole_rows.at[entry] if which else whole.at[entry]
            return send_to(
                place.peer(turn, 0, 0, 0),
                slab,
                slab,
                out_send.at[which, turn - 1],
                out_recv.at[which, turn - 1],
            )

        def over(which, turn, entry):
            slab = whole_rows.at[entry] if which else whole.at[entry]
            return send_to(
                place.peer(0, 1, 0, 0),
                slab,
                slab,
                over_send.at[which, turn],
                over_recv.at[which, turn],
            )

        order = [*range(1, layers), 0]
        for which in (0, 1):
            for turn in order:
                start(across(which, turn))
        for index in range(len(steps)):
            start(tail_copy(index))
        yield
        for which in (0, 1):
            for turn in order[:-1]:
                across(which, turn).wait_recv()
                entry = layer_at(turn) * 2 + core
                if which:
                    merged_rows[turn - 1] = (
                        row_terms[entry].astype(F32) + landed_rows[turn].astype(F32)
                    ).astype(BF16)
                else:
                    for shard in range(shards):
                        merged[turn - 1, shard] = (
                            terms[shard, entry].astype(F32) + landed[turn, shard].astype(F32)
                        ).astype(BF16)
                start(along(which, turn))
                yield
        for which in (0, 1):
            across(which, 0).wait_recv()
        for index in range(len(steps)):
            tail_copy(index).wait_recv()
        tails[me] = tail[me]
        tail_sum = tails[0]
        for shard in range(1, shards):
            tail_sum = tail_sum + tails[shard]
        tail_sums[group] = tail_sum
        for index in range(len(group_steps)):
            start(sum_copy(index))
        yield
        for turn in order[:-1]:
            along(0, turn).wait_recv()
        for shard in range(shards):
            value = terms[shard, group].astype(F32) + landed[0, shard].astype(F32)
            for turn in order[:-1]:
                value = value + summed[turn - 1, shard].astype(F32)
            ready[shard] = value.astype(BF16)
        for index in range(len(steps)):
            start(swap(index))
        whole[group, me] = ready[me]
        yield
        for turn in order[:-1]:
            along(1, turn).wait_recv()
        value = row_terms[group].astype(F32) + landed_rows[0].astype(F32)
        for turn in order[:-1]:
            value = value + summed_rows[turn - 1].astype(F32)
        whole_rows[group] = value.astype(BF16)
        for turn in order[:-1]:
            start(out(1, turn, group))
        start(over(1, 0, group))
        yield
        for index in range(len(steps)):
            swap(index).wait_recv()
        for turn in order[:-1]:
            start(out(0, turn, group))
        start(over(0, 0, group))
        yield
        for which in (1, 0):
            for turn in order[:-1]:
                entry = layer_at(layers - turn) * 2 + core
                out(which, turn, entry).wait_recv()
                start(over(which, turn, entry))
                yield
        for index in range(len(group_steps)):
            sum_copy(index).wait_recv()
        tail_sum = tail_sums[0]
        for index in range(1, place.groups):
            tail_sum = tail_sum + tail_sums[index]
        tail_out[...] = tail_sum
        depth = terms.shape[3] // 3
        for which in (1, 0):
            for turn in range(layers):
                entry = layer_at(layers - turn) * 2 + 1 - core
                over(which, turn, entry).wait_recv()
                yield
        for entry in range(place.groups):
            for shard in range(shards):
                here = pl.ds(shard * depth, depth)
                value = whole[entry, shard]
                query_out[entry, :, here] = value[:, :depth]
                key_out[entry, :, here] = value[:, depth : 2 * depth]
                value_out[entry, :, here] = value[:, 2 * depth :]
            yield
        for copy in sends:
            copy.wait_send()


def turn(values, cosine, sine):
    return values * cosine + pltpu.roll(values, HDIM // 2, 1) * sine


def head_forward(projected, place, gain, cosine, sine):
    proj = projected[:, place * HDIM : (place + 1) * HDIM]
    scale = rms_scale(proj)
    unit = proj * scale
    return scale, unit, turn(unit * gain, cosine, sine).astype(BF16)


def head_probs(query_rot, key_rot, seg_column, seg_row):
    scores = dot(query_rot, key_rot, NT) * (1.0 / math.sqrt(HDIM))
    scores = jnp.where(seg_column == seg_row, scores, MASK_FILL)
    exponent = jnp.exp(scores - jnp.max(scores, axis=-1, keepdims=True))
    return exponent * (1.0 / jnp.sum(exponent, axis=-1, keepdims=True))


def forward_steps(
    hidden,
    projections,
    output_weight,
    gain,
    head_gains,
    cosine,
    sine,
    seg_column,
    seg_row,
    mixer,
    projected,
    attended,
    parts,
):
    micros, span = seg_column.shape[0], seg_column.shape[1]
    heads = output_weight.shape[0] // HDIM
    tile = min(span, 256)
    for micro in range(micros):
        for start in range(0, span, tile):
            rows = pl.ds(micro * span + start, tile)
            values = hidden[rows, :].astype(F32)
            mixer[rows, :] = (values * rms_scale(values) * gain[...]).astype(BF16)
        rows = pl.ds(micro * span, span)
        projected[rows, :] = dot(mixer[rows, :], projections[...], NN)
        yield
        for head in range(heads):
            own = projected[rows, :]
            _, _, query_rot = head_forward(own, head, head_gains[0:1], cosine[...], sine[...])
            _, _, key_rot = head_forward(
                own, heads + head, head_gains[1:2], cosine[...], sine[...]
            )
            values = own[:, (2 * heads + head) * HDIM : (2 * heads + head + 1) * HDIM]
            probs = head_probs(query_rot, key_rot, seg_column[micro], seg_row[micro])
            attended[rows, head * HDIM : (head + 1) * HDIM] = dot(
                probs.astype(BF16), values.astype(BF16), NN
            ).astype(BF16)
            yield
        parts[rows, :] = dot(attended[rows, :], output_weight[...], NN).astype(BF16)
        yield


def backward_steps(
    branch,
    mixer,
    projected,
    attended,
    projections,
    output_weight,
    head_gains,
    cosine,
    sine,
    seg_column,
    seg_row,
    parts,
    projection_terms,
    output_terms,
    gain_terms,
    attended_grad,
    projected_grad,
):
    micros, span = seg_column.shape[0], seg_column.shape[1]
    heads = output_weight.shape[0] // HDIM
    scale = 1.0 / math.sqrt(HDIM)
    gain_terms[...] = jnp.zeros_like(gain_terms)
    for micro in range(micros):
        rows = pl.ds(micro * span, span)
        attended_grad[rows, :] = dot(branch[rows, :], output_weight[...], NT).astype(BF16)
        yield
        for head in range(heads):
            own = projected[rows, :]
            query_scale, query_unit, query_rot = head_forward(
                own, head, head_gains[0:1], cosine[...], sine[...]
            )
            key_scale, key_unit, key_rot = head_forward(
                own, heads + head, head_gains[1:2], cosine[...], sine[...]
            )
            values = own[:, (2 * heads + head) * HDIM : (2 * heads + head + 1) * HDIM]
            probs = head_probs(query_rot, key_rot, seg_column[micro], seg_row[micro])
            out_grad = attended_grad[rows, head * HDIM : (head + 1) * HDIM]
            prob_grad = dot(out_grad, values.astype(BF16), NT)
            row_delta = jnp.sum(probs * prob_grad, axis=-1, keepdims=True)
            score_grad = (probs * (prob_grad - row_delta)).astype(BF16)
            projected_grad[rows, (2 * heads + head) * HDIM : (2 * heads + head + 1) * HDIM] = dot(
                probs.astype(BF16), out_grad, TN
            ).astype(BF16)
            for which, (rot_grad, unit, unit_scale) in enumerate(
                (
                    (dot(score_grad, key_rot, NN) * scale, query_unit, query_scale),
                    (dot(score_grad, query_rot, TN) * scale, key_unit, key_scale),
                )
            ):
                unit_grad = turn(rot_grad, cosine[...], -sine[...])
                gain_terms[which : which + 1] += jnp.sum(unit_grad * unit, axis=0, keepdims=True)
                place = (which * heads + head) * HDIM
                projected_grad[rows, place : place + HDIM] = norm_back(
                    unit_grad * head_gains[which : which + 1], unit, unit_scale
                ).astype(BF16)
            yield
        parts[rows, :] = dot(projected_grad[rows, :], projections[...], NT).astype(BF16)
        yield
    tile = min(512, branch.shape[1])
    for start in range(0, branch.shape[1], tile):
        here = pl.ds(start, tile)
        output_terms[:, here] = dot(attended[...], branch[:, here], TN).astype(BF16)
        projection_terms[here, :] = dot(mixer[:, here], projected_grad[...], TN).astype(BF16)
        yield


def whole_kernel(steps):
    def kernel(*refs):
        for _ in steps(*refs):
            pass

    return kernel


def attention_forward(hidden, projections, output_weight, gain, head_gains, tables, segments):
    tokens, width = hidden.shape
    column_width = output_weight.shape[0]
    return pl.pallas_call(
        whole_kernel(forward_steps),
        in_specs=[RESIDENT] * 9,
        out_specs=[RESIDENT] * 4,
        out_shape=[
            jax.ShapeDtypeStruct((tokens, width), BF16),
            jax.ShapeDtypeStruct((tokens, 3 * column_width), F32),
            jax.ShapeDtypeStruct((tokens, column_width), BF16),
            jax.ShapeDtypeStruct((tokens, width), BF16),
        ],
        compiler_params=pltpu.CompilerParams(vmem_limit_bytes=VMEM_LIMIT),
        name="attention_forward",
    )(hidden, projections, output_weight, gain, head_gains, *tables, *segments)


def attention_backward(
    branch, mixer, projected, attended, projections, output_weight, head_gains, tables, segments
):
    tokens, width = branch.shape
    column_width = output_weight.shape[0]
    return pl.pallas_call(
        whole_kernel(backward_steps),
        in_specs=[RESIDENT] * 11,
        out_specs=[RESIDENT] * 4,
        out_shape=[
            jax.ShapeDtypeStruct((tokens, width), BF16),
            jax.ShapeDtypeStruct((width, 3 * column_width), BF16),
            jax.ShapeDtypeStruct((column_width, width), BF16),
            jax.ShapeDtypeStruct((8, HDIM), F32),
        ],
        scratch_shapes=[
            pltpu.VMEM((tokens, column_width), BF16),
            pltpu.VMEM((tokens, 3 * column_width), BF16),
        ],
        compiler_params=pltpu.CompilerParams(vmem_limit_bytes=VMEM_LIMIT),
        name="attention_backward",
    )(
        branch,
        mixer,
        projected,
        attended,
        projections,
        output_weight,
        head_gains,
        *tables,
        *segments,
    )


def units_kernel(
    span,
    rows_ref,
    upstream_ref,
    share_ref,
    gate_ref,
    up_ref,
    down_ref,
    hidden_ref,
    gate_pre_ref,
    up_pre_ref,
    dot_ref,
):
    half = pl.program_id(0)
    half_width = gate_ref.shape[2]
    lanes = lax.broadcasted_iota(jnp.int32, share_ref.shape, 1)
    share = jnp.sum(jnp.where(lanes == half, share_ref[...], 0.0), axis=1, keepdims=True)

    def body(step, carry):
        units = pl.ds(pl.multiple_of(step * span, span), span)
        gate_pre = dot(rows_ref[...], gate_ref[0, :, units], NN)
        up_pre = dot(rows_ref[...], up_ref[0, :, units], NN)
        units_grad = dot(upstream_ref[...], down_ref[0, units, :], NT)
        sigmoid_gate = 1.0 / (1.0 + jnp.exp(-gate_pre))
        swish_gate = gate_pre * sigmoid_gate
        activated = swish_gate * up_pre
        dots = jnp.sum(activated * units_grad, axis=1, keepdims=True)
        dot_ref[...] += jnp.where(lanes == half, dots, 0.0)
        hidden_ref[0, :, units] = (activated * share).astype(BF16)
        weighted = units_grad * share
        gate_pre_ref[0, :, units] = (
            weighted * up_pre * (sigmoid_gate * (1.0 + gate_pre * (1.0 - sigmoid_gate)))
        ).astype(BF16)
        up_pre_ref[0, :, units] = (weighted * swish_gate).astype(BF16)
        return carry

    @pl.when(half == 0)
    def _():
        dot_ref[...] = jnp.zeros_like(dot_ref)

    lax.fori_loop(0, half_width // span, body, 0)


def expert_units(rows, upstream, share, gate_all, up_all, down_all):
    tokens, width = rows.shape
    halves, _, units = gate_all.shape

    def each(*shape):
        return pl.BlockSpec((1,) + shape, lambda half: (half,) + (0,) * len(shape))

    whole = pl.BlockSpec(memory_space=pltpu.VMEM)
    return pl.pallas_call(
        functools.partial(units_kernel, 256 if tokens <= 1024 else 128),
        grid=(halves,),
        in_specs=[whole, whole, whole, each(width, units), each(width, units), each(units, width)],
        out_specs=[each(tokens, units), each(tokens, units), each(tokens, units), whole],
        out_shape=[
            jax.ShapeDtypeStruct((halves, tokens, units), BF16),
            jax.ShapeDtypeStruct((halves, tokens, units), BF16),
            jax.ShapeDtypeStruct((halves, tokens, units), BF16),
            jax.ShapeDtypeStruct(share.shape, F32),
        ],
        compiler_params=pltpu.CompilerParams(vmem_limit_bytes=VMEM_LIMIT),
        cost_estimate=pl.CostEstimate(
            flops=6 * tokens * width * units * halves,
            bytes_accessed=6 * width * units * halves,
            transcendentals=0,
        ),
    )(rows, upstream, share, gate_all, up_all, down_all)


def merge_kernel(gate_pre_ref, up_pre_ref, gate_ref, up_ref, grad_ref):
    halves = gate_pre_ref.shape[0]
    grad = dot(gate_pre_ref[0], gate_ref[0], NT) + dot(up_pre_ref[0], up_ref[0], NT)
    for half in range(1, halves):
        grad = grad + dot(gate_pre_ref[half], gate_ref[half], NT)
        grad = grad + dot(up_pre_ref[half], up_ref[half], NT)
    grad_ref[...] = grad.astype(BF16)


def expert_merge(gate_pre, up_pre, gate_all, up_all):
    halves, tokens, units = gate_pre.shape
    width = gate_all.shape[1]
    span = 256
    batch = min(tokens, 1024)
    slab = pl.BlockSpec(
        (halves, batch, units), lambda turn, step: (0, turn, 0), pipeline_mode=pl.Buffered(1)
    )
    tile = pl.BlockSpec((halves, span, units), lambda turn, step: (0, step, 0))
    return pl.pallas_call(
        merge_kernel,
        grid=(tokens // batch, width // span),
        in_specs=[slab, slab, tile, tile],
        out_specs=pl.BlockSpec((batch, span), lambda turn, step: (turn, step)),
        out_shape=jax.ShapeDtypeStruct((tokens, width), BF16),
        compiler_params=pltpu.CompilerParams(vmem_limit_bytes=VMEM_LIMIT),
        cost_estimate=pl.CostEstimate(
            flops=4 * tokens * width * units * halves,
            bytes_accessed=4 * width * units * halves,
            transcendentals=0,
        ),
    )(gate_pre, up_pre, gate_all, up_all)


def output_kernel(hidden_ref, down_ref, out_ref):
    halves = hidden_ref.shape[0]
    out = dot(hidden_ref[0], down_ref[0], NN)
    for half in range(1, halves):
        out = out + dot(hidden_ref[half], down_ref[half], NN)
    out_ref[...] = out.astype(BF16)


def expert_output(hidden, down_all):
    halves, tokens, units = hidden.shape
    width = down_all.shape[2]
    span = 256
    batch = min(tokens, 1024)
    slab = pl.BlockSpec(
        (halves, batch, units), lambda turn, step: (0, turn, 0), pipeline_mode=pl.Buffered(1)
    )
    return pl.pallas_call(
        output_kernel,
        grid=(tokens // batch, width // span),
        in_specs=[slab, pl.BlockSpec((halves, units, span), lambda turn, step: (0, 0, step))],
        out_specs=pl.BlockSpec((batch, span), lambda turn, step: (turn, step)),
        out_shape=jax.ShapeDtypeStruct((tokens, width), BF16),
        compiler_params=pltpu.CompilerParams(vmem_limit_bytes=VMEM_LIMIT),
        cost_estimate=pl.CostEstimate(
            flops=2 * tokens * width * units * halves,
            bytes_accessed=2 * width * units * halves,
            transcendentals=0,
        ),
    )(hidden, down_all)


def weights_kernel(
    span,
    rows_ref,
    upstream_ref,
    hidden_ref,
    gate_pre_ref,
    up_pre_ref,
    gate_grad_ref,
    up_grad_ref,
    down_grad_ref,
):
    def body(step, carry):
        units = pl.ds(pl.multiple_of(step * span, span), span)
        gate_grad_ref[0, :, units] = dot(rows_ref[...], gate_pre_ref[0, :, units], TN).astype(BF16)
        up_grad_ref[0, :, units] = dot(rows_ref[...], up_pre_ref[0, :, units], TN).astype(BF16)
        down_grad_ref[0, units, :] = dot(
            hidden_ref[0, :, units], upstream_ref[...], TN
        ).astype(BF16)
        return carry

    lax.fori_loop(0, gate_grad_ref.shape[2] // span, body, 0)


def expert_weights(rows, upstream, hidden, gate_pre, up_pre):
    tokens, width = rows.shape
    halves, _, units = hidden.shape

    def each(*shape):
        return pl.BlockSpec((1,) + shape, lambda half: (half,) + (0,) * len(shape))

    whole = pl.BlockSpec(memory_space=pltpu.VMEM)
    slab = each(tokens, units)
    return pl.pallas_call(
        functools.partial(weights_kernel, 256),
        grid=(halves,),
        in_specs=[whole, whole, slab, slab, slab],
        out_specs=[each(width, units), each(width, units), each(units, width)],
        out_shape=[
            jax.ShapeDtypeStruct((halves, width, units), BF16),
            jax.ShapeDtypeStruct((halves, width, units), BF16),
            jax.ShapeDtypeStruct((halves, units, width), BF16),
        ],
        compiler_params=pltpu.CompilerParams(vmem_limit_bytes=VMEM_LIMIT),
        cost_estimate=pl.CostEstimate(
            flops=6 * tokens * width * units * halves,
            bytes_accessed=6 * width * units * halves,
            transcendentals=0,
        ),
    )(rows, upstream, hidden, gate_pre, up_pre)


def per_device(
    groups,
    shards,
    wide,
    inputs,
    segment_ids,
    routes,
    cotangent,
    query_weight,
    key_weight,
    value_weight,
    output_weight,
    router_weight,
    attention_gain,
    expert_gain,
    query_gain,
    key_gain,
    gate_weight,
    up_weight,
    down_weight,
):
    micros, rows, width = inputs.shape
    deep = shards // wide
    span = shards * rows
    tokens = micros * span
    experts = router_weight.shape[1]
    column_width = width // shards
    shard_place = lax.axis_index("shard")
    layout = (groups, deep, shards // deep)

    gate_all = lax.all_gather(gate_weight, "expert", axis=0, tiled=True)
    up_all = lax.all_gather(up_weight, "expert", axis=0, tiled=True)
    down_all = lax.all_gather(down_weight, "expert", axis=0, tiled=True)

    cuts = [
        column_width * experts,
        column_width,
        column_width,
        HDIM // shards,
        HDIM // shards,
        routes.size,
    ]
    starts = [sum(cuts[:place]) for place in range(len(cuts))]
    small_own = jnp.concatenate(
        [
            router_weight.reshape(-1),
            attention_gain,
            expert_gain,
            query_gain,
            key_gain,
            routes.reshape(-1).astype(BF16),
        ]
    )
    small_own = jnp.pad(small_own, (0, -sum(cuts) % 2048)).reshape(-1, 128)
    (projections, small), (hidden_all, upstream_all) = fuse(
        [
            Columns((query_weight, key_weight, value_weight), small_own, layout),
            Chain(Gather(inputs, layout), Gather(cotangent, layout)),
        ],
        layout,
        0,
        "entry",
    )
    hidden_all = hidden_all.reshape(tokens, width)
    upstream_all = upstream_all.reshape(tokens, width)
    projections = projections.reshape(width, 3 * column_width)
    small = small.reshape(shards, -1)
    router_full, attn_gain, expert_gain_full, query_gain_full, key_gain_full, routes_all = (
        small[:, start : start + length]
        for start, length in zip(starts, cuts, strict=True)
    )
    router_full = router_full.reshape(width, experts)
    attn_gain = attn_gain.reshape(-1).astype(F32)
    expert_gain_full = expert_gain_full.reshape(-1).astype(F32)
    query_gain_full = query_gain_full.reshape(-1).astype(F32)
    key_gain_full = key_gain_full.reshape(-1).astype(F32)
    routes_all = routes_all.reshape(shards, micros, rows, -1).transpose(1, 0, 2, 3)
    routes_all = routes_all.reshape(tokens, -1).astype(jnp.int32)

    head_gains = jnp.pad(jnp.stack([query_gain_full, key_gain_full]), ((0, 6), (0, 0)))
    tables = rotary(span)
    segments = (segment_ids[:, :, None], segment_ids[:, None, :])
    mixer_all, projected, attended, middle_parts = attention_forward(
        hidden_all, projections, output_weight, attn_gain[None], head_gains, tables, segments
    )
    hidden = inputs.astype(F32)
    ((middle_total,),) = fuse(
        [Scatter(middle_parts.reshape(micros, shards, rows, width), layout)], layout, 1, "middle"
    )
    middle = hidden + middle_total

    scale_second = rms_scale(middle)
    normed_second = middle * scale_second
    expert_input = (normed_second * expert_gain_full).astype(BF16)
    ((expert_all,),) = fuse([Gather(expert_input, layout)], layout, 2, "experts_in")
    expert_all = expert_all.reshape(tokens, width)
    logits = jnp.dot(expert_all, router_full, preferred_element_type=F32)
    choose = (routes_all[:, :, None] == jnp.arange(experts, dtype=jnp.int32)).astype(F32)
    share = softmax_rows(jnp.sum(choose * logits[:, None, :], axis=-1))
    share_wide = jnp.sum(choose * share[:, :, None], axis=1)
    served = (jnp.arange(groups, dtype=jnp.int32) * shards + shard_place) // 2
    serves = (served[:, None] == jnp.arange(experts, dtype=jnp.int32)).astype(F32)
    share_own = jnp.pad(
        jnp.dot(share_wide, serves.T, precision=PRECISE), ((0, 0), (0, 128 - groups))
    )
    activated, gate_pre, up_pre, dots = expert_units(
        expert_all, upstream_all, share_own, gate_all, up_all, down_all
    )
    early = tokens <= 1024
    expert_grad_parts = expert_merge(gate_pre, up_pre, gate_all, up_all)
    if not early:
        gate_pre, expert_grad_parts = lax.optimization_barrier((gate_pre, expert_grad_parts))
        gate_terms, up_terms, down_terms = expert_weights(
            expert_all, upstream_all, activated, gate_pre, up_pre
        )
        out_parts = expert_output(activated, down_all)

    halves = groups * shards
    lanes = 2 * halves + -2 * halves % 128
    columns = jnp.arange(groups, dtype=jnp.int32) * shards + shard_place
    columns = (columns[:, None] == jnp.arange(halves, dtype=jnp.int32)).astype(F32)
    placed = jnp.dot(dots[:, :groups], columns, precision=PRECISE)
    placed_high = placed.astype(BF16)
    placed_low = (placed - placed_high.astype(F32)).astype(BF16)
    placed = jnp.pad(
        jnp.concatenate([placed_high, placed_low], axis=1), ((0, 0), (0, lanes - 2 * halves))
    )
    returned = [
        Scatter(placed.reshape(micros, shards, rows, lanes), layout),
        Scatter(expert_grad_parts.reshape(micros, shards, rows, width), layout),
    ]
    if early:
        returned.append(
            ExpertWeights(
                expert_all, upstream_all, activated, gate_pre, up_pre, down_all, layout
            )
        )
        (dot_total,), (expert_grad,), (_, up_terms, down_terms, out_parts, gate_grad) = fuse(
            returned, layout, 3, "experts_out"
        )
    else:
        returned.append(ExpertScatter(gate_terms, layout))
        (dot_total,), (expert_grad,), (gate_grad,) = fuse(returned, layout, 3, "experts_out")

    def own_rows(values):
        return lax.dynamic_slice_in_dim(
            values.reshape((micros, span) + values.shape[1:]), shard_place * rows, rows, 1
        )

    own_choose, own_share = own_rows(choose), own_rows(share)
    share_grad_wide = dot_total[..., :halves] + dot_total[..., halves : 2 * halves]
    share_grad_wide = share_grad_wide.reshape(micros, rows, experts, 2).sum(axis=-1)
    share_grad = jnp.sum(own_choose * share_grad_wide[:, :, None, :], axis=-1)
    chosen_grad = own_share * (
        share_grad - jnp.sum(own_share * share_grad, axis=-1, keepdims=True)
    )
    own_logits_grad = jnp.sum(own_choose * chosen_grad[..., None], axis=2)
    expert_grad = expert_grad + jnp.dot(
        own_logits_grad, router_full.astype(F32).T, precision=PRECISE
    )
    expert_gain_term = jnp.sum(expert_grad * normed_second, axis=(0, 1))
    middle_grad = cotangent.astype(F32) + norm_back(
        expert_grad * expert_gain_full, normed_second, scale_second
    )
    router_term = jnp.einsum(
        "mtd,mte->de", expert_input.astype(F32), own_logits_grad, precision=PRECISE
    )
    (branch_all,), (up_grad,) = fuse(
        [Gather(middle_grad.astype(BF16), layout), ExpertScatter(up_terms, layout)],
        layout,
        4,
        "branch",
    )
    branch_all = branch_all.reshape(tokens, width)

    mixer_parts, projection_terms, output_term, head_gain_terms = attention_backward(
        branch_all,
        mixer_all,
        projected,
        attended,
        projections,
        output_weight,
        head_gains,
        tables,
        segments,
    )
    (mixer_grad,), (down_grad,) = fuse(
        [
            Scatter(mixer_parts.reshape(micros, shards, rows, width), layout),
            ExpertScatter(down_terms, layout),
        ],
        layout,
        5,
        "mixer",
    )
    scale_first = rms_scale(hidden)
    normed_first = hidden * scale_first
    attn_gain_term = jnp.sum(mixer_grad * normed_first, axis=(0, 1))
    hidden_grad = middle_grad + norm_back(mixer_grad * attn_gain, normed_first, scale_first)

    part = column_width // groups
    tail = jnp.concatenate(
        [
            term.reshape(shards, -1)
            for term in (
                router_term,
                attn_gain_term,
                expert_gain_term,
                head_gain_terms[0],
                head_gain_terms[1],
            )
        ],
        axis=1,
    )
    tail = jnp.pad(tail, ((0, 0), (0, -tail.shape[1] % 1024))).reshape(shards, -1, 128)
    (outs,), (output_grad, tail, query_grad, key_grad, value_grad) = fuse(
        [
            Scatter(out_parts.reshape(micros, shards, rows, width), layout),
            Rows(
                projection_terms.reshape(shards, groups, part, 3 * column_width),
                output_term.reshape(groups, part, width),
                tail,
                layout,
            ),
        ],
        layout,
        6,
        "exit",
    )
    result = middle + outs
    tail = tail.reshape(-1)
    tails = [
        tail[start : start + length]
        for start, length in zip(starts[:5], cuts[:5], strict=True)
    ]
    return (
        result.astype(BF16),
        hidden_grad.astype(BF16),
        query_grad.astype(F32).reshape(column_width, width),
        key_grad.astype(F32).reshape(column_width, width),
        value_grad.astype(F32).reshape(column_width, width),
        output_grad.astype(F32).reshape(column_width, width),
        tails[0].reshape(column_width, experts),
        tails[1],
        tails[2],
        tails[3],
        tails[4],
        gate_grad.astype(F32)[None],
        up_grad.astype(F32)[None],
        down_grad.astype(F32)[None],
    )


def solution(mesh):
    groups, shards = mesh.shape["expert"], mesh.shape["shard"]
    wide = shards // 4 if shards % 4 == 0 else 1
    in_specs = (
        P(None, ("expert", "shard"), None),
        P(None, "expert"),
        P(None, ("expert", "shard"), None),
        P(None, ("expert", "shard"), None),
        P("shard", None),
        P("shard", None),
        P("shard", None),
        P("shard", None),
        P("shard", None),
        P("shard"),
        P("shard"),
        P("shard"),
        P("shard"),
        P(("expert", "shard"), None, None),
        P(("expert", "shard"), None, None),
        P(("expert", "shard"), None, None),
    )
    out_specs = (
        P(None, ("expert", "shard"), None),
        P(None, ("expert", "shard"), None),
        P("shard", None),
        P("shard", None),
        P("shard", None),
        P("shard", None),
        P("shard", None),
        P("shard"),
        P("shard"),
        P("shard"),
        P("shard"),
        P(("expert", "shard"), None, None),
        P(("expert", "shard"), None, None),
        P(("expert", "shard"), None, None),
    )
    return jax.shard_map(
        functools.partial(per_device, groups, shards, wide),
        mesh=mesh,
        in_specs=in_specs,
        out_specs=out_specs,
        check_vma=False,
    )
```

time: 1270 us -> 812 us (0.64)
  waiting for transfers between devices: 298 us -> 2.06 us
  local copies, waits for them, and re-layouts: 74 us -> 18.8 us
  matrix products: 55.6 us -> 9.81 us
  blocking collectives: 23.6 us -> 0 us
  other arithmetic: 48.5 us -> 27.2 us
    reduce_scatter x3 -> x0, waiting for transfers between devices: 208 us -> none  [the longest x1 70.2 us: per_device(): lax.psum_scatter(down_terms, 'expert', scatter_dimension=0, tiled=True)]
    psum x3 -> x0, waiting for transfers between devices: 88.3 us -> none  [the longest x1 83.6 us: per_device(): lax.psum((projection_terms, output_term.astype(BF16)), 'expert')]
    dot_general x12 -> x1, matrix products: 41.4 us -> 1.51 us  [per_device(): placed = jnp.dot(dots[:, :groups], columns, precision=PRECISE)]
    convert_element_type x10 -> x3, other arithmetic: 24.3 us -> 0.09 us  [the longest x1 0.08 us: per_device(): routes_all = routes_all.reshape(tokens, -1).astype(jnp.int32)]
    all_gather x1 -> x0, blocking collectives: 23.6 us -> none  [per_device(): lax.all_gather(routes, 'shard', axis=1, tiled=True).reshape(tokens, -1)]
    reshape x7 -> x5, local copies, waits for them, and re-layouts: 21.2 us -> 3.22 us  [the longest x3 2.22 us: per_device(): term.reshape(shards, -1)]
    pallas_call x10 -> x9, Pallas kernels: 669 us -> 668 us  [the longest x7 624 us: fuse(): pl.pallas_call(kernel, out_shape=out_shape, in_specs=in_specs, out_specs=...]
  transfers between devices with their start and end apart: 12 -> 3, of which waited for: 5 -> 0; matrix products, arithmetic and copies ran while one was open for 9% -> 2% of each run, Pallas kernels for 50% -> 35%
where the time goes in v2:
time: 812 us; the launch traced here: 803 us
  Pallas kernels  730 us (90%)
  other arithmetic  27.2 us (3%)
  local copies, waits for them, and re-layouts  18.8 us (2%)
  between operations  14.7 us (2%)
  matrix products  9.81 us (1%)
    pallas_call x7, Pallas kernels, fuse(): pl.pallas_call(kernel, out_shape=out_shape, in_specs=in_specs, out_specs=...  624 us
    pallas_call x1, Pallas kernels, expert_units(): pl.pallas_call(functools.partial(units_kernel, 256 if tokens <= 1024 else...  37.5 us
    pallas_call x1, Pallas kernels, attention_backward(): pl.pallas_call(whole_kernel(backward_steps), in_specs=[RESIDENT] * 11, ou...  28.2 us
    pallas_call x1, Pallas kernels, expert_merge(): pl.pallas_call(merge_kernel, grid=(tokens // batch, width // span), in_sp...  24.4 us
  transfers between devices with their start and end apart: 3, of which 0 were waited for; matrix products, arithmetic and copies ran while one was open for 2% of the time, Pallas kernels for 35%

profile of v2, /device:TPU:11, one launch (start us, length us, event | category | flops | bytes accessed | tf_op | source)
XLA Modules:
  0.0 803.0 jit_solution(4528550840781129544)
XLA Ops:
  10.7 145.8 %entry.1 = (bf16[8,4,64,768]{3,2,1,0:T(8,128)(2,1)}, bf16[8,48,128]{2,1,0:T(8,128)(2,1)}, bf16[2,8,64,2048]{3,2,1,0:T(8,128)(2,1)}, bf16[2,8,64,2048]{3,2,1,0:T(8,128)(2,1)}) custom-call(bf16[256,2048]{1,0:T(8,128)(2,1)} %refs_0_.1, bf16[256,2048]{1,0:T(8,128)(2,1)} %refs_1_.1, bf16[256,2048]{1,0:T(8,128)(2,1)} %refs_2_.2, ...), custom_call_target="tpu_custom_call" | custom-call | flops 60000002048 | bytes 8388608 | tf_op jit(solution)/shard_map/entry/pallas_call | solution.py:157
  164.5 16.2 %attention_forward.1 = (bf16[1024,2048]{1,0:T(8,128)(2,1)}, f32[1024,768]{1,0:T(8,128)}, bf16[1024,256]{1,0:T(8,128)(2,1)}, bf16[1024,2048]{1,0:T(8,128)(2,1)}) custom-call(bf16[1024,2048]{1,0:T(8,128)(2,1)} %bitcast.91, bf16[2048,768]{1,0:T(8,128)(2,1)} %bitcast.87, bf16[256,2048]{1,0:T(8,128)(2,1)} %refs_5_.3, f32[1,2048]{1,0:T(1,128)} %bitcast.109, ...), custom_call_target="tpu_custom_call" | custom-call | tf_op jit(solution)/shard_map/attention_forward/pallas_call | solution.py:1109
  180.7 62.2 %middle.1 = f32[2,64,2048]{2,1,0:T(8,128)} custom-call(bf16[2,8,64,2048]{3,2,1,0:T(8,128)(2,1)} %bitcast.113), custom_call_target="tpu_custom_call" | custom-call | flops 60000002048 | bytes 8388608 | tf_op jit(solution)/shard_map/middle/pallas_call | solution.py:157
  242.9 1.5 multiply_reduce_fusion.2
  246.4 58.7 %experts_in.1 = bf16[2,8,64,2048]{3,2,1,0:T(8,128)(2,1)} custom-call(bf16[2,64,2048]{2,1,0:T(8,128)(2,1)} %multiply_convert_fusion.refs_0_), custom_call_target="tpu_custom_call" | custom-call | flops 60000002048 | bytes 8388608 | tf_op jit(solution)/shard_map/experts_in/pallas_call | solution.py:157
  305.1 3.4 fusion.30
  311.0 37.5 %shard_map.263 = (bf16[4,1024,512]{2,1,0:T(8,128)(2,1)}, bf16[4,1024,512]{2,1,0:T(8,128)(2,1)}, bf16[4,1024,512]{2,1,0:T(8,128)(2,1)}, f32[1024,128]{1,0:T(8,128)}) custom-call(bf16[1024,2048]{1,0:T(8,128)(2,1)} %bitcast.85, bf16[1024,2048]{1,0:T(8,128)(2,1)} %bitcast.116, f32[1024,128]{1,0:T(8,128)} %pad.25.share_ref, ...), custom_call_target="tpu_custom_call" | custom-call | flops 25769803776 | bytes 25165824 | tf_op jit(solution)/shard_map/pallas_call | solution.py:1209
  351.0 24.4 %shard_map.264 = bf16[1024,2048]{1,0:T(8,128)(2,1)} custom-call(bf16[4,1024,512]{2,1,0:T(8,128)(2,1)} %get-tuple-element.52.gate_pre_ref.refs_5_, bf16[4,1024,512]{2,1,0:T(8,128)(2,1)} %get-tuple-element.53.up_pre_ref.refs_6_, bf16[4,2048,512]{2,1,0:T(8,128)(2,1)} %all-gather.4.cloned.1.call-done.gate_ref, ...), custom_call_target="tpu_custom_call" | custom-call | flops 17179869184 | bytes 16777216 | tf_op jit(solution)/shard_map/pallas_call | solution.py:1247
  375.4 102.3 %experts_out.1 = (f32[2,64,128]{2,1,0:T(8,128)}, f32[2,64,2048]{2,1,0:T(8,128)}, bf16[4,2048,512]{2,1,0:T(8,128)(2,1)}, bf16[4,2048,512]{2,1,0:T(8,128)(2,1)}, b...) custom-call(bf16[2,8,64,128]{3,2,1,0:T(8,128)(2,1)} %bitcast.99, ...), custom_call_target="tpu_custom_call" | custom-call | flops 60000002048 | bytes 8388608 | tf_op jit(solution)/shard_map/experts_out/pallas_call | solution.py:157
  479.1 2.2 convolution_bitcast_fusion
  481.3 2.1 multiply_reduce_fusion
  483.5 2.2 reshape.321
  486.8 66.8 %branch.1 = (bf16[2,8,64,2048]{3,2,1,0:T(8,128)(2,1)}, bf16[2048,512]{1,0:T(8,128)(2,1)}) custom-call(bf16[2,64,2048]{2,1,0:T(8,128)(2,1)} %fusion.15.refs_0_, bf16[4,2048,512]{2,1,0:T(8,128)(2,1)} %get-tuple-element.58.refs_1_), custom_call_target="tpu_custom_call" | custom-call | flops 60000002048 | bytes 8388608 | tf_op jit(solution)/shard_map/branch/pallas_call | solution.py:157
  553.7 28.2 %attention_backward.1 = (bf16[1024,2048]{1,0:T(8,128)(2,1)}, bf16[2048,768]{1,0:T(8,128)(2,1)}, bf16[256,2048]{1,0:T(8,128)(2,1)}, f32[8,128]{1,0:T(8,128)}) custom-call(bf16[1024,2048]{1,0:T(8,128)(2,1)} %bitcast.92, bf16[1024,2048]{1,0:T(8,128)(2,1)} %get-tuple-element.60.refs_1_, f32[1024,768]{1,0:T(8,128)} %get-tuple-element.61.refs_2_, ...), custom_call_target="tpu_custom_call" | custom-call | tf_op jit(solution)/shard_map/attention_backward/pallas_call | solution.py:1129
  582.8 77.4 %mixer.1 = (f32[2,64,2048]{2,1,0:T(8,128)}, bf16[512,2048]{1,0:T(8,128)(2,1)}) custom-call(bf16[2,8,64,2048]{3,2,1,0:T(8,128)(2,1)} %bitcast.112, bf16[4,512,2048]{2,1,0:T(8,128)(2,1)} %get-tuple-element.66.refs_1_), custom_call_target="tpu_custom_call" | custom-call | flops 60000002048 | bytes 8388608 | tf_op jit(solution)/shard_map/mixer/pallas_call | solution.py:157
  660.3 1.6 fusion.4
  662.7 110.8 %exit.1 = (f32[2,64,2048]{2,1,0:T(8,128)}, bf16[4,64,2048]{2,1,0:T(8,128)(2,1)}, f32[40,128]{1,0:T(8,128)}, bf16[4,64,2048]{2,1,0:T(8,128)(2,1)}, bf16[4,64,2048...) custom-call(bf16[2,8,64,2048]{3,2,1,0:T(8,128)(2,1)} %bitcast.118, bf16[8,4,64,768]{3,2,1,0:T(8,128)(2,1)} %bitcast.114, ...), custom_call_target="tpu_custom_call" | custom-call | flops 60000002048 | bytes 8388608 | tf_op jit(solution)/shard_map/exit/pallas_call | solution.py:157
  777.8 2.9 bitcast_convert_fusion.6
  780.7 1.6 bitcast_convert_fusion.5
  782.3 1.6 bitcast_convert_fusion.4
  784.0 1.6 bitcast_convert_fusion.3
  785.6 2.5 bitcast_convert_fusion
  788.2 2.6 bitcast_convert_fusion.1
  790.8 2.7 bitcast_convert_fusion.2
  (154 shorter events, 29.3 us)
Async XLA Ops:
  7.2 303.8 %all-gather.4.cloned.1.call-start = ((), (), s32[]{:S(2)}) async-start(), calls=%async_computation | async-start | bytes 10485760 | tf_op jit(solution)/shard_map/all_gather | solution.py:1374
  8.0 303.0 %all-gather.6.cloned.1.call-start = ((), (), s32[]{:S(2)}) async-start(), calls=%async_computation.1 | async-start | bytes 10485760 | tf_op jit(solution)/shard_map/all_gather | solution.py:1375
  8.7 302.3 %all-gather.8.cloned.1.call-start = ((), (), s32[]{:S(2)}) async-start(), calls=%async_computation.2 | async-start | bytes 10485760 | tf_op jit(solution)/shard_map/all_gather | solution.py:1376
  10.7 147.6 %copy-start.25 = (s32[2,512]{1,0:T(2,128)S(1)}, s32[2,512]{1,0:T(2,128)}, u32[]{:S(2)}) copy-start(s32[2,512]{1,0:T(2,128)} %param.17) | copy-start | bytes 12292
  160.8 83.7 %copy-start.18 = (f32[1,2,8,128]{3,1,2,0:T(2,128)}, f32[1,2,8,128]{3,1,2,0:T(2,128)S(1)}, u32[]{:S(2)}) copy-start(f32[1,2,8,128]{3,1,2,0:T(2,128)S(1)} %copy.85) | copy-start | bytes 24580
  180.7 62.2 %copy-start.5 = (bf16[2,64,2048]{2,1,0:T(8,128)(2,1)S(1)}, bf16[2,64,2048]{2,1,0:T(8,128)(2,1)}, u32[]{:S(2)}) copy-start(bf16[2,64,2048]{2,1,0:T(8,128)(2,1)} %refs_4_.1) | copy-start | bytes 1572868
  244.4 60.6 %copy-start.22 = (f32[2,64]{1,0:T(2,128)}, f32[2,64]{1,0:T(2,128)S(1)}, u32[]{:S(2)}) copy-start(f32[2,64]{1,0:T(2,128)S(1)} %add_rsqrt_fusion.1) | copy-start | bytes 1540
  375.4 103.7 %copy-start.11 = (bf16[2,64,2048]{2,1,0:T(8,128)(2,1)S(1)}, bf16[2,64,2048]{2,1,0:T(8,128)(2,1)}, u32[]{:S(2)}) copy-start(bf16[2,64,2048]{2,1,0:T(8,128)(2,1)} %multiply_convert_fusion.refs_0_) | copy-start | bytes 1572868
  375.4 105.9 %copy-start.1 = (f32[2,64,2048]{2,1,0:T(8,128)S(1)}, f32[2,64,2048]{2,1,0:T(8,128)}, u32[]{:S(2)}) copy-start(f32[2,64,2048]{2,1,0:T(8,128)} %copy-done) | copy-start | bytes 3145732
  375.4 105.9 %copy-start.19 = (f32[1,2,8,128]{3,1,2,0:T(2,128)S(1)}, f32[1,2,8,128]{3,1,2,0:T(2,128)}, u32[]{:S(2)}) copy-start(f32[1,2,8,128]{3,1,2,0:T(2,128)} %copy-done.18) | copy-start | bytes 24580
  375.4 105.9 %copy-start.23 = (f32[2,64]{1,0:T(2,128)S(1)}, f32[2,64]{1,0:T(2,128)}, u32[]{:S(2)}) copy-start(f32[2,64]{1,0:T(2,128)} %copy-done.22) | copy-start | bytes 1540
  477.7 8.0 copy-start.12
  483.4 70.2 %copy-start.3 = (f32[2,64,2048]{2,1,0:T(8,128)}, f32[2,64,2048]{2,1,0:T(8,128)S(1)}, u32[]{:S(2)}) copy-start(f32[2,64,2048]{2,1,0:T(8,128)S(1)} %get-tuple-element.159) | copy-start | bytes 3145732
  483.5 70.2 %copy-start.27 = (f32[2,64]{1,0:T(2,128)}, f32[2,64]{1,0:T(2,128)S(1)}, u32[]{:S(2)}) copy-start(f32[2,64]{1,0:T(2,128)S(1)} %broadcast_multiply_fusion.1) | copy-start | bytes 1540
  582.8 77.5 %copy-start.6 = (bf16[2,64,2048]{2,1,0:T(8,128)(2,1)S(1)}, bf16[2,64,2048]{2,1,0:T(8,128)(2,1)}, u32[]{:S(2)}) copy-start(bf16[2,64,2048]{2,1,0:T(8,128)(2,1)} %refs_4_.1) | copy-start | bytes 1572868
  582.8 77.5 %copy-start.21 = (f32[1,2,8,128]{3,1,2,0:T(2,128)S(1)}, f32[1,2,8,128]{3,1,2,0:T(2,128)}, u32[]{:S(2)}) copy-start(f32[1,2,8,128]{3,1,2,0:T(2,128)} %copy.87) | copy-start | bytes 24580
  582.8 77.5 %copy-start.26 = (f32[2,64]{1,0:T(2,128)S(1)}, f32[2,64]{1,0:T(2,128)}, u32[]{:S(2)}) copy-start(f32[2,64]{1,0:T(2,128)} %add_rsqrt_fusion) | copy-start | bytes 1540
  773.5 7.1 copy-start.16
  773.6 8.8 %copy-start.15 = (bf16[4,64,2048]{2,1,0:T(8,128)(2,1)S(1)}, bf16[4,64,2048]{2,1,0:T(8,128)(2,1)}, u32[]{:S(2)}) copy-start(bf16[4,64,2048]{2,1,0:T(8,128)(2,1)} %get-tuple-element.72) | copy-start | bytes 3145732
  777.8 6.2 copy-start.14
  780.7 4.9 copy-start.10
  784.0 4.2 copy-start.9
  790.8 3.8 copy-start.17
  790.8 3.8 copy-start.20
  (14 other events, 38.6 us)
Sparse Core Ops, SparseCore 0:
  9.6 76.6 all-gather.3
  87.9 58.2 all-gather.5
  147.8 58.2 all-gather.7

commit v3 on v2

--- a/solution.py
+++ b/solution.py
@@ -19,7 +19,7 @@
 NN = (((1,), (0,)), ((), ()))
 NT = (((1,), (1,)), ((), ()))
 TN = (((0,), (0,)), ((), ()))
-VMEM_LIMIT = 60 << 20
+VMEM_LIMIT = 63 << 20
 LINK_COST = pl.CostEstimate(flops=60 * 10**9, bytes_accessed=8 << 20, transcendentals=0)
 
 
@@ -147,12 +147,19 @@
             part_outs = [outs.pop(0) for _ in part.outs]
             part_buffers = [buffers.pop(0) for _ in part.scratch]
             running.append(part.run(place, *part_ins, *part_outs, *part_buffers))
-        while running:
-            for part in list(running):
-                try:
-                    next(part)
-                except StopIteration:
-                    running.remove(part)
+        late = [
+            run for run, part in zip(running, parts, strict=True) if isinstance(part, ExpertScatter)
+        ]
+        first = [run for run in running if run not in late]
+        for run in late:
+            next(run)
+        for index, _ in enumerate(together(*first)):
+            if index in (1, 2):
+                for run in late:
+                    next(run)
+        for run in late:
+            for _ in run:
+                pass
 
     results = pl.pallas_call(
         kernel,
@@ -170,6 +177,296 @@
     return [[results.pop(0) for _ in part.outs] for part in parts]
 
 
+END = object()
+
+
+def together(*runs):
+    runs = list(runs)
+    while runs:
+        for run in list(runs):
+            if next(run, END) is END:
+                runs.remove(run)
+        yield
+
+
+def until(run, token):
+    for value in run:
+        if value == token:
+            return
+        yield
+
+
+def gather_scratch(pieces, deep, wide):
+    return [
+        dma(pieces, 2, deep - 1),
+        dma(pieces, 2, deep - 1),
+        dma(pieces, 2 * deep, wide - 1),
+        dma(pieces, 2 * deep, wide - 1),
+        dma(1),
+    ]
+
+
+def start_all(copies):
+    for copy in copies:
+        copy.start()
+
+
+def end_all(copies):
+    for copy in copies:
+        copy.wait_send()
+
+
+def gather_steps(place, own, whole, row_send, row_recv, col_send, col_recv, local):
+    pieces, rows, _ = own.shape
+    deep, wide, shards = place.deep, place.wide, place.shards
+    row, column = place.row, place.column
+    ends = []
+
+    def slot(piece, source_row, source_column):
+        source = piece * shards + source_row * wide + source_column
+        return whole.at[pl.ds(pl.multiple_of(source * rows, rows), rows)]
+
+    def known(piece, step, source_row):
+        return slot(piece, source_row, column) if step else own.at[piece]
+
+    def hop(piece, way, step, source_row):
+        return send_to(
+            (place.group, (row + 1 - 2 * way) * wide + column),
+            known(piece, step, source_row),
+            slot(piece, source_row, column),
+            row_send.at[piece, way, step],
+            row_recv.at[piece, way, step],
+        )
+
+    def across(piece, step, way, move, source_row, source_column):
+        key = 2 * step - 1 + way if step else 0
+        return send_to(
+            place.peer(0, 0, 0, move),
+            known(piece, step, source_row),
+            slot(piece, source_row, source_column),
+            col_send.at[piece, key, move - 1],
+            col_recv.at[piece, key, move - 1],
+        )
+
+    def start_if(condition, copies):
+        pl.when(condition)(functools.partial(start_all, copies))
+        ends.append((condition, copies))
+
+    def forward(piece, step, way, condition, source_row):
+        start_if(
+            condition,
+            [across(piece, step, way, move, source_row, column) for move in range(1, wide)],
+        )
+
+    def begin(piece):
+        start_if(row < deep - 1, [hop(piece, 0, 0, row)])
+        start_if(row > 0, [hop(piece, 1, 0, row)])
+        forward(piece, 0, 0, row >= 0, row)
+
+    here = [
+        pltpu.make_async_copy(own.at[piece], slot(piece, row, column), local.at[0])
+        for piece in range(pieces)
+    ]
+    begin(0)
+    for copy in here:
+        copy.start()
+    yield 0
+    for piece in range(pieces):
+        sources = []
+        for step in range(1, deep):
+            for way in (0, 1):
+                source_row = row - step if way == 0 else row + step
+                there = source_row >= 0 if way == 0 else source_row < deep
+                onward = row < deep - 1 if way == 0 else row > 0
+                pl.when(there)(hop(piece, way, step - 1, source_row).wait_recv)
+                if step < deep - 1:
+                    start_if(there & onward, [hop(piece, way, step, source_row)])
+                forward(piece, step, way, there, source_row)
+                sources.append((step, way, there, source_row))
+            if step == 1 and piece + 1 < pieces:
+                begin(piece + 1)
+            yield 0
+        for step, way, there, source_row in [(0, 0, row >= 0, row)] + sources:
+            for move in range(1, wide):
+                source_column = lax.rem(column + wide - move, wide)
+                copy = across(piece, step, way, move, source_row, source_column)
+                pl.when(there)(copy.wait_recv)
+            if way or not step:
+                yield 0
+        if piece == 0:
+            for copy in here:
+                copy.wait()
+        yield piece + 1
+    for condition, copies in ends:
+        pl.when(condition)(functools.partial(end_all, copies))
+
+
+class Gather:
+    def __init__(self, own, layout):
+        _, deep, wide = layout
+        pieces, rows, width = own.shape
+        self.operands, self.in_specs = [own], [ANYWHERE]
+        self.outs = [jax.ShapeDtypeStruct((pieces * deep * wide * rows, width), own.dtype)]
+        self.out_specs = [ANYWHERE]
+        self.scratch = gather_scratch(pieces, deep, wide)
+        self.steps = grid_steps(deep, wide)
+        self.run = gather_steps
+
+
+def scatter_scratch(rows, width, deep, wide):
+    return [
+        pltpu.VMEM((deep, max(1, wide - 1), rows, width), BF16),
+        pltpu.VMEM((deep + 1, rows, width), BF16),
+        dma(2 * deep, wide - 1),
+        dma(2 * deep, wide - 1),
+        dma(2 * deep),
+        dma(2 * deep),
+    ]
+
+
+def scatter_steps(
+    place, parts, piece, total, landed, summed, col_send, col_recv, row_send, row_recv
+):
+    deep, wide, shards = place.deep, place.wide, place.shards
+    row, column = place.row, place.column
+    rows = total.shape[0]
+    ends = []
+
+    def block(target_row, target_column):
+        target = piece * shards + target_row * wide + target_column
+        return pl.ds(pl.multiple_of(target * rows, rows), rows)
+
+    def along_row(key, target_row, move):
+        target_column = lax.rem(column + move, wide)
+        return send_to(
+            place.peer(0, 0, 0, move),
+            parts.at[block(target_row, target_column)],
+            landed.at[target_row, move - 1],
+            col_send.at[key, move - 1],
+            col_recv.at[key, move - 1],
+        )
+
+    def hop(key, step, way, target_row):
+        return send_to(
+            (place.group, (row + 1 - 2 * way) * wide + column),
+            landed.at[target_row, 0],
+            summed.at[deep if step == 1 and way else target_row],
+            row_send.at[key],
+            row_recv.at[key],
+        )
+
+    order = []
+    for step in range(deep - 1, 0, -1):
+        for way in (0, 1):
+            target_row = row - step if way else row + step
+            there = target_row >= 0 if way else target_row < deep
+            order.append((2 * step + way, step, way, target_row, there))
+    order.append((0, 0, 0, row, row >= 0))
+
+    def send_row(index):
+        key, _, _, target_row, there = order[index]
+        copies = [along_row(key, target_row, move) for move in range(1, wide)]
+        pl.when(there)(functools.partial(start_all, copies))
+        ends.append((there, copies))
+
+    def fold(index):
+        key, step, way, target_row, there = order[index]
+
+        def body():
+            for move in range(1, wide):
+                along_row(key, target_row, move).wait_recv()
+            value = parts[block(target_row, column), :].astype(F32)
+            for move in range(1, wide):
+                value = value + landed[target_row, move - 1].astype(F32)
+            if step:
+                landed[target_row, 0] = value.astype(BF16)
+            else:
+                total[...] = value
+
+        pl.when(there)(body)
+
+    def join(index):
+        key, step, way, target_row, there = order[index]
+        behind = row < deep - 1 if way else row > 0
+
+        def body():
+            hop(key + 2, step + 1, way, target_row).wait_recv()
+            landed[target_row, 0] = (
+                landed[target_row, 0].astype(F32) + summed[target_row].astype(F32)
+            ).astype(BF16)
+
+        if step < deep - 1:
+            pl.when(there & behind)(body)
+        copy = hop(key, step, way, target_row)
+        pl.when(there)(copy.start)
+        ends.append((there, [copy]))
+
+    def finish(way):
+        def body():
+            hop(2 + way, 1, way, row).wait_recv()
+            total[...] = total[...] + summed[deep if way else row].astype(F32)
+
+        pl.when(row < deep - 1 if way else row > 0)(body)
+
+    ahead = 4
+    for index in range(min(ahead, len(order))):
+        send_row(index)
+    yield
+    for index in range(len(order)):
+        fold(index)
+        if index + ahead < len(order):
+            send_row(index + ahead)
+        if index < len(order) - 1:
+            join(index)
+        if index % 2:
+            yield
+    yield
+    for way in (0, 1):
+        finish(way)
+        yield
+    for there, copies in ends:
+        pl.when(there)(functools.partial(end_all, copies))
+
+
+def scatter_pieces(runs, deep):
+    running = []
+    for run in runs:
+        running.append(run)
+        for _ in range(deep + 1):
+            for each in list(running):
+                if next(each, END) is END:
+                    running.remove(each)
+            yield
+    yield from together(*running)
+
+
+class Scatter:
+    def __init__(self, parts, pieces, layout):
+        _, deep, wide = layout
+        tokens, width = parts.shape
+        rows = tokens // (pieces * deep * wide)
+        self.pieces = pieces
+        self.operands, self.in_specs = [parts], [RESIDENT]
+        self.outs = [jax.ShapeDtypeStruct((pieces, rows, width), F32)]
+        self.out_specs = [RESIDENT]
+        self.scratch = scatter_scratch(rows, width, deep, wide) * pieces
+        self.steps = grid_steps(deep, wide)
+
+    def run(self, place, parts, total, *scratch):
+        each = len(scratch) // self.pieces
+        runs = [
+            scatter_steps(
+                place,
+                parts,
+                piece,
+                total.at[piece],
+                *scratch[piece * each : (piece + 1) * each],
+            )
+            for piece in range(self.pieces)
+        ]
+        yield from scatter_pieces(runs, place.deep)
+
+
 class Chain:
     def __init__(self, *parts):
         self.parts = parts
@@ -185,146 +482,6 @@
                 own.extend(refs.pop(0) for _ in getattr(part, name))
         for part, own in zip(self.parts, taken, strict=True):
             yield from part.run(place, *own)
-
-
-class Gather:
-    def __init__(self, own, layout):
-        _, deep, wide = layout
-        pieces, rows, width = own.shape
-        self.operands, self.in_specs = [own], [ANYWHERE]
-        self.outs = [jax.ShapeDtypeStruct((pieces, deep * wide, rows, width), own.dtype)]
-        self.out_specs = [ANYWHERE]
-        self.scratch = [
-            dma(pieces, deep - 1),
-            dma(pieces, deep - 1),
-            dma(pieces, deep, wide - 1),
-            dma(pieces, deep, wide - 1),
-            dma(1),
-        ]
-        self.steps = grid_steps(deep, wide)
-
-    def run(self, place, own, whole, row_send, row_recv, col_send, col_recv, local):
-        pieces, deep, wide = own.shape[0], place.deep, place.wide
-        here = pltpu.make_async_copy(own, whole.at[:, place.me], local.at[0])
-        here.start()
-        sends = []
-
-        def along_column(piece, step):
-            return send_to(
-                place.peer(0, 0, step, 0),
-                own.at[piece],
-                whole.at[piece, place.me],
-                row_send.at[piece, step - 1],
-                row_recv.at[piece, step - 1],
-            )
-
-        def along_row(piece, turn, step, block, source):
-            return send_to(
-                place.peer(0, 0, 0, step),
-                block,
-                whole.at[piece, source],
-                col_send.at[piece, turn, step - 1],
-                col_recv.at[piece, turn, step - 1],
-            )
-
-        def forward(piece, turn, block, source):
-            for step in range(1, wide):
-                sends.append(along_row(piece, turn, step, block, source))
-                sends[-1].start()
-
-        for piece in range(pieces):
-            for step in range(1, deep):
-                sends.append(along_column(piece, step))
-                sends[-1].start()
-            forward(piece, 0, own.at[piece], place.me)
-        yield
-        for piece in range(pieces):
-            for step in range(1, deep):
-                source = place.grid_place(deep - step, 0)
-                along_column(piece, step).wait_recv()
-                forward(piece, step, whole.at[piece, source], source)
-                yield
-        for piece in range(pieces):
-            for turn in range(deep):
-                for step in range(1, wide):
-                    source = place.grid_place(deep - turn, wide - step)
-                    along_row(piece, turn, step, own.at[piece], source).wait_recv()
-                yield
-        for copy in sends:
-            copy.wait_send()
-        here.wait()
-
-
-class Scatter:
-    def __init__(self, parts, layout):
-        _, deep, wide = layout
-        pieces, _, rows, width = parts.shape
-        self.operands, self.in_specs = [parts], [RESIDENT]
-        self.outs = [jax.ShapeDtypeStruct((pieces, rows, width), F32)]
-        self.out_specs = [RESIDENT]
-        self.scratch = [
-            pltpu.VMEM((pieces, deep, max(1, wide - 1), rows, width), BF16),
-            pltpu.VMEM((pieces, deep - 1, rows, width), BF16),
-            pltpu.VMEM((pieces, deep - 1, rows, width), BF16),
-            dma(pieces, deep, wide - 1),
-            dma(pieces, deep, wide - 1),
-            dma(pieces, deep - 1),
-            dma(pieces, deep - 1),
-        ]
-        self.steps = grid_steps(deep, wide)
-
-    def run(
-        self, place, parts, total, landed, merged, summed, col_send, col_recv, row_send, row_recv
-    ):
-        pieces, deep, wide = parts.shape[0], place.deep, place.wide
-        sends = []
-
-        def along_row(piece, turn, step):
-            return send_to(
-                place.peer(0, 0, 0, step),
-                parts.at[piece, place.grid_place(turn + 1, step)],
-                landed.at[piece, turn, step - 1],
-                col_send.at[piece, turn, step - 1],
-                col_recv.at[piece, turn, step - 1],
-            )
-
-        def along_column(piece, turn):
-            return send_to(
-                place.peer(0, 0, turn + 1, 0),
-                merged.at[piece, turn],
-                summed.at[piece, turn],
-                row_send.at[piece, turn],
-                row_recv.at[piece, turn],
-            )
-
-        for piece in range(pieces):
-            for turn in range(deep):
-                for step in range(1, wide):
-                    sends.append(along_row(piece, turn, step))
-                    sends[-1].start()
-        yield
-        for piece in range(pieces):
-            for turn in range(deep):
-                value = parts[piece, place.grid_place((turn + 1) % deep, 0)].astype(F32)
-                for step in range(1, wide):
-                    along_row(piece, turn, step).wait_recv()
-                    value = value + landed[piece, turn, step - 1].astype(F32)
-                if turn < deep - 1:
-                    merged[piece, turn] = value.astype(BF16)
-                    sends.append(along_column(piece, turn))
-                    sends[-1].start()
-                else:
-                    total[piece] = value
-                yield
-        for piece in range(pieces):
-            value = total[piece]
-            for turn in range(deep - 1):
-                along_column(piece, turn).wait_recv()
-                value = value + summed[piece, turn].astype(F32)
-            total[piece] = value
-            yield
-        for copy in sends:
-            copy.wait_send()
 
 
 class ExpertScatter:
@@ -439,165 +596,275 @@
             copy.wait_send()
 
 
-class ExpertWeights:
+class Experts:
     SPAN = 256
 
-    def __init__(self, rows, upstream, hidden, gate_pre, up_pre, down_all, layout):
-        tokens, width = rows.shape
-        halves, _, units = hidden.shape
-        self.terms = jax.ShapeDtypeStruct((halves, width, units), BF16)
-        self.inner = ExpertScatter(self.terms, layout)
-        self.operands = [rows, upstream, hidden, gate_pre, up_pre, down_all]
-        self.in_specs = [RESIDENT] * 5 + [ANYWHERE]
+    def __init__(self, own, upstream, mask, router, gate_all, up_all, down_all, layout):
+        _, deep, wide = layout
+        pieces, rows, width = own.shape
+        halves, _, units = gate_all.shape
+        tokens, lanes = mask.shape
+        self.operands = [own, upstream, mask, router, gate_all, up_all, down_all]
+        self.in_specs = [ANYWHERE, ANYWHERE, RESIDENT, RESIDENT] + [ANYWHERE] * 3
         self.outs = [
-            self.terms,
-            self.terms,
+            jax.ShapeDtypeStruct((halves, width, units), BF16),
+            jax.ShapeDtypeStruct((halves, width, units), BF16),
             jax.ShapeDtypeStruct((halves, units, width), BF16),
             jax.ShapeDtypeStruct((tokens, width), BF16),
-            *self.inner.outs,
+            jax.ShapeDtypeStruct((tokens, lanes), F32),
+            jax.ShapeDtypeStruct((pieces, rows, width), F32),
+            jax.ShapeDtypeStruct((pieces, rows, lanes), F32),
         ]
-        self.out_specs = [ANYWHERE] * 3 + [RESIDENT] * 2
+        self.out_specs = [ANYWHERE] * 4 + [RESIDENT] * 3
+        gathers = gather_scratch(pieces, deep, wide)
+        scatters = scatter_scratch(rows, width, deep, wide)
+        dots = scatter_scratch(rows, lanes, deep, wide)
+        self.sizes = [len(gathers), len(scatters)]
+        acts = pltpu.VMEM((halves, tokens, units), BF16)
         self.scratch = [
-            pltpu.VMEM((2, width, units), BF16),
-            pltpu.VMEM((units, width), BF16),
-            pltpu.VMEM((2, halves, units, self.SPAN), BF16),
+            pltpu.VMEM((tokens, width), BF16),
+            pltpu.VMEM((tokens, width), BF16),
+            acts,
+            acts,
+            acts,
+            pltpu.VMEM((halves, width, units), BF16),
+            pltpu.VMEM((halves, width, units), BF16),
+            pltpu.VMEM((halves, units, width), BF16),
+            pltpu.VMEM((tokens, width), BF16),
+            pltpu.VMEM((tokens, lanes), F32),
+            pltpu.VMEM((tokens, lanes), BF16),
+            dma(3, halves),
+            dma(3, halves),
             dma(2),
-            dma(1),
-            dma(2),
-            *self.inner.scratch,
+            *gathers,
+            *scatters * pieces,
+            *dots * pieces,
         ]
-        self.steps = self.inner.steps
+        self.steps = grid_steps(deep, wide)
 
     def run(
         self,
         place,
+        own,
+        upstream_in,
+        mask,
+        router,
+        gate_all,
+        up_all,
+        down_all,
+        gate_terms,
+        up_terms,
+        down_terms,
+        out,
+        share,
+        total,
+        dot_total,
         rows,
         upstream,
         hidden,
         gate_pre,
         up_pre,
-        down_all,
-        gate_terms,
-        up_terms,
-        down_terms,
-        out,
-        gate_total,
-        stage,
-        stage_down,
-        tiles,
-        stage_sem,
-        stage_down_sem,
-        tile_sem,
-        *inner_scratch,
+        gate_weight,
+        up_weight,
+        down_weight,
+        parts,
+        dots,
+        placed,
+        load_sem,
+        store_sem,
+        local_sem,
+        *scratch,
     ):
+        pieces = own.shape[0]
         halves, _, units = hidden.shape
-        width = rows.shape[1]
+        tokens, width = rows.shape
+        lanes = mask.shape[1]
+        count = tokens // pieces
         span = self.SPAN
-        state = {"slot": 0, "busy": [None, None], "down": None}
-
-        def columns(grads, target):
+        shards = place.shards
+        scratch = list(scratch)
+
+        def take(number):
+            return [scratch.pop(0) for _ in range(number)]
+
+        inward = gather_steps(place, own, rows, *take(self.sizes[0]))
+        scatters = [
+            scatter_steps(place, parts, piece, total.at[piece], *take(self.sizes[1]))
+            for piece in range(pieces)
+        ]
+        dot_scatters = [
+            scatter_steps(place, placed, piece, dot_total.at[piece], *take(self.sizes[1]))
+            for piece in range(pieces)
+        ]
+        running = []
+
+        def others():
+            for each in list(running):
+                if next(each, END) is END:
+                    running.remove(each)
+
+        kept = (gate_weight, up_weight, down_weight)
+
+        def load(half):
+            return [
+                pltpu.make_async_copy(source.at[half], kept[which].at[half], load_sem.at[which, half])
+                for which, source in enumerate((gate_all, up_all, down_all))
+            ]
+
+        def store(which, half):
+            target = (gate_terms, up_terms, down_terms)[which]
+            return pltpu.make_async_copy(
+                kept[which].at[half], target.at[half], store_sem.at[which, half]
+            )
+
+        def wait_all(copies):
+            for copy in copies:
+                copy.wait()
+
+        def shares(piece):
+            here = pl.ds(piece * count, count)
+            known = mask[here, :]
+            logits = dot(rows[here, :], router[...], NN)
+            peak = jnp.max(jnp.where(known > 0, logits, MASK_FILL), axis=1, keepdims=True)
+            exponent = jnp.where(known > 0, jnp.exp(jnp.minimum(logits - peak, 0.0)), 0.0)
+            share[here, :] = exponent / jnp.sum(exponent, axis=1, keepdims=True)
+
+        def units_of(piece):
+            here = pl.ds(piece * count, count)
+            which_lane = lax.broadcasted_iota(jnp.int32, (count, lanes), 1)
             for half in range(halves):
-                slot = state["slot"]
-                if state["busy"][slot] is not None:
-                    state["busy"][slot].wait()
+                if piece == 0:
+                    wait_all(load(half))
+                column = half * shards + place.me
+                chosen = jnp.where(which_lane == column // 2, share[here, :], 0.0)
+                weight = jnp.sum(chosen, axis=1, keepdims=True)
                 for step in range(units // span):
-                    here = pl.ds(step * span, span)
-                    stage[slot, :, here] = dot(rows[...], grads[half, :, here], TN).astype(BF16)
-                    if step < units // span - 1:
+                    there = pl.ds(step * span, span)
+                    gate = dot(rows[here, :], gate_weight[half, :, there], NN)
+                    up = dot(rows[here, :], up_weight[half, :, there], NN)
+                    grad = dot(upstream[here, :], down_weight[half, there, :], NT)
+                    sigmoid_gate = 1.0 / (1.0 + jnp.exp(-gate))
+                    swish_gate = gate * sigmoid_gate
+                    activated = swish_gate * up
+                    products = jnp.sum(activated * grad, axis=1, keepdims=True)
+                    dots[here, :] += jnp.where(which_lane == column, products, 0.0)
+                    hidden[half, here, there] = (activated * weight).astype(BF16)
+                    grad = grad * weight
+                    gate_pre[half, here, there] = (
+                        grad * up * (sigmoid_gate * (1.0 + gate * (1.0 - sigmoid_gate)))
+                    ).astype(BF16)
+                    up_pre[half, here, there] = (grad * swish_gate).astype(BF16)
+                    yield
+
+        def merge(piece):
+            here = pl.ds(piece * count, count)
+            for step in range(width // span):
+                there = pl.ds(step * span, span)
+                value = dot(gate_pre[0, here, :], gate_weight[0, there, :], NT)
+                value = value + dot(up_pre[0, here, :], up_weight[0, there, :], NT)
+                for half in range(1, halves):
+                    value = value + dot(gate_pre[half, here, :], gate_weight[half, there, :], NT)
+                    value = value + dot(up_pre[half, here, :], up_weight[half, there, :], NT)
+                parts[here, there] = value.astype(BF16)
+                yield
+
+        def place_dots(piece):
+            here = pl.ds(piece * count, count)
+            value = dots[here, :]
+            high = value.astype(BF16).astype(F32)
+            low = pltpu.roll(value - high, lanes // 2, 1)
+            placed[here, :] = (high + low).astype(BF16)
+
+        def weights():
+            ends = []
+
+            def put(copy):
+                copy.start()
+                ends.append(copy)
+
+            for which, grads in enumerate((gate_pre, up_pre)):
+                for half in range(halves):
+                    for step in range(units // span):
+                        there = pl.ds(step * span, span)
+                        kept[which][half, :, there] = dot(
+                            rows[...], grads[half, :, there], TN
+                        ).astype(BF16)
                         yield
-                copy = pltpu.make_async_copy(stage.at[slot], target.at[half], stage_sem.at[slot])
-                copy.start()
-                state["busy"][slot] = copy
-                state["slot"] = 1 - slot
+                    put(store(which, half))
+            for step in range(width // span):
+                there = pl.ds(step * span, span)
+                value = dot(hidden[0], down_weight[0, :, there], NN)
+                for half in range(1, halves):
+                    value = value + dot(hidden[half], down_weight[half, :, there], NN)
+                rows[:, there] = value.astype(BF16)
                 yield
-
-        def drain():
-            for slot in (0, 1):
-                if state["busy"][slot] is not None:
-                    state["busy"][slot].wait()
-                    state["busy"][slot] = None
-
-        def downs():
-            copy = None
+            put(pltpu.make_async_copy(rows, out, local_sem.at[1]))
             for half in range(halves):
-                if copy is not None:
-                    copy.wait()
                 for step in range(units // span):
-                    here = pl.ds(step * span, span)
-                    stage_down[here, :] = dot(hidden[half, :, here], upstream[...], TN).astype(
-                        BF16
-                    )
-                    if step < units // span - 1:
-                        yield
-                copy = pltpu.make_async_copy(
-                    stage_down, down_terms.at[half], stage_down_sem.at[0]
-                )
-                copy.start()
+                    there = pl.ds(step * span, span)
+                    down_weight[half, there, :] = dot(
+                        hidden[half, :, there], upstream[...], TN
+                    ).astype(BF16)
+                    yield
+                put(store(2, half))
+            wait_all(ends)
+
+        next(inward)
+        upstream_copy = pltpu.make_async_copy(upstream_in, upstream, local_sem.at[0])
+        upstream_copy.start()
+        for half in range(halves):
+            start_all(load(half))
+        dots[...] = jnp.zeros_like(dots)
+        yield from until(inward, 1)
+        upstream_copy.wait()
+        running.append(inward)
+        for piece in range(pieces):
+            if piece:
+                while inward in running:
+                    others()
+                    yield
+            shares(piece)
+            for index, _ in enumerate(units_of(piece)):
+                if piece == 0 or index % 2:
+                    others()
                 yield
-            copy.wait()
-
-        def tile(step):
-            return pltpu.make_async_copy(
-                down_all.at[:, :, pl.ds(step * span, span)],
-                tiles.at[step % 2],
-                tile_sem.at[step % 2],
-            )
-
-        def outputs():
-            for step in range(width // span):
-                if step + 1 < width // span:
-                    tile(step + 1).start()
-                tile(step).wait()
-                value = dot(hidden[0], tiles[step % 2, 0], NN)
-                for half in range(1, halves):
-                    value = value + dot(hidden[half], tiles[step % 2, half], NN)
-                out[:, pl.ds(step * span, span)] = value.astype(BF16)
+            place_dots(piece)
+            running.append(dot_scatters[piece])
+            next(dot_scatters[piece])
+            for index, _ in enumerate(merge(piece)):
+                if piece == 0 or index % 4 == 3:
+                    others()
                 yield
-
-        def rest():
-            yield from columns(up_pre, up_terms)
-            yield from downs()
-            yield from outputs()
-            drain()
-
-        tile(0).start()
-        for index, _ in enumerate(columns(gate_pre, gate_terms)):
+            running.append(scatters[piece])
+            next(scatters[piece])
+        for index, _ in enumerate(weights()):
             if index % 4 == 3:
+                others()
                 yield
-        drain()
-        inner = self.inner.run(place, gate_terms, gate_total, *inner_scratch)
-        next(inner)
-        others = rest()
-        waiting, working = True, True
-        while waiting or working:
-            for _ in range(4):
-                working = working and next(others, "end") != "end"
-            if waiting:
-                waiting = next(inner, "end") != "end"
-            yield
+        yield from together(*running)
 
 
 class Columns:
-    def __init__(self, weights, small, layout):
+    def __init__(self, weights, smalls, layout):
         groups, deep, wide = layout
         shards = deep * wide
         depth = weights[0].shape[0]
-        self.operands, self.in_specs = [*weights, small], [ANYWHERE] * 4
+        self.operands, self.in_specs = [*weights, *smalls], [ANYWHERE] * 5
         self.outs = [
             jax.ShapeDtypeStruct((shards, groups, depth // groups, 3 * depth), BF16),
-            jax.ShapeDtypeStruct((shards,) + small.shape, BF16),
+            *[jax.ShapeDtypeStruct((shards,) + small.shape, BF16) for small in smalls],
         ]
-        self.out_specs = [ANYWHERE] * 2
+        self.out_specs = [ANYWHERE] * 3
         self.scratch = [
             dma(3, shards - 1),
             dma(3, shards - 1),
-            dma(shards - 1),
-            dma(shards - 1),
+            dma(2, shards - 1),
+            dma(2, shards - 1),
             dma(groups // 2 - 1),
             dma(groups // 2 - 1),
             dma(groups // 2),
             dma(groups // 2),
-            dma(4),
+            dma(5),
         ]
         self.steps = shard_steps(deep, wide) | expert_steps(groups // 2)
 
@@ -608,8 +875,10 @@
         key_weight,
         value_weight,
         small,
+        gains,
         projections,
         small_all,
+        gains_all,
         weight_send,
         weight_recv,
         small_send,
@@ -621,6 +890,7 @@
         local,
     ):
         weights = (query_weight, key_weight, value_weight)
+        smalls = ((small, small_all), (gains, gains_all))
         layers, group, me = place.layers, place.group, place.me
         part = projections.shape[2]
         depth = query_weight.shape[0]
@@ -645,13 +915,13 @@
                 weight_recv.at[which, index],
             )
 
-        def small_copy(index):
+        def small_copy(which, index):
             return send_to(
                 place.peer(*steps[index]),
-                small,
-                small_all.at[me],
-                small_send.at[index],
-                small_recv.at[index],
+                smalls[which][0],
+                smalls[which][1].at[me],
+                small_send.at[which, index],
+                small_recv.at[which, index],
             )
 
         def slab_copy(peer, layer, core, send_sem, recv_sem):
@@ -676,15 +946,17 @@
             pltpu.make_async_copy(block(which, me), slot(which, me), local.at[which])
             for which in range(3)
         ]
-        here.append(pltpu.make_async_copy(small, small_all.at[me], local.at[3]))
+        for which, (own, whole) in enumerate(smalls):
+            here.append(pltpu.make_async_copy(own, whole.at[me], local.at[3 + which]))
         for copy in here:
             copy.start()
         for index in range(len(steps)):
             for which in range(3):
                 sends.append(weight_copy(which, index))
                 sends[-1].start()
-            sends.append(small_copy(index))
-            sends[-1].start()
+            for which in (0, 1):
+                sends.append(small_copy(which, index))
+                sends[-1].start()
         yield
         for copy in here:
             copy.wait()
@@ -708,7 +980,8 @@
             core_copy(step, layer, 1 - place.core).wait_recv()
             yield
         for index in range(len(steps)):
-            small_copy(index).wait_recv()
+            for which in (0, 1):
+                small_copy(which, index).wait_recv()
         for copy in sends:
             copy.wait_send()
 
@@ -987,6 +1260,7 @@
 
 
 def forward_steps(
+    micro,
     hidden,
     projections,
     output_weight,
@@ -1001,38 +1275,35 @@
     attended,
     parts,
 ):
-    micros, span = seg_column.shape[0], seg_column.shape[1]
-    heads = output_weight.shape[0] // HDIM
+    span = seg_column.shape[1]
+    depth = projections.shape[1] // 3
+    heads = depth // HDIM
     tile = min(span, 256)
-    for micro in range(micros):
-        for start in range(0, span, tile):
-            rows = pl.ds(micro * span + start, tile)
-            values = hidden[rows, :].astype(F32)
-            mixer[rows, :] = (values * rms_scale(values) * gain[...]).astype(BF16)
-        rows = pl.ds(micro * span, span)
-        projected[rows, :] = dot(mixer[rows, :], projections[...], NN)
+    rows = pl.ds(micro * span, span)
+    for start in range(0, span, tile):
+        here = pl.ds(micro * span + start, tile)
+        values = hidden[here, :].astype(F32)
+        mixer[here, :] = (values * rms_scale(values) * gain).astype(BF16)
+    projected[rows, :] = dot(mixer[rows, :], projections[...], NN)
+    yield
+    for head in range(heads):
+        own = projected[rows, :]
+        _, _, query_rot = head_forward(own, head, head_gains[0], cosine[...], sine[...])
+        _, _, key_rot = head_forward(own, heads + head, head_gains[1], cosine[...], sine[...])
+        values = own[:, (2 * heads + head) * HDIM : (2 * heads + head + 1) * HDIM]
+        probs = head_probs(query_rot, key_rot, seg_column[micro], seg_row[micro])
+        attended[rows, head * HDIM : (head + 1) * HDIM] = dot(
+            probs.astype(BF16), values.astype(BF16), NN
+        ).astype(BF16)
         yield
-        for head in range(heads):
-            own = projected[rows, :]
-            _, _, query_rot = head_forward(own, head, head_gains[0:1], cosine[...], sine[...])
-            _, _, key_rot = head_forward(
-                own, heads + head, head_gains[1:2], cosine[...], sine[...]
-            )
-            values = own[:, (2 * heads + head) * HDIM : (2 * heads + head + 1) * HDIM]
-            probs = head_probs(query_rot, key_rot, seg_column[micro], seg_row[micro])
-            attended[rows, head * HDIM : (head + 1) * HDIM] = dot(
-                probs.astype(BF16), values.astype(BF16), NN
-            ).astype(BF16)
-            yield
-        parts[rows, :] = dot(attended[rows, :], output_weight[...], NN).astype(BF16)
-        yield
+    parts[rows, :] = dot(attended[rows, :], output_weight[...], NN).astype(BF16)
+    yield
 
 
 def backward_steps(
+    micro,
     branch,
-    mixer,
     projected,
-    attended,
     projections,
     output_weight,
     head_gains,
@@ -1041,108 +1312,209 @@
     seg_column,
     seg_row,
     parts,
-    projection_terms,
-    output_terms,
     gain_terms,
     attended_grad,
     projected_grad,
 ):
-    micros, span = seg_column.shape[0], seg_column.shape[1]
+    span = seg_column.shape[1]
     heads = output_weight.shape[0] // HDIM
     scale = 1.0 / math.sqrt(HDIM)
-    gain_terms[...] = jnp.zeros_like(gain_terms)
-    for micro in range(micros):
-        rows = pl.ds(micro * span, span)
-        attended_grad[rows, :] = dot(branch[rows, :], output_weight[...], NT).astype(BF16)
+    rows = pl.ds(micro * span, span)
+    attended_grad[rows, :] = dot(branch[rows, :], output_weight[...], NT).astype(BF16)
+    yield
+    for head in range(heads):
+        own = projected[rows, :]
+        query_scale, query_unit, query_rot = head_forward(
+            own, head, head_gains[0], cosine[...], sine[...]
+        )
+        key_scale, key_unit, key_rot = head_forward(
+            own, heads + head, head_gains[1], cosine[...], sine[...]
+        )
+        values = own[:, (2 * heads + head) * HDIM : (2 * heads + head + 1) * HDIM]
+        probs = head_probs(query_rot, key_rot, seg_column[micro], seg_row[micro])
+        out_grad = attended_grad[rows, head * HDIM : (head + 1) * HDIM]
+        prob_grad = dot(out_grad, values.astype(BF16), NT)
+        row_delta = jnp.sum(probs * prob_grad, axis=-1, keepdims=True)
+        score_grad = (probs * (prob_grad - row_delta)).astype(BF16)
+        projected_grad[rows, (2 * heads + head) * HDIM : (2 * heads + head + 1) * HDIM] = dot(
+            probs.astype(BF16), out_grad, TN
+        ).astype(BF16)
+        for which, (rot_grad, unit, unit_scale) in enumerate(
+            (
+                (dot(score_grad, key_rot, NN) * scale, query_unit, query_scale),
+                (dot(score_grad, query_rot, TN) * scale, key_unit, key_scale),
+            )
+        ):
+            unit_grad = turn(rot_grad, cosine[...], -sine[...])
+            gain_terms[which : which + 1] += jnp.sum(unit_grad * unit, axis=0, keepdims=True)
+            place = (which * heads + head) * HDIM
+            projected_grad[rows, place : place + HDIM] = norm_back(
+                unit_grad * head_gains[which], unit, unit_scale
+            ).astype(BF16)
         yield
-        for head in range(heads):
-            own = projected[rows, :]
-            query_scale, query_unit, query_rot = head_forward(
-                own, head, head_gains[0:1], cosine[...], sine[...]
-            )
-            key_scale, key_unit, key_rot = head_forward(
-                own, heads + head, head_gains[1:2], cosine[...], sine[...]
-            )
-            values = own[:, (2 * heads + head) * HDIM : (2 * heads + head + 1) * HDIM]
-            probs = head_probs(query_rot, key_rot, seg_column[micro], seg_row[micro])
-            out_grad = attended_grad[rows, head * HDIM : (head + 1) * HDIM]
-            prob_grad = dot(out_grad, values.astype(BF16), NT)
-            row_delta = jnp.sum(probs * prob_grad, axis=-1, keepdims=True)
-            score_grad = (probs * (prob_grad - row_delta)).astype(BF16)
-            projected_grad[rows, (2 * heads + head) * HDIM : (2 * heads + head + 1) * HDIM] = dot(
-                probs.astype(BF16), out_grad, TN
-            ).astype(BF16)
-            for which, (rot_grad, unit, unit_scale) in enumerate(
-                (
-                    (dot(score_grad, key_rot, NN) * scale, query_unit, query_scale),
-                    (dot(score_grad, query_rot, TN) * scale, key_unit, key_scale),
-                )
-            ):
-                unit_grad = turn(rot_grad, cosine[...], -sine[...])
-                gain_terms[which : which + 1] += jnp.sum(unit_grad * unit, axis=0, keepdims=True)
-                place = (which * heads + head) * HDIM
-                projected_grad[rows, place : place + HDIM] = norm_back(
-                    unit_grad * head_gains[which : which + 1], unit, unit_scale
-                ).astype(BF16)
-            yield
-        parts[rows, :] = dot(projected_grad[rows, :], projections[...], NT).astype(BF16)
-        yield
-    tile = min(512, branch.shape[1])
-    for start in range(0, branch.shape[1], tile):
+    parts[rows, :] = dot(projected_grad[rows, :], projections[...], NT).astype(BF16)
+    yield
+
+
+def weight_steps(branch, mixer, attended, projected_grad, projection_terms, output_terms):
+    width = branch.shape[1]
+    tile = min(512, width)
+    for start in range(0, width, tile):
         here = pl.ds(start, tile)
         output_terms[:, here] = dot(attended[...], branch[:, here], TN).astype(BF16)
         projection_terms[here, :] = dot(mixer[:, here], projected_grad[...], TN).astype(BF16)
         yield
 
 
-def whole_kernel(steps):
-    def kernel(*refs):
-        for _ in steps(*refs):
-            pass
-
-    return kernel
-
-
-def attention_forward(hidden, projections, output_weight, gain, head_gains, tables, segments):
-    tokens, width = hidden.shape
-    column_width = output_weight.shape[0]
-    return pl.pallas_call(
-        whole_kernel(forward_steps),
-        in_specs=[RESIDENT] * 9,
-        out_specs=[RESIDENT] * 4,
-        out_shape=[
+class AttentionForward:
+    def __init__(
+        self, weights, smalls, inputs, cotangent, output_weight, tables, segments, layout
+    ):
+        _, deep, wide = layout
+        micros, rows, width = inputs.shape
+        shards = deep * wide
+        tokens = micros * shards * rows
+        depth = output_weight.shape[0]
+        self.columns = Columns(weights, smalls, layout)
+        self.operands = [
+            *self.columns.operands,
+            inputs,
+            cotangent,
+            output_weight,
+            *tables,
+            *segments,
+        ]
+        self.in_specs = [*self.columns.in_specs, ANYWHERE, ANYWHERE, *[RESIDENT] * 5]
+        self.outs = [
+            *self.columns.outs[1:],
+            jax.ShapeDtypeStruct((shards, depth, 3 * depth), BF16),
             jax.ShapeDtypeStruct((tokens, width), BF16),
-            jax.ShapeDtypeStruct((tokens, 3 * column_width), F32),
-            jax.ShapeDtypeStruct((tokens, column_width), BF16),
             jax.ShapeDtypeStruct((tokens, width), BF16),
-        ],
-        compiler_params=pltpu.CompilerParams(vmem_limit_bytes=VMEM_LIMIT),
-        name="attention_forward",
-    )(hidden, projections, output_weight, gain, head_gains, *tables, *segments)
-
-
-def attention_backward(
-    branch, mixer, projected, attended, projections, output_weight, head_gains, tables, segments
-):
-    tokens, width = branch.shape
-    column_width = output_weight.shape[0]
-    return pl.pallas_call(
-        whole_kernel(backward_steps),
-        in_specs=[RESIDENT] * 11,
-        out_specs=[RESIDENT] * 4,
-        out_shape=[
-            jax.ShapeDtypeStruct((tokens, width), BF16),
-            jax.ShapeDtypeStruct((width, 3 * column_width), BF16),
-            jax.ShapeDtypeStruct((column_width, width), BF16),
-            jax.ShapeDtypeStruct((8, HDIM), F32),
-        ],
-        scratch_shapes=[
-            pltpu.VMEM((tokens, column_width), BF16),
-            pltpu.VMEM((tokens, 3 * column_width), BF16),
-        ],
-        compiler_params=pltpu.CompilerParams(vmem_limit_bytes=VMEM_LIMIT),
-        name="attention_backward",
-    )(
+            jax.ShapeDtypeStruct((tokens, 3 * depth), F32),
+            jax.ShapeDtypeStruct((tokens, depth), BF16),
+            jax.ShapeDtypeStruct((micros, rows, width), F32),
+        ]
+        self.out_specs = [ANYWHERE, RESIDENT, RESIDENT, ANYWHERE, *[RESIDENT] * 4]
+        gathers = gather_scratch(micros, deep, wide)
+        scatters = scatter_scratch(rows, width, deep, wide)
+        self.sizes = [len(self.columns.scratch), len(gathers), len(gathers), len(scatters)]
+        columns_out = self.columns.outs[0]
+        self.scratch = [
+            pltpu.VMEM(columns_out.shape, BF16),
+            pltpu.VMEM((tokens, width), BF16),
+            pltpu.VMEM((tokens, width), BF16),
+            pltpu.VMEM((1, width), F32),
+            *self.columns.scratch,
+            *gathers,
+            *gathers,
+            *scatters * micros,
+        ]
+        self.steps = self.columns.steps | grid_steps(deep, wide)
+
+    def run(
+        self,
+        place,
+        query_weight,
+        key_weight,
+        value_weight,
+        small,
+        gains,
+        inputs,
+        cotangent,
+        output_weight,
+        cosine,
+        sine,
+        seg_column,
+        seg_row,
+        small_all,
+        gains_all,
+        projections,
+        upstream,
+        mixer,
+        projected,
+        attended,
+        total,
+        swapped,
+        hidden,
+        parts,
+        gain,
+        *scratch,
+    ):
+        micros, shards, deep = inputs.shape[0], place.shards, place.deep
+        scratch = list(scratch)
+
+        def take(count):
+            return [scratch.pop(0) for _ in range(count)]
+
+        columns = self.columns.run(
+            place,
+            query_weight,
+            key_weight,
+            value_weight,
+            small,
+            gains,
+            swapped,
+            small_all,
+            gains_all,
+            *take(self.sizes[0]),
+        )
+        inward = gather_steps(place, inputs, hidden, *take(self.sizes[1]))
+        upward = gather_steps(place, cotangent, upstream, *take(self.sizes[2]))
+        scatters = [
+            scatter_steps(place, parts, micro, total.at[micro], *take(self.sizes[3]))
+            for micro in range(micros)
+        ]
+        next(columns)
+        next(inward)
+        next(columns)
+        yield from until(inward, 1)
+        yield from columns
+        part, depth = swapped.shape[2], output_weight.shape[0]
+        head_gains = jnp.zeros((1, 2 * HDIM), F32)
+        for shard in range(shards):
+            for group in range(place.groups):
+                projections[shard, group * part : (group + 1) * part, :] = swapped[shard, group]
+            known = gains_all[shard].astype(F32)
+            gain[:, shard * depth : (shard + 1) * depth] = known[0:1, :depth]
+            head_gains = head_gains + known[1:2, : 2 * HDIM]
+        head_gains = (head_gains[:, :HDIM], head_gains[:, HDIM:])
+        weight = projections[...].reshape(-1, projections.shape[2])
+        running = []
+        for micro in range(micros):
+            for _ in forward_steps(
+                micro,
+                hidden,
+                weight,
+                output_weight,
+                gain[...],
+                head_gains,
+                cosine,
+                sine,
+                seg_column,
+                seg_row,
+                mixer,
+                projected,
+                attended,
+                parts,
+            ):
+                for each in list(running):
+                    if next(each, END) is END:
+                        running.remove(each)
+                if micro + 1 < micros:
+                    next(inward, END)
+                yield
+            if micro + 1 < micros:
+                yield from until(inward, micro + 2)
+            running.append(scatters[micro])
+            next(scatters[micro])
+        running.append(upward)
+        yield from inward
+        yield from together(*running)
+
+
+class AttentionBackward:
+    def __init__(
+        self,
         branch,
         mixer,
         projected,
@@ -1150,9 +1522,135 @@
         projections,
         output_weight,
         head_gains,
-        *tables,
-        *segments,
-    )
+        tables,
+        segments,
+        beside,
+        layout,
+    ):
+        _, deep, wide = layout
+        micros, rows, width = branch.shape
+        tokens = micros * deep * wide * rows
+        depth = output_weight.shape[0]
+        self.beside = beside
+        self.operands = [
+            branch,
+            mixer,
+            projected,
+            attended,
+            projections,
+            output_weight,
+            head_gains,
+            *tables,
+            *segments,
+            *[operand for part in beside for operand in part.operands],
+        ]
+        self.in_specs = [ANYWHERE] + [RESIDENT] * 10
+        self.in_specs += [spec for part in beside for spec in part.in_specs]
+        self.outs = [
+            jax.ShapeDtypeStruct((width, 3 * depth), BF16),
+            jax.ShapeDtypeStruct((depth, width), BF16),
+            jax.ShapeDtypeStruct((8, HDIM), F32),
+            jax.ShapeDtypeStruct((micros, rows, width), F32),
+            *[out for part in beside for out in part.outs],
+        ]
+        self.out_specs = [RESIDENT] * 4 + [spec for part in beside for spec in part.out_specs]
+        gathers = gather_scratch(micros, deep, wide)
+        scatters = scatter_scratch(rows, width, deep, wide)
+        self.sizes = [len(gathers), len(scatters)]
+        self.scratch = [
+            pltpu.VMEM((tokens, width), BF16),
+            pltpu.VMEM((tokens, width), BF16),
+            pltpu.VMEM((tokens, depth), BF16),
+            pltpu.VMEM((tokens, 3 * depth), BF16),
+            *gathers,
+            *scatters * micros,
+            *[buffer for part in beside for buffer in part.scratch],
+        ]
+        self.steps = grid_steps(deep, wide).union(*(part.steps for part in beside))
+
+    def run(self, place, *refs):
+        refs = list(refs)
+
+        def take(count):
+            return [refs.pop(0) for _ in range(count)]
+
+        (
+            branch,
+            mixer,
+            projected,
+            attended,
+            projections,
+            output_weight,
+            head_gains,
+            cosine,
+            sine,
+            seg_column,
+            seg_row,
+        ) = take(11)
+        beside_in = [take(len(part.operands)) for part in self.beside]
+        projection_terms, output_terms, gain_terms, total = take(4)
+        beside_out = [take(len(part.outs)) for part in self.beside]
+        branch_all, parts, attended_grad, projected_grad = take(4)
+        micros = branch.shape[0]
+        inward = gather_steps(place, branch, branch_all, *take(self.sizes[0]))
+        scatters = [
+            scatter_steps(place, parts, micro, total.at[micro], *take(self.sizes[1]))
+            for micro in range(micros)
+        ]
+        sides = [
+            part.run(place, *own_in, *own_out, *take(len(part.scratch)))
+            for part, own_in, own_out in zip(self.beside, beside_in, beside_out, strict=True)
+        ]
+        next(inward)
+        for side in sides:
+            next(side)
+        gain_terms[...] = jnp.zeros_like(gain_terms)
+        gains = (head_gains[0:1], head_gains[1:2])
+        yield from until(inward, 1)
+        for side in sides[:1]:
+            next(side)
+            next(side)
+        running = []
+        for micro in range(micros):
+            for _ in backward_steps(
+                micro,
+                branch_all,
+                projected,
+                projections,
+                output_weight,
+                gains,
+                cosine,
+                sine,
+                seg_column,
+                seg_row,
+                parts,
+                gain_terms,
+                attended_grad,
+                projected_grad,
+            ):
+                for each in list(running):
+                    if next(each, END) is END:
+                        running.remove(each)
+                if micro + 1 < micros:
+                    next(inward, END)
+                yield
+            running.append(scatters[micro])
+            next(scatters[micro])
+            if micro == 0:
+                for side in sides[1:]:
+                    next(side)
+                    next(side)
+            if micro + 1 < micros:
+                yield from until(inward, micro + 2)
+        running.append(inward)
+        running.append(
+            weight_steps(
+                branch_all, mixer, attended, projected_grad, projection_terms, output_terms
+            )
+        )
+        yield from together(*running)
+        for side in sides:
+            yield from side
 
 
 def units_kernel(
@@ -1339,6 +1837,49 @@
             transcendentals=0,
         ),
     )(rows, upstream, hidden, gate_pre, up_pre)
+
+
+def experts_in_turn(
+    expert_input, upstream_all, choose, router_full, gate_all, up_all, down_all, layout, micros
+):
+    groups, deep, wide = layout
+    shards = deep * wide
+    experts = router_full.shape[1]
+    shard_place = lax.axis_index("shard")
+    ((expert_all,),) = fuse([Gather(expert_input, layout)], layout, 2, "experts_in")
+    logits = jnp.dot(expert_all, router_full, preferred_element_type=F32)
+    share = softmax_rows(jnp.sum(choose * logits[:, None, :], axis=-1))
+    share_wide = jnp.sum(choose * share[:, :, None], axis=1)
+    served = (jnp.arange(groups, dtype=jnp.int32) * shards + shard_place) // 2
+    serves = (served[:, None] == jnp.arange(experts, dtype=jnp.int32)).astype(F32)
+    share_own = jnp.pad(
+        jnp.dot(share_wide, serves.T, precision=PRECISE), ((0, 0), (0, 128 - groups))
+    )
+    activated, gate_pre, up_pre, dots = expert_units(
+        expert_all, upstream_all, share_own, gate_all, up_all, down_all
+    )
+    expert_grad_parts = expert_merge(gate_pre, up_pre, gate_all, up_all)
+    gate_pre, expert_grad_parts = lax.optimization_barrier((gate_pre, expert_grad_parts))
+    gate_terms, up_terms, down_terms = expert_weights(
+        expert_all, upstream_all, activated, gate_pre, up_pre
+    )
+    out_parts = expert_output(activated, down_all)
+
+    halves = groups * shards
+    lanes = halves + -halves % 128
+    columns = jnp.arange(groups, dtype=jnp.int32) * shards + shard_place
+    columns = (columns[:, None] == jnp.arange(lanes, dtype=jnp.int32)).astype(F32)
+    placed = jnp.dot(dots[:, :groups], columns, precision=PRECISE)
+    placed_high = placed.astype(BF16)
+    placed_low = (placed - placed_high.astype(F32)).astype(BF16)
+    placed = jnp.concatenate([placed_high, placed_low], axis=1)
+    (dot_total,), (expert_grad,) = fuse(
+        [Scatter(placed, micros, layout), Scatter(expert_grad_parts, micros, layout)],
+        layout,
+        3,
+        "experts_out",
+    )
+    return gate_terms, up_terms, down_terms, out_parts, share, expert_grad, dot_total, lanes
 
 
 def per_device(
@@ -1375,115 +1916,124 @@
     up_all = lax.all_gather(up_weight, "expert", axis=0, tiled=True)
     down_all = lax.all_gather(down_weight, "expert", axis=0, tiled=True)
 
-    cuts = [
-        column_width * experts,
-        column_width,
-        column_width,
-        HDIM // shards,
-        HDIM // shards,
-        routes.size,
-    ]
-    starts = [sum(cuts[:place]) for place in range(len(cuts))]
+    cuts = [column_width * experts, routes.size]
     small_own = jnp.concatenate(
+        [router_weight.reshape(-1), routes.reshape(-1).astype(BF16)]
+    )
+    small_own = jnp.pad(small_own, (0, -sum(cuts) % 2048)).reshape(-1, 128)
+
+    def placed_row(gain):
+        row = jnp.zeros((gain.shape[0] * shards,), BF16)
+        return lax.dynamic_update_slice_in_dim(row, gain, shard_place * gain.shape[0], 0)
+
+    gains_own = jnp.zeros((16, max(2 * column_width, 2 * HDIM)), BF16)
+    gains_own = gains_own.at[0, : 2 * column_width].set(
+        jnp.concatenate([attention_gain, expert_gain])
+    )
+    gains_own = gains_own.at[1, : 2 * HDIM].set(
+        jnp.concatenate([placed_row(query_gain), placed_row(key_gain)])
+    )
+
+    tables = rotary(span)
+    segments = (segment_ids[:, :, None], segment_ids[:, None, :])
+    (
+        (
+            small,
+            gains_all,
+            projections,
+            upstream_all,
+            mixer_all,
+            projected,
+            attended,
+            middle_total,
+        ),
+    ) = fuse(
         [
-            router_weight.reshape(-1),
-            attention_gain,
-            expert_gain,
-            query_gain,
-            key_gain,
-            routes.reshape(-1).astype(BF16),
-        ]
-    )
-    small_own = jnp.pad(small_own, (0, -sum(cuts) % 2048)).reshape(-1, 128)
-    (projections, small), (hidden_all, upstream_all) = fuse(
-        [
-            Columns((query_weight, key_weight, value_weight), small_own, layout),
-            Chain(Gather(inputs, layout), Gather(cotangent, layout)),
+            AttentionForward(
+                (query_weight, key_weight, value_weight),
+                (small_own, gains_own),
+                inputs,
+                cotangent,
+                output_weight,
+                tables,
+                segments,
+                layout,
+            )
         ],
         layout,
         0,
-        "entry",
-    )
-    hidden_all = hidden_all.reshape(tokens, width)
-    upstream_all = upstream_all.reshape(tokens, width)
+        "attention_forward",
+    )
     projections = projections.reshape(width, 3 * column_width)
     small = small.reshape(shards, -1)
-    router_full, attn_gain, expert_gain_full, query_gain_full, key_gain_full, routes_all = (
-        small[:, start : start + length]
-        for start, length in zip(starts, cuts, strict=True)
-    )
-    router_full = router_full.reshape(width, experts)
-    attn_gain = attn_gain.reshape(-1).astype(F32)
-    expert_gain_full = expert_gain_full.reshape(-1).astype(F32)
-    query_gain_full = query_gain_full.reshape(-1).astype(F32)
-    key_gain_full = key_gain_full.reshape(-1).astype(F32)
-    routes_all = routes_all.reshape(shards, micros, rows, -1).transpose(1, 0, 2, 3)
-    routes_all = routes_all.reshape(tokens, -1).astype(jnp.int32)
-
-    head_gains = jnp.pad(jnp.stack([query_gain_full, key_gain_full]), ((0, 6), (0, 0)))
-    tables = rotary(span)
-    segments = (segment_ids[:, :, None], segment_ids[:, None, :])
-    mixer_all, projected, attended, middle_parts = attention_forward(
-        hidden_all, projections, output_weight, attn_gain[None], head_gains, tables, segments
-    )
+    router_full = small[:, : cuts[0]].reshape(width, experts)
+    routes_all = small[:, cuts[0] : sum(cuts)].reshape(shards, micros, rows, -1)
+    routes_all = routes_all.transpose(1, 0, 2, 3).reshape(tokens, -1).astype(jnp.int32)
+    attn_gain = gains_all[:, 0, :column_width].reshape(-1).astype(F32)
+    expert_gain_full = gains_all[:, 0, column_width : 2 * column_width].reshape(-1).astype(F32)
+    head_gains = jnp.sum(gains_all[:, 1, : 2 * HDIM].astype(F32), axis=0).reshape(2, HDIM)
+    head_gains = jnp.pad(head_gains, ((0, 6), (0, 0)))
     hidden = inputs.astype(F32)
-    ((middle_total,),) = fuse(
-        [Scatter(middle_parts.reshape(micros, shards, rows, width), layout)], layout, 1, "middle"
-    )
     middle = hidden + middle_total
 
     scale_second = rms_scale(middle)
     normed_second = middle * scale_second
     expert_input = (normed_second * expert_gain_full).astype(BF16)
-    ((expert_all,),) = fuse([Gather(expert_input, layout)], layout, 2, "experts_in")
-    expert_all = expert_all.reshape(tokens, width)
-    logits = jnp.dot(expert_all, router_full, preferred_element_type=F32)
+    early = tokens <= 1024 and 4 * groups * shards <= 256
     choose = (routes_all[:, :, None] == jnp.arange(experts, dtype=jnp.int32)).astype(F32)
-    share = softmax_rows(jnp.sum(choose * logits[:, None, :], axis=-1))
-    share_wide = jnp.sum(choose * share[:, :, None], axis=1)
-    served = (jnp.arange(groups, dtype=jnp.int32) * shards + shard_place) // 2
-    serves = (served[:, None] == jnp.arange(experts, dtype=jnp.int32)).astype(F32)
-    share_own = jnp.pad(
-        jnp.dot(share_wide, serves.T, precision=PRECISE), ((0, 0), (0, 128 - groups))
-    )
-    activated, gate_pre, up_pre, dots = expert_units(
-        expert_all, upstream_all, share_own, gate_all, up_all, down_all
-    )
-    early = tokens <= 1024
-    expert_grad_parts = expert_merge(gate_pre, up_pre, gate_all, up_all)
-    if not early:
-        gate_pre, expert_grad_parts = lax.optimization_barrier((gate_pre, expert_grad_parts))
-        gate_terms, up_terms, down_terms = expert_weights(
-            expert_all, upstream_all, activated, gate_pre, up_pre
+    if early:
+        mask = jnp.pad(jnp.sum(choose, axis=1), ((0, 0), (0, 128 - experts)))
+        router_wide = jnp.pad(router_full, ((0, 0), (0, 128 - experts)))
+        (
+            (
+                gate_terms,
+                up_terms,
+                down_terms,
+                out_parts,
+                share_wide,
+                expert_grad,
+                dot_total,
+            ),
+        ) = fuse(
+            [
+                Experts(
+                    expert_input,
+                    upstream_all,
+                    mask,
+                    router_wide,
+                    gate_all,
+                    up_all,
+                    down_all,
+                    layout,
+                )
+            ],
+            layout,
+            2,
+            "experts",
         )
-        out_parts = expert_output(activated, down_all)
-
-    halves = groups * shards
-    lanes = 2 * halves + -2 * halves % 128
-    columns = jnp.arange(groups, dtype=jnp.int32) * shards + shard_place
-    columns = (columns[:, None] == jnp.arange(halves, dtype=jnp.int32)).astype(F32)
-    placed = jnp.dot(dots[:, :groups], columns, precision=PRECISE)
-    placed_high = placed.astype(BF16)
-    placed_low = (placed - placed_high.astype(F32)).astype(BF16)
-    placed = jnp.pad(
-        jnp.concatenate([placed_high, placed_low], axis=1), ((0, 0), (0, lanes - 2 * halves))
-    )
-    returned = [
-        Scatter(placed.reshape(micros, shards, rows, lanes), layout),
-        Scatter(expert_grad_parts.reshape(micros, shards, rows, width), layout),
-    ]
-    if early:
-        returned.append(
-            ExpertWeights(
-                expert_all, upstream_all, activated, gate_pre, up_pre, down_all, layout
-            )
+        share = jnp.sum(choose * share_wide[:, None, :experts], axis=-1)
+        half_lanes = 64
+    else:
+        (
+            gate_terms,
+            up_terms,
+            down_terms,
+            out_parts,
+            share,
+            expert_grad,
+            dot_total,
+            half_lanes,
+        ) = experts_in_turn(
+            expert_input,
+            upstream_all,
+            choose,
+            router_full,
+            gate_all,
+            up_all,
+            down_all,
+            layout,
+            micros,
         )
-        (dot_total,), (expert_grad,), (_, up_terms, down_terms, out_parts, gate_grad) = fuse(
-            returned, layout, 3, "experts_out"
-        )
-    else:
-        returned.append(ExpertScatter(gate_terms, layout))
-        (dot_total,), (expert_grad,), (gate_grad,) = fuse(returned, layout, 3, "experts_out")
 
     def own_rows(values):
         return lax.dynamic_slice_in_dim(
@@ -1491,7 +2041,10 @@
         )
 
     own_choose, own_share = own_rows(choose), own_rows(share)
-    share_grad_wide = dot_total[..., :halves] + dot_total[..., halves : 2 * halves]
+    halves = groups * shards
+    share_grad_wide = (
+        dot_total[..., :halves] + dot_total[..., half_lanes : half_lanes + halves]
+    )
     share_grad_wide = share_grad_wide.reshape(micros, rows, experts, 2).sum(axis=-1)
     share_grad = jnp.sum(own_choose * share_grad_wide[:, :, None, :], axis=-1)
     chosen_grad = own_share * (
@@ -1508,33 +2061,29 @@
     router_term = jnp.einsum(
         "mtd,mte->de", expert_input.astype(F32), own_logits_grad, precision=PRECISE
     )
-    (branch_all,), (up_grad,) = fuse(
-        [Gather(middle_grad.astype(BF16), layout), ExpertScatter(up_terms, layout)],
+
+    beside = []
+    if early:
+        beside = [ExpertScatter(gate_terms, layout), ExpertScatter(up_terms, layout)]
+    ((projection_terms, output_term, head_gain_terms, mixer_grad, *side_grads),) = fuse(
+        [
+            AttentionBackward(
+                middle_grad.astype(BF16),
+                mixer_all,
+                projected,
+                attended,
+                projections,
+                output_weight,
+                head_gains,
+                tables,
+                segments,
+                beside,
+                layout,
+            )
+        ],
         layout,
         4,
-        "branch",
-    )
-    branch_all = branch_all.reshape(tokens, width)
-
-    mixer_parts, projection_terms, output_term, head_gain_terms = attention_backward(
-        branch_all,
-        mixer_all,
-        projected,
-        attended,
-        projections,
-        output_weight,
-        head_gains,
-        tables,
-        segments,
-    )
-    (mixer_grad,), (down_grad,) = fuse(
-        [
-            Scatter(mixer_parts.reshape(micros, shards, rows, width), layout),
-            ExpertScatter(down_terms, layout),
-        ],
-        layout,
-        5,
-        "mixer",
+        "attention_backward",
     )
     scale_first = rms_scale(hidden)
     normed_first = hidden * scale_first
@@ -1556,25 +2105,35 @@
         axis=1,
     )
     tail = jnp.pad(tail, ((0, 0), (0, -tail.shape[1] % 1024))).reshape(shards, -1, 128)
-    (outs,), (output_grad, tail, query_grad, key_grad, value_grad) = fuse(
+    (output_grad, tail, query_grad, key_grad, value_grad), (outs,), *last_grads = fuse(
         [
-            Scatter(out_parts.reshape(micros, shards, rows, width), layout),
             Rows(
                 projection_terms.reshape(shards, groups, part, 3 * column_width),
                 output_term.reshape(groups, part, width),
                 tail,
                 layout,
             ),
+            Scatter(out_parts, micros, layout),
+            *([ExpertScatter(down_terms, layout)] if early else []),
         ],
         layout,
-        6,
+        5,
         "exit",
     )
+    if early:
+        gate_grad, up_grad = side_grads
+        ((down_grad,),) = last_grads
+    else:
+        gate_grad, up_grad, down_grad = (
+            fuse([ExpertScatter(terms, layout)], layout, 6 + index, "weights")[0][0]
+            for index, terms in enumerate((gate_terms, up_terms, down_terms))
+        )
     result = middle + outs
     tail = tail.reshape(-1)
+    lengths = [column_width * experts] + [column_width] * 2 + [HDIM // shards] * 2
+    starts = [sum(lengths[:place]) for place in range(len(lengths))]
     tails = [
-        tail[start : start + length]
-        for start, length in zip(starts[:5], cuts[:5], strict=True)
+        tail[start : start + length] for start, length in zip(starts, lengths, strict=True)
     ]
     return (
         result.astype(BF16),

time: 812 us -> 673 us (0.83)
  Pallas kernels: 730 us -> 594 us
    pallas_call x4 -> x0, Pallas kernels: 106 us -> none  [the longest x1 37.5 us: expert_units(): pl.pallas_call(functools.partial(units_kernel, 256 if tokens <= 1024 else...]
    pallas_call x7 -> x4, Pallas kernels: 624 us -> 594 us  [fuse(): pl.pallas_call(kernel, out_shape=out_shape, in_specs=in_specs, out_specs=...]
  transfers between devices with their start and end apart: 3 -> 3, of which waited for: 0 -> 0; matrix products, arithmetic and copies ran while one was open for 2% -> 2% of each run, Pallas kernels for 35% -> 28%
where the time goes in v3:
time: 673 us; the launch traced here: 664 us
  Pallas kernels  594 us (88%)
  other arithmetic  29.2 us (4%)
  local copies, waits for them, and re-layouts  18.3 us (3%)
  between operations  14.6 us (2%)
    pallas_call x4, Pallas kernels, fuse(): pl.pallas_call(kernel, out_shape=out_shape, in_specs=in_specs, out_specs=...  594 us
  transfers between devices with their start and end apart: 3, of which 0 were waited for; matrix products, arithmetic and copies ran while one was open for 2% of the time, Pallas kernels for 28%

profile of v3, /device:TPU:11, one launch (start us, length us, event | category | flops | bytes accessed | tf_op | source)
XLA Modules:
  0.0 664.0 jit_solution(1663970166350687983)
XLA Ops:
  11.1 1.0 copy.59.refs_10_.refs_9_
  14.0 1.0 pad_maximum_fusion
  15.0 183.4 %attention_forward.1 = (bf16[8,48,128]{2,1,0:T(8,128)(2,1)}, bf16[8,16,512]{2,1,0:T(8,128)(2,1)}, bf16[8,256,768]{2,1,0:T(8,128)(2,1)}, bf16[1024,2048]{1,0:T(8,...) custom-call(bf16[256,2048]{1,0:T(8,128)(2,1)} %refs_0_.1, ...), custom_call_target="tpu_custom_call" | custom-call | flops 60000002048 | bytes 8388608 | tf_op jit(solution)/shard_map/attention_forward/pallas_call | solution.py:164
  204.2 1.6 multiply_reduce_fusion.2
  207.7 154.0 %experts.1 = (bf16[4,2048,512]{2,1,0:T(8,128)(2,1)}, bf16[4,2048,512]{2,1,0:T(8,128)(2,1)}, bf16[4,512,2048]{2,1,0:T(8,128)(2,1)}, bf16[1024,2048]{1,0:T(8,128)(...) custom-call(bf16[2,64,2048]{2,1,0:T(8,128)(2,1)} %multiply_convert_fusion.refs_0_, ...), custom_call_target="tpu_custom_call" | custom-call | flops 60000002048 | bytes 8388608 | tf_op jit(solution)/shard_map/experts/pallas_call | solution.py:164
  361.7 1.3 copy.63
  363.2 1.0 slice_add_fusion
  364.5 3.2 convolution_bitcast_fusion
  367.8 2.1 multiply_reduce_fusion
  369.9 2.2 reshape.247
  372.2 2.2 fusion.13.refs_0_
  374.3 138.0 %attention_backward.1 = (bf16[2048,768]{1,0:T(8,128)(2,1)}, bf16[256,2048]{1,0:T(8,128)(2,1)}, f32[8,128]{1,0:T(8,128)}, f32[2,64,2048]{2,1,0:T(8,128)}, bf16[20...) custom-call(bf16[2,64,2048]{2,1,0:T(8,128)(2,1)} %fusion.13.refs_0_, bf16[1024,2048]{1,0:T(8,128)(2,1)} %get-tuple-element.73.refs_1_, ...), custom_call_target="tpu_custom_call" | custom-call | flops 60000002048 | bytes 8388608 | tf_op jit(solution)/shard_map/attention_backward/pallas_call | solution.py:164
  513.2 1.6 fusion.4
  515.7 118.9 %exit.1 = (bf16[4,64,2048]{2,1,0:T(8,128)(2,1)}, f32[40,128]{1,0:T(8,128)}, bf16[4,64,2048]{2,1,0:T(8,128)(2,1)}, bf16[4,64,2048]{2,1,0:T(8,128)(2,1)}, bf16[4,6...) custom-call(bf16[8,4,64,768]{3,2,1,0:T(8,128)(2,1)} %bitcast.86, ...), custom_call_target="tpu_custom_call" | custom-call | flops 60000002048 | bytes 8388608 | tf_op jit(solution)/shard_map/exit/pallas_call | solution.py:164
  634.6 1.3 slice_bitcast_fusion
  636.6 1.3 fusion.19
  638.7 2.9 bitcast_convert_fusion.6
  641.6 1.6 bitcast_convert_fusion.5
  643.2 1.6 bitcast_convert_fusion.4
  644.9 1.6 bitcast_convert_fusion.3
  646.5 2.5 bitcast_convert_fusion
  649.1 2.6 bitcast_convert_fusion.2
  651.7 2.7 bitcast_convert_fusion.1
  655.5 1.5 fusion.8
  (117 shorter events, 18.0 us)
Async XLA Ops:
  7.2 2.6 copy-start.23
  7.2 2.8 copy-start.20
  7.2 2.8 copy-start.21
  7.2 2.8 copy-start.16
  7.2 3.4 copy-start.19
  7.2 3.6 copy-start.18
  7.3 200.4 %all-gather.4.cloned.1.call-start = ((), (), s32[]{:S(2)}) async-start(), calls=%async_computation | async-start | bytes 10485760 | tf_op jit(solution)/shard_map/all_gather | solution.py:1915
  8.0 199.7 %all-gather.6.cloned.1.call-start = ((), (), s32[]{:S(2)}) async-start(), calls=%async_computation.1 | async-start | bytes 10485760 | tf_op jit(solution)/shard_map/all_gather | solution.py:1916
  8.7 199.0 %all-gather.8.cloned.1.call-start = ((), (), s32[]{:S(2)}) async-start(), calls=%async_computation.2 | async-start | bytes 10485760 | tf_op jit(solution)/shard_map/all_gather | solution.py:1917
  12.3 2.6 copy-start.17
  198.4 5.8 copy-start.5
  361.7 6.0 copy-start.1
  369.9 4.4 copy-start.3
  374.3 138.9 %copy-start.6 = (bf16[2,64,2048]{2,1,0:T(8,128)(2,1)S(1)}, bf16[2,64,2048]{2,1,0:T(8,128)(2,1)}, u32[]{:S(2)}) copy-start(bf16[2,64,2048]{2,1,0:T(8,128)(2,1)} %refs_5_.2) | copy-start | bytes 1572868
  634.5 7.1 %copy-start.14 = (bf16[4,64,2048]{2,1,0:T(8,128)(2,1)S(1)}, bf16[4,64,2048]{2,1,0:T(8,128)(2,1)}, u32[]{:S(2)}) copy-start(bf16[4,64,2048]{2,1,0:T(8,128)(2,1)} %get-tuple-element.87) | copy-start | bytes 3145732
  638.7 4.5 copy-start.13
  641.6 3.3 copy-start.12
  643.2 3.3 copy-start.10
  649.1 2.6 copy-start.8
  651.7 2.8 copy-start.2
  651.7 2.8 copy-start.4
  651.7 2.8 copy-start.7
  651.7 3.1 copy-start.11
  651.7 3.8 copy-start.15
  (3 other events, 5.9 us)
Sparse Core Ops, SparseCore 0:
  9.6 76.6 all-gather.3
  87.9 58.2 all-gather.5
  147.8 58.2 all-gather.7

commit v4 on v3

--- a/solution.py
+++ b/solution.py
@@ -154,7 +154,7 @@
         for run in late:
             next(run)
         for index, _ in enumerate(together(*first)):
-            if index in (1, 2):
+            if index in (1, 7):
                 for run in late:
                     next(run)
         for run in late:
@@ -823,20 +823,22 @@
                 while inward in running:
                     others()
                     yield
+                running.extend([dot_scatters[piece - 1], scatters[piece - 1]])
+                next(dot_scatters[piece - 1])
+                next(scatters[piece - 1])
             shares(piece)
             for index, _ in enumerate(units_of(piece)):
                 if piece == 0 or index % 2:
                     others()
                 yield
             place_dots(piece)
-            running.append(dot_scatters[piece])
-            next(dot_scatters[piece])
             for index, _ in enumerate(merge(piece)):
                 if piece == 0 or index % 4 == 3:
                     others()
                 yield
-            running.append(scatters[piece])
-            next(scatters[piece])
+        running.extend([dot_scatters[-1], scatters[-1]])
+        next(dot_scatters[-1])
+        next(scatters[-1])
         for index, _ in enumerate(weights()):
             if index % 4 == 3:
                 others()
@@ -1602,12 +1604,17 @@
             for part, own_in, own_out in zip(self.beside, beside_in, beside_out, strict=True)
         ]
         next(inward)
-        for side in sides:
+        for side in sides[:1]:
+            next(side)
+            for _ in range(2):
+                next(inward)
+                next(side)
+        for side in sides[1:]:
             next(side)
         gain_terms[...] = jnp.zeros_like(gain_terms)
         gains = (head_gains[0:1], head_gains[1:2])
         yield from until(inward, 1)
-        for side in sides[:1]:
+        for side in sides[1:]:
             next(side)
             next(side)
         running = []
@@ -1634,14 +1641,10 @@
                 if micro + 1 < micros:
                     next(inward, END)
                 yield
+            if micro + 1 < micros:
+                yield from until(inward, micro + 2)
             running.append(scatters[micro])
             next(scatters[micro])
-            if micro == 0:
-                for side in sides[1:]:
-                    next(side)
-                    next(side)
-            if micro + 1 < micros:
-                yield from until(inward, micro + 2)
         running.append(inward)
         running.append(
             weight_steps(

time: 673 us -> 648 us (0.963)
  Pallas kernels: 594 us -> 566 us
    pallas_call x4, Pallas kernels: 594 us -> 566 us  [fuse(): pl.pallas_call(kernel, out_shape=out_shape, in_specs=in_specs, out_specs=...]
  transfers between devices with their start and end apart: 3 -> 3, of which waited for: 0 -> 0; matrix products, arithmetic and copies ran while one was open for 2% -> 2% of each run, Pallas kernels for 28% -> 29%
where the time goes in v4:
time: 648 us; the launch traced here: 636 us
  Pallas kernels  566 us (87%)
  other arithmetic  29.2 us (5%)
  local copies, waits for them, and re-layouts  18.3 us (3%)
  between operations  14.6 us (2%)
    pallas_call x4, Pallas kernels, fuse(): pl.pallas_call(kernel, out_shape=out_shape, in_specs=in_specs, out_specs=...  566 us
  transfers between devices with their start and end apart: 3, of which 0 were waited for; matrix products, arithmetic and copies ran while one was open for 2% of the time, Pallas kernels for 29%

profile of v4, /device:TPU:11, one launch (start us, length us, event | category | flops | bytes accessed | tf_op | source)
XLA Modules:
  0.0 636.1 jit_solution(11714488505266425999)
XLA Ops:
  11.1 1.0 copy.59.refs_10_.refs_9_
  14.0 1.0 pad_maximum_fusion
  15.0 183.6 %attention_forward.1 = (bf16[8,48,128]{2,1,0:T(8,128)(2,1)}, bf16[8,16,512]{2,1,0:T(8,128)(2,1)}, bf16[8,256,768]{2,1,0:T(8,128)(2,1)}, bf16[1024,2048]{1,0:T(8,...) custom-call(bf16[256,2048]{1,0:T(8,128)(2,1)} %refs_0_.1, ...), custom_call_target="tpu_custom_call" | custom-call | flops 60000002048 | bytes 8388608 | tf_op jit(solution)/shard_map/attention_forward/pallas_call | solution.py:164
  204.4 1.6 multiply_reduce_fusion.2
  207.9 149.7 %experts.1 = (bf16[4,2048,512]{2,1,0:T(8,128)(2,1)}, bf16[4,2048,512]{2,1,0:T(8,128)(2,1)}, bf16[4,512,2048]{2,1,0:T(8,128)(2,1)}, bf16[1024,2048]{1,0:T(8,128)(...) custom-call(bf16[2,64,2048]{2,1,0:T(8,128)(2,1)} %multiply_convert_fusion.refs_0_, ...), custom_call_target="tpu_custom_call" | custom-call | flops 60000002048 | bytes 8388608 | tf_op jit(solution)/shard_map/experts/pallas_call | solution.py:164
  357.7 1.3 copy.63
  359.1 1.0 slice_add_fusion
  360.5 3.2 convolution_bitcast_fusion
  363.7 2.1 multiply_reduce_fusion
  365.9 2.2 reshape.247
  368.1 2.2 fusion.13.refs_0_
  370.3 119.4 %attention_backward.1 = (bf16[2048,768]{1,0:T(8,128)(2,1)}, bf16[256,2048]{1,0:T(8,128)(2,1)}, f32[8,128]{1,0:T(8,128)}, f32[2,64,2048]{2,1,0:T(8,128)}, bf16[20...) custom-call(bf16[2,64,2048]{2,1,0:T(8,128)(2,1)} %fusion.13.refs_0_, bf16[1024,2048]{1,0:T(8,128)(2,1)} %get-tuple-element.73.refs_1_, ...), custom_call_target="tpu_custom_call" | custom-call | flops 60000002048 | bytes 8388608 | tf_op jit(solution)/shard_map/attention_backward/pallas_call | solution.py:164
  490.6 1.6 fusion.4
  493.0 113.6 %exit.1 = (bf16[4,64,2048]{2,1,0:T(8,128)(2,1)}, f32[40,128]{1,0:T(8,128)}, bf16[4,64,2048]{2,1,0:T(8,128)(2,1)}, bf16[4,64,2048]{2,1,0:T(8,128)(2,1)}, bf16[4,6...) custom-call(bf16[8,4,64,768]{3,2,1,0:T(8,128)(2,1)} %bitcast.86, ...), custom_call_target="tpu_custom_call" | custom-call | flops 60000002048 | bytes 8388608 | tf_op jit(solution)/shard_map/exit/pallas_call | solution.py:164
  606.6 1.3 slice_bitcast_fusion
  608.7 1.3 fusion.19
  610.8 2.9 bitcast_convert_fusion.6
  613.7 1.6 bitcast_convert_fusion.5
  615.3 1.6 bitcast_convert_fusion.4
  617.0 1.6 bitcast_convert_fusion.3
  618.6 2.5 bitcast_convert_fusion
  621.1 2.6 bitcast_convert_fusion.2
  623.8 2.7 bitcast_convert_fusion.1
  627.6 1.5 fusion.8
  (117 shorter events, 18.0 us)
Async XLA Ops:
  7.2 2.6 copy-start.23
  7.2 2.8 copy-start.20
  7.2 2.8 copy-start.21
  7.2 2.8 copy-start.16
  7.2 3.4 copy-start.19
  7.2 3.6 copy-start.18
  7.3 200.7 %all-gather.4.cloned.1.call-start = ((), (), s32[]{:S(2)}) async-start(), calls=%async_computation | async-start | bytes 10485760 | tf_op jit(solution)/shard_map/all_gather | solution.py:1918
  8.0 200.0 %all-gather.6.cloned.1.call-start = ((), (), s32[]{:S(2)}) async-start(), calls=%async_computation.1 | async-start | bytes 10485760 | tf_op jit(solution)/shard_map/all_gather | solution.py:1919
  8.7 199.2 %all-gather.8.cloned.1.call-start = ((), (), s32[]{:S(2)}) async-start(), calls=%async_computation.2 | async-start | bytes 10485760 | tf_op jit(solution)/shard_map/all_gather | solution.py:1920
  12.3 2.6 copy-start.17
  198.6 5.8 copy-start.5
  357.7 6.0 copy-start.1
  365.9 4.4 copy-start.3
  370.3 120.3 %copy-start.6 = (bf16[2,64,2048]{2,1,0:T(8,128)(2,1)S(1)}, bf16[2,64,2048]{2,1,0:T(8,128)(2,1)}, u32[]{:S(2)}) copy-start(bf16[2,64,2048]{2,1,0:T(8,128)(2,1)} %refs_5_.2) | copy-start | bytes 1572868
  606.6 7.1 %copy-start.14 = (bf16[4,64,2048]{2,1,0:T(8,128)(2,1)S(1)}, bf16[4,64,2048]{2,1,0:T(8,128)(2,1)}, u32[]{:S(2)}) copy-start(bf16[4,64,2048]{2,1,0:T(8,128)(2,1)} %get-tuple-element.87) | copy-start | bytes 3145732
  610.8 4.5 copy-start.13
  613.7 3.3 copy-start.12
  615.3 3.3 copy-start.10
  621.1 2.6 copy-start.8
  623.8 2.8 copy-start.2
  623.8 2.8 copy-start.4
  623.8 2.8 copy-start.7
  623.8 3.1 copy-start.11
  623.8 3.8 copy-start.15
  (3 other events, 5.9 us)
Sparse Core Ops, SparseCore 0:
  9.6 76.6 all-gather.3
  87.9 58.2 all-gather.5
  147.8 58.2 all-gather.7

commit v5 on v4

--- a/solution.py
+++ b/solution.py
@@ -1645,6 +1645,8 @@
                 yield from until(inward, micro + 2)
             running.append(scatters[micro])
             next(scatters[micro])
+        for side in sides[:1]:
+            yield from side
         running.append(inward)
         running.append(
             weight_steps(
@@ -1652,7 +1654,7 @@
             )
         )
         yield from together(*running)
-        for side in sides:
+        for side in sides[1:]:
             yield from side
 
 
@@ -2054,16 +2056,23 @@
         share_grad - jnp.sum(own_share * share_grad, axis=-1, keepdims=True)
     )
     own_logits_grad = jnp.sum(own_choose * chosen_grad[..., None], axis=2)
-    expert_grad = expert_grad + jnp.dot(
-        own_logits_grad, router_full.astype(F32).T, precision=PRECISE
+    logits_high = lax.reduce_precision(own_logits_grad, 8, 7)
+    logits_pair = jnp.concatenate([logits_high, own_logits_grad - logits_high], axis=-1)
+    logits_pair = logits_pair.astype(BF16)
+    expert_grad = expert_grad + jnp.einsum(
+        "mte,de->mtd",
+        logits_pair,
+        jnp.concatenate([router_full, router_full], axis=1),
+        preferred_element_type=F32,
     )
     expert_gain_term = jnp.sum(expert_grad * normed_second, axis=(0, 1))
     middle_grad = cotangent.astype(F32) + norm_back(
         expert_grad * expert_gain_full, normed_second, scale_second
     )
     router_term = jnp.einsum(
-        "mtd,mte->de", expert_input.astype(F32), own_logits_grad, precision=PRECISE
-    )
+        "mtd,mte->de", expert_input, logits_pair, preferred_element_type=F32
+    )
+    router_term = router_term[:, :experts] + router_term[:, experts:]
 
     beside = []
     if early:

time: 648 us -> 642 us (level)
  no operation moved by 1% of the time
where the time goes in v5:
time: 642 us; the launch traced here: 631 us
  Pallas kernels  566 us (88%)
  other arithmetic  28.3 us (4%)
  local copies, waits for them, and re-layouts  17.4 us (3%)
  between operations  14.6 us (2%)
    pallas_call x4, Pallas kernels, fuse(): pl.pallas_call(kernel, out_shape=out_shape, in_specs=in_specs, out_specs=...  566 us
  transfers between devices with their start and end apart: 3, of which 0 were waited for; matrix products, arithmetic and copies ran while one was open for 2% of the time, Pallas kernels for 29%

profile of v5, /device:TPU:11, one launch (start us, length us, event | category | flops | bytes accessed | tf_op | source)
XLA Modules:
  0.0 631.4 jit_solution(7643311498344121827)
XLA Ops:
  11.1 1.0 copy.61.refs_10_.refs_9_
  13.0 1.0 fusion.15
  14.0 1.0 pad_maximum_fusion
  15.0 183.6 %attention_forward.1 = (bf16[8,48,128]{2,1,0:T(8,128)(2,1)}, bf16[8,16,512]{2,1,0:T(8,128)(2,1)}, bf16[8,256,768]{2,1,0:T(8,128)(2,1)}, bf16[1024,2048]{1,0:T(8,...) custom-call(bf16[256,2048]{1,0:T(8,128)(2,1)} %refs_0_.1, ...), custom_call_target="tpu_custom_call" | custom-call | flops 60000002048 | bytes 8388608 | tf_op jit(solution)/shard_map/attention_forward/pallas_call | solution.py:164
  198.6 1.0 copy.77
  206.9 149.8 %experts.1 = (bf16[4,2048,512]{2,1,0:T(8,128)(2,1)}, bf16[4,2048,512]{2,1,0:T(8,128)(2,1)}, bf16[4,512,2048]{2,1,0:T(8,128)(2,1)}, bf16[1024,2048]{1,0:T(8,128)(...) custom-call(bf16[2,64,2048]{2,1,0:T(8,128)(2,1)} %multiply_convert_fusion.refs_0_, ...), custom_call_target="tpu_custom_call" | custom-call | flops 60000002048 | bytes 8388608 | tf_op jit(solution)/shard_map/experts/pallas_call | solution.py:164
  356.8 1.3 copy.65
  358.2 1.0 slice_add_fusion.1
  359.6 1.3 convolution_bitcast_fusion
  360.9 2.1 multiply_reduce_fusion
  363.0 2.5 fusion.14.refs_0_
  365.5 118.6 %attention_backward.1 = (bf16[2048,768]{1,0:T(8,128)(2,1)}, bf16[256,2048]{1,0:T(8,128)(2,1)}, f32[8,128]{1,0:T(8,128)}, f32[2,64,2048]{2,1,0:T(8,128)}, bf16[20...) custom-call(bf16[2,64,2048]{2,1,0:T(8,128)(2,1)} %fusion.14.refs_0_, bf16[1024,2048]{1,0:T(8,128)(2,1)} %get-tuple-element.73.refs_1_, ...), custom_call_target="tpu_custom_call" | custom-call | flops 60000002048 | bytes 8388608 | tf_op jit(solution)/shard_map/attention_backward/pallas_call | solution.py:164
  485.1 1.6 fusion.4
  488.4 113.5 %exit.1 = (bf16[4,64,2048]{2,1,0:T(8,128)(2,1)}, f32[40,128]{1,0:T(8,128)}, bf16[4,64,2048]{2,1,0:T(8,128)(2,1)}, bf16[4,64,2048]{2,1,0:T(8,128)(2,1)}, bf16[4,6...) custom-call(bf16[8,4,64,768]{3,2,1,0:T(8,128)(2,1)} %bitcast.84, ...), custom_call_target="tpu_custom_call" | custom-call | flops 60000002048 | bytes 8388608 | tf_op jit(solution)/shard_map/exit/pallas_call | solution.py:164
  601.9 1.3 slice_bitcast_fusion
  604.0 1.3 fusion.23
  606.1 2.9 bitcast_convert_fusion.6
  609.0 1.6 bitcast_convert_fusion.5
  610.6 1.6 bitcast_convert_fusion.4
  612.3 1.6 bitcast_convert_fusion.3
  613.9 2.5 bitcast_convert_fusion
  616.5 2.6 bitcast_convert_fusion.2
  619.1 2.7 bitcast_convert_fusion.1
  622.9 1.5 fusion.8
  (121 shorter events, 17.6 us)
Async XLA Ops:
  7.2 2.6 copy-start.23
  7.2 2.8 copy-start.20
  7.2 2.8 copy-start.21
  7.2 2.8 copy-start.16
  7.2 3.4 copy-start.19
  7.2 3.6 copy-start.18
  7.3 199.7 %all-gather.4.cloned.1.call-start = ((), (), s32[]{:S(2)}) async-start(), calls=%async_computation | async-start | bytes 10485760 | tf_op jit(solution)/shard_map/all_gather | solution.py:1920
  8.0 198.9 %all-gather.6.cloned.1.call-start = ((), (), s32[]{:S(2)}) async-start(), calls=%async_computation.1 | async-start | bytes 10485760 | tf_op jit(solution)/shard_map/all_gather | solution.py:1921
  8.7 198.2 %all-gather.8.cloned.1.call-start = ((), (), s32[]{:S(2)}) async-start(), calls=%async_computation.2 | async-start | bytes 10485760 | tf_op jit(solution)/shard_map/all_gather | solution.py:1922
  12.3 2.6 copy-start.17
  198.6 6.0 copy-start.5
  198.6 6.0 copy-start.14
  356.8 6.3 copy-start.1
  363.0 2.6 copy-start.3
  601.9 7.1 %copy-start.13 = (bf16[4,64,2048]{2,1,0:T(8,128)(2,1)S(1)}, bf16[4,64,2048]{2,1,0:T(8,128)(2,1)}, u32[]{:S(2)}) copy-start(bf16[4,64,2048]{2,1,0:T(8,128)(2,1)} %get-tuple-element.87) | copy-start | bytes 3145732
  606.1 4.5 copy-start.12
  609.0 3.3 copy-start.11
  610.6 3.3 copy-start.9
  616.5 2.6 copy-start.7
  619.1 2.8 copy-start.2
  619.1 2.8 copy-start.4
  619.1 2.8 copy-start.6
  619.1 3.1 copy-start.10
  619.1 3.8 copy-start.15
  (3 other events, 5.9 us)
Sparse Core Ops, SparseCore 0:
  9.6 76.6 all-gather.3
  87.9 58.2 all-gather.5
  147.8 58.2 all-gather.7
